TPU v7x, 32 devices: a whole 2x2x4 slice. The times are simulated.
32 devices in a mesh: fsdp: 4 (over z), ctx: 2 (over core), tp: 4 (over y, x).
Axes of the slice: x: 2, y: 2, z: 4, core: 2. Of those that a mesh axis runs over, the one named last changes fastest.
Arguments:
- token_ids: int32 [4, 1024], P('fsdp', 'ctx'), may hold values from 0 to 1023
- masked: int32 [4, 1024], P('fsdp', 'ctx'), may hold values from 0 to 1, as said below
- tile_slot: int32 [36], replicated, may hold values from 0 to 47, as said below
- tile_master: float32 [48, 768, 768], P('fsdp', 'tp'), may hold values from -0.21875 to 0.21875
- tile_first: float32 [48, 768, 768], P('fsdp', 'tp'), may hold values from -0.0009765625 to 0.0009765625
- tile_second: float32 [48, 768, 768], P('fsdp', 'tp'), may hold values from 2.4414062e-09 to 9.765625e-09
- embedding: float32 [768, 2025], P('fsdp'), may hold values from -0.3125 to 0.3125
- embed_first: float32 [768, 2025], P('fsdp'), may hold values from -0.0009765625 to 0.0009765625
- embed_second: float32 [768, 2025], P('fsdp'), may hold values from 2.4414062e-09 to 9.765625e-09
- position_table: float32 [768, 1024], P('fsdp'), may hold values from -0.3125 to 0.3125
- position_first: float32 [768, 1024], P('fsdp'), may hold values from -0.00030517578 to 0.00030517578
- position_second: float32 [768, 1024], P('fsdp'), may hold values from 2.384186e-10 to 9.536744e-10
- norm_params: float32 [2, 7, 768], P(None, None, 'fsdp')
- norm_first: float32 [2, 7, 768], P(None, None, 'fsdp'), may hold values from -0.0009765625 to 0.0009765625
- norm_second: float32 [2, 7, 768], P(None, None, 'fsdp'), may hold values from 2.4414062e-09 to 9.765625e-09
- head_bias: float32 [2025], replicated, may hold values from -3 to 3
- bias_first: float32 [2025], replicated, may hold values from -0.0009765625 to 0.0009765625
- bias_second: float32 [2025], replicated, may hold values from 2.4414062e-09 to 9.765625e-09
Outputs:
- loss_value: float32 [], replicated
- tile_new: float32 [48, 768, 768], P('fsdp', 'tp')
- tile_first_new: float32 [48, 768, 768], P('fsdp', 'tp')
- tile_second_new: float32 [48, 768, 768], P('fsdp', 'tp')
- embedding_new: float32 [768, 2025], P('fsdp')
- embed_first_new: float32 [768, 2025], P('fsdp')
- embed_second_new: float32 [768, 2025], P('fsdp')
- position_new: float32 [768, 1024], P('fsdp')
- position_first_new: float32 [768, 1024], P('fsdp')
- position_second_new: float32 [768, 1024], P('fsdp')
- norm_new: float32 [2, 7, 768], P(None, None, 'fsdp')
- norm_first_new: float32 [2, 7, 768], P(None, None, 'fsdp')
- norm_second_new: float32 [2, 7, 768], P(None, None, 'fsdp')
- bias_new: float32 [2025], replicated
- bias_first_new: float32 [2025], replicated
- bias_second_new: float32 [2025], replicated
Inputs may be any that keep to these rules, and one draw needn't show every extreme that they name: The last place of every image is masked. `tile_slot`: tile t belongs to layer t // 12, in the order q, k, v, output, four input tiles, four output tiles. The values are distinct; slot s belongs to index s // 12 of fsdp, and some index holds 12 tiles.
All inputs are finite; a program needn't handle non-finite values.
Results may differ from a plain program's by a relative error of at most 0.025.
The roundings to bfloat16 on the way count: a program that leaves them out, or rounds other values in their place, can miss the bound.
Values may be sent and summed in bfloat16 or wider, within the bound.
No kernel may reach another device: no remote copies, remote signals or barrier semaphores. Data moves between devices by JAX's collectives and lax.ppermute only.
A program may use at most 320 MiB of HBM per device.

v0:
```python
import jax
import jax.numpy as jnp
from jax import lax
from jax.sharding import PartitionSpec as P

HEAD_DIM = 48
VOCAB = 2025
LAYERS = 3
STEP = 10


norm_eps = 1e-05
beta_first = 0.9
beta_second = 0.999
learn_rate = 0.05
small_rate = 0.5
weight_decay = 0.01
adam_eps = 1e-08


def norm_parts(stream, gain, shift):
    centered = stream - jnp.mean(stream, -1, keepdims=True)
    inverse = lax.rsqrt(jnp.mean(centered * centered, -1, keepdims=True) + norm_eps)
    normal_hat = centered * inverse
    return (normal_hat * gain + shift, normal_hat, inverse)


def norm_back(gradient, normal_hat, inverse, gain):
    scaled = gradient * gain
    return inverse * (
        scaled
        - jnp.mean(scaled, -1, keepdims=True)
        - normal_hat * jnp.mean(scaled * normal_hat, -1, keepdims=True)
    )


def gelu_slope(pre_gelu):
    return (
        0.5 * (1.0 + lax.erf(pre_gelu * 0.7071067811865476))
        + pre_gelu * jnp.exp(-0.5 * pre_gelu * pre_gelu) * 0.3989422804014327
    )


def tensor_forward(partial_out):
    return lax.psum(partial_out.astype(jnp.bfloat16), "tp").astype(jnp.float32)


def tensor_backward(partial_grad):
    return lax.psum(partial_grad.astype(jnp.bfloat16), "tp").astype(jnp.float32)


def row_share(values, first_row, share):
    return jnp.sum(lax.dynamic_slice_in_dim(values, first_row, share, 0), 0)


def attention_scores(queries, key_rows):
    return jnp.einsum(
        "iqhc,ikhc->ihqk", queries, key_rows, preferred_element_type=jnp.float32
    ) * HEAD_DIM ** (-0.5)


def layer_forward(stream, layer_tiles, gains, layer_idx, images, half_len):
    row_count = stream.shape[0]
    local_width = layer_tiles.shape[1]
    head_count = local_width // HEAD_DIM
    normed = norm_parts(stream, gains[0, 2 * layer_idx], gains[1, 2 * layer_idx])[0].astype(
        jnp.bfloat16
    )
    projected = jnp.einsum(
        "rd,tcd->trc", normed, layer_tiles[0:3], preferred_element_type=jnp.float32
    ).astype(jnp.bfloat16)
    key_rows, value_rows = (
        lax.all_gather(
            projected[1].reshape(images, half_len, local_width), "ctx", axis=1, tiled=True
        ),
        lax.all_gather(
            projected[2].reshape(images, half_len, local_width), "ctx", axis=1, tiled=True
        ),
    )
    queries = projected[0].reshape(images, half_len, head_count, HEAD_DIM)
    key_rows = key_rows.reshape(images, -1, head_count, HEAD_DIM)
    value_rows = value_rows.reshape(images, -1, head_count, HEAD_DIM)
    scores = attention_scores(queries, key_rows)
    row_top = jnp.max(scores, -1, keepdims=True)
    log_total = row_top + jnp.log(jnp.sum(jnp.exp(scores - row_top), -1, keepdims=True))
    attn_weights = jnp.exp(scores - log_total).astype(jnp.bfloat16)
    mixed_heads = (
        jnp.einsum("ihqk,ikhc->iqhc", attn_weights, value_rows, preferred_element_type=jnp.float32)
        .reshape(row_count, local_width)
        .astype(jnp.bfloat16)
    )
    attn_out = jnp.dot(mixed_heads, layer_tiles[3], preferred_element_type=jnp.float32)
    middle = stream + tensor_forward(attn_out)
    normed_mlp = norm_parts(middle, gains[0, 2 * layer_idx + 1], gains[1, 2 * layer_idx + 1])[
        0
    ].astype(jnp.bfloat16)
    pre_gelu = jnp.einsum(
        "rd,tcd->rtc", normed_mlp, layer_tiles[4:8], preferred_element_type=jnp.float32
    )
    activation = jax.nn.gelu(pre_gelu, approximate=False).astype(jnp.bfloat16)
    mlp_out = jnp.einsum(
        "rtc,tcd->rd", activation, layer_tiles[8:12], preferred_element_type=jnp.float32
    )
    kept = (stream, middle, projected, key_rows, value_rows, log_total, mixed_heads, pre_gelu)
    return (middle + tensor_forward(mlp_out), kept)


def layer_backward(gradient, kept, layer_tiles, gains, layer_idx, first_row, share):
    stream, middle, projected, key_rows, value_rows, log_total, mixed_heads, pre_gelu = kept
    row_count = stream.shape[0]
    images, seq_len, head_count, _ = key_rows.shape
    half_len = row_count // images
    local_width = layer_tiles.shape[1]
    branch = gradient.astype(jnp.bfloat16)
    activation = jax.nn.gelu(pre_gelu, approximate=False).astype(jnp.bfloat16)
    grad_out = jnp.einsum("rtc,rd->tcd", activation, branch, preferred_element_type=jnp.float32)
    grad_act = jnp.einsum(
        "rd,tcd->rtc", branch, layer_tiles[8:12], preferred_element_type=jnp.float32
    )
    grad_pre = (grad_act * gelu_slope(pre_gelu)).astype(jnp.bfloat16)
    normed_mlp, hat_mlp, inv_mlp = norm_parts(
        middle, gains[0, 2 * layer_idx + 1], gains[1, 2 * layer_idx + 1]
    )
    grad_in = jnp.einsum(
        "rtc,rd->tcd", grad_pre, normed_mlp.astype(jnp.bfloat16), preferred_element_type=jnp.float32
    )
    grad_normed_mlp = tensor_backward(
        jnp.einsum("rtc,tcd->rd", grad_pre, layer_tiles[4:8], preferred_element_type=jnp.float32)
    )
    grad_middle = gradient + norm_back(
        grad_normed_mlp, hat_mlp, inv_mlp, gains[0, 2 * layer_idx + 1]
    )
    norm_mlp_grads = (
        row_share(grad_normed_mlp * hat_mlp, first_row, share),
        row_share(grad_normed_mlp, first_row, share),
    )
    branch = grad_middle.astype(jnp.bfloat16)
    grad_proj_out = lax.dot_general(
        mixed_heads, branch, (((0,), (0,)), ((), ())), preferred_element_type=jnp.float32
    )
    grad_mixed = lax.dot_general(
        branch, layer_tiles[3], (((1,), (1,)), ((), ())), preferred_element_type=jnp.float32
    ).astype(jnp.bfloat16)
    grad_mixed = grad_mixed.reshape(images, half_len, head_count, HEAD_DIM)
    queries = projected[0].reshape(images, half_len, head_count, HEAD_DIM)
    attn_soft = jnp.exp(attention_scores(queries, key_rows) - log_total)
    grad_soft = jnp.einsum(
        "iqhc,ikhc->ihqk", grad_mixed, value_rows, preferred_element_type=jnp.float32
    )
    grad_scores = (
        attn_soft * (grad_soft - jnp.sum(attn_soft * grad_soft, -1, keepdims=True))
    ).astype(jnp.bfloat16)
    grad_queries = jnp.einsum(
        "ihqk,ikhc->iqhc", grad_scores, key_rows, preferred_element_type=jnp.float32
    ) * HEAD_DIM ** (-0.5)
    grad_keys = jnp.einsum(
        "ihqk,iqhc->ikhc", grad_scores, queries, preferred_element_type=jnp.float32
    ) * HEAD_DIM ** (-0.5)
    grad_values = jnp.einsum(
        "ihqk,iqhc->ikhc",
        attn_soft.astype(jnp.bfloat16),
        grad_mixed,
        preferred_element_type=jnp.float32,
    )
    grad_keys, grad_values = (
        lax.psum_scatter(
            grad_keys.reshape(images, seq_len, local_width).astype(jnp.bfloat16),
            "ctx",
            scatter_dimension=1,
            tiled=True,
        ).astype(jnp.float32),
        lax.psum_scatter(
            grad_values.reshape(images, seq_len, local_width).astype(jnp.bfloat16),
            "ctx",
            scatter_dimension=1,
            tiled=True,
        ).astype(jnp.float32),
    )
    grad_proj = jnp.stack(
        [
            grad_queries.reshape(row_count, local_width),
            grad_keys.reshape(row_count, local_width),
            grad_values.reshape(row_count, local_width),
        ]
    ).astype(jnp.bfloat16)
    normed, hat_attn, inv_attn = norm_parts(
        stream, gains[0, 2 * layer_idx], gains[1, 2 * layer_idx]
    )
    grad_qkv = jnp.einsum(
        "trc,rd->tcd", grad_proj, normed.astype(jnp.bfloat16), preferred_element_type=jnp.float32
    )
    grad_normed = tensor_backward(
        jnp.einsum("trc,tcd->rd", grad_proj, layer_tiles[0:3], preferred_element_type=jnp.float32)
    )
    grad_stream = grad_middle + norm_back(grad_normed, hat_attn, inv_attn, gains[0, 2 * layer_idx])
    norm_attn_grads = (
        row_share(grad_normed * hat_attn, first_row, share),
        row_share(grad_normed, first_row, share),
    )
    tile_grads = jnp.concatenate([grad_qkv, grad_proj_out[None], grad_in, grad_out], 0)
    return (grad_stream, tile_grads, norm_attn_grads, norm_mlp_grads)


def adamw_update(weight, moment_one, moment_two, gradient, rate):
    moment_one = beta_first * moment_one + (1.0 - beta_first) * gradient
    moment_two = beta_second * moment_two + (1.0 - beta_second) * gradient * gradient
    first_hat = moment_one / (1.0 - beta_first**STEP)
    second_hat = moment_two / (1.0 - beta_second**STEP)
    weight = weight - rate * (first_hat / (jnp.sqrt(second_hat) + adam_eps) + weight_decay * weight)
    return (weight, moment_one, moment_two)


def body(
    token_ids,
    masked,
    tile_slot,
    tile_master,
    tile_first,
    tile_second,
    embedding,
    embed_first,
    embed_second,
    position_table,
    position_first,
    position_second,
    norm_params,
    norm_first,
    norm_second,
    head_bias,
    bias_first,
    bias_second,
):
    context_at = lax.axis_index("ctx")
    tensor_at = lax.axis_index("tp")
    owner_at = lax.axis_index("fsdp")
    slot_all, embed_all, position_all, norm_all = (
        lax.all_gather(tile_master.astype(jnp.bfloat16), "fsdp", axis=0, tiled=True),
        lax.all_gather(embedding.astype(jnp.bfloat16), "fsdp", axis=0, tiled=True),
        lax.all_gather(position_table.astype(jnp.bfloat16), "fsdp", axis=0, tiled=True),
        lax.all_gather(norm_params.astype(jnp.bfloat16), "fsdp", axis=2, tiled=True),
    )
    model_width = slot_all.shape[2]
    weights = slot_all[tile_slot].reshape(LAYERS, 12, slot_all.shape[1], model_width)
    gains = norm_all.astype(jnp.float32)
    images, half_len = token_ids.shape
    row_count = images * half_len
    share = row_count // lax.axis_size("tp")
    first_row = tensor_at * share
    inputs = jnp.where(masked == 1, VOCAB - 1, token_ids).reshape(row_count)
    local_positions = lax.dynamic_slice_in_dim(
        position_all, context_at * half_len, half_len, 1
    ).T.astype(jnp.float32)
    looked_up = jnp.take(embed_all, inputs, axis=1).T.astype(jnp.float32)
    stream = (looked_up.reshape(images, half_len, model_width) + local_positions[None]).reshape(
        row_count, model_width
    )
    kept_layers = []
    for layer_idx in range(LAYERS):
        stream, kept = layer_forward(stream, weights[layer_idx], gains, layer_idx, images, half_len)
        kept_layers.append(kept)
    final_rows = lax.dynamic_slice_in_dim(stream, first_row, share, 0)
    final_normed, hat_final, inv_final = norm_parts(
        final_rows, gains[0, 2 * LAYERS], gains[1, 2 * LAYERS]
    )
    final_normed = final_normed.astype(jnp.bfloat16)
    logits = jnp.dot(final_normed, embed_all, preferred_element_type=jnp.float32) + head_bias
    targets = lax.dynamic_slice_in_dim(token_ids.reshape(row_count), first_row, share, 0)
    row_weights = lax.dynamic_slice_in_dim(masked.reshape(row_count), first_row, share, 0).astype(
        jnp.float32
    )
    row_top = jnp.max(logits, -1, keepdims=True)
    log_total = row_top + jnp.log(jnp.sum(jnp.exp(logits - row_top), -1, keepdims=True))
    is_target = lax.broadcasted_iota(jnp.int32, logits.shape, 1) == targets[:, None]
    picked = jnp.sum(jnp.where(is_target, logits, 0.0), -1)
    loss_sum, masked_count = lax.psum(
        (jnp.sum((log_total[:, 0] - picked) * row_weights), jnp.sum(row_weights)),
        ("fsdp", "ctx", "tp"),
    )
    loss_value = loss_sum / masked_count
    grad_logits = (
        (jnp.exp(logits - log_total) - is_target.astype(jnp.float32))
        * (row_weights / masked_count)[:, None]
    ).astype(jnp.bfloat16)
    bias_grad = jnp.sum(grad_logits.astype(jnp.float32), 0)
    embed_grad = lax.dot_general(
        final_normed, grad_logits, (((0,), (0,)), ((), ())), preferred_element_type=jnp.float32
    )
    grad_final = lax.dot_general(
        grad_logits, embed_all, (((1,), (1,)), ((), ())), preferred_element_type=jnp.float32
    )
    norm_grad = jnp.zeros((2, gains.shape[1], model_width), jnp.float32)
    norm_grad = (
        norm_grad.at[0, 2 * LAYERS]
        .set(jnp.sum(grad_final * hat_final, 0))
        .at[1, 2 * LAYERS]
        .set(jnp.sum(grad_final, 0))
    )
    gradient = lax.all_gather(
        norm_back(grad_final, hat_final, inv_final, gains[0, 2 * LAYERS]).astype(jnp.bfloat16),
        "tp",
        axis=0,
        tiled=True,
    ).astype(jnp.float32)
    tile_grads = [None] * LAYERS
    for layer_idx in reversed(range(LAYERS)):
        gradient, tile_grads[layer_idx], attn_norm, mlp_norm = layer_backward(
            gradient, kept_layers[layer_idx], weights[layer_idx], gains, layer_idx, first_row, share
        )
        norm_grad = (
            norm_grad.at[0, 2 * layer_idx].set(attn_norm[0]).at[1, 2 * layer_idx].set(attn_norm[1])
        )
        norm_grad = (
            norm_grad.at[0, 2 * layer_idx + 1]
            .set(mlp_norm[0])
            .at[1, 2 * layer_idx + 1]
            .set(mlp_norm[1])
        )
    first_grads = lax.dynamic_slice_in_dim(gradient, first_row, share, 0)
    embed_grad = embed_grad.at[:, lax.dynamic_slice_in_dim(inputs, first_row, share, 0)].add(
        first_grads.T
    )
    places = context_at * half_len + jnp.arange(row_count, dtype=jnp.int32) % half_len
    position_grad = (
        jnp.zeros(position_all.shape, jnp.float32)
        .at[:, lax.dynamic_slice_in_dim(places, first_row, share, 0)]
        .add(first_grads.T)
    )
    slot_grads = (
        jnp.zeros(slot_all.shape, jnp.float32).at[tile_slot].set(jnp.concatenate(tile_grads, 0))
    )
    owned, embed_grad, position_grad, norm_grad = (
        lax.psum_scatter(
            slot_grads.astype(jnp.bfloat16), "fsdp", scatter_dimension=0, tiled=True
        ).astype(jnp.float32),
        lax.psum_scatter(
            embed_grad.astype(jnp.bfloat16), "fsdp", scatter_dimension=0, tiled=True
        ).astype(jnp.float32),
        lax.psum_scatter(
            position_grad.astype(jnp.bfloat16), "fsdp", scatter_dimension=0, tiled=True
        ).astype(jnp.float32),
        lax.psum_scatter(
            norm_grad.astype(jnp.bfloat16), "fsdp", scatter_dimension=2, tiled=True
        ).astype(jnp.float32),
    )
    owned = lax.psum(owned.astype(jnp.bfloat16), "ctx").astype(jnp.float32)
    embed_grad, position_grad, norm_grad = (
        lax.psum(embed_grad.astype(jnp.bfloat16), ("ctx", "tp")).astype(jnp.float32),
        lax.psum(position_grad.astype(jnp.bfloat16), ("ctx", "tp")).astype(jnp.float32),
        lax.psum(norm_grad.astype(jnp.bfloat16), ("ctx", "tp")).astype(jnp.float32),
    )
    bias_grad = lax.psum(bias_grad, ("fsdp", "ctx", "tp"))
    slot_count = tile_master.shape[0]
    owned_slots = owner_at * slot_count + jnp.arange(slot_count, dtype=jnp.int32)
    in_use = jnp.any(owned_slots[:, None] == tile_slot[None, :], 1)[:, None, None]
    tile_upd = adamw_update(tile_master, tile_first, tile_second, owned, learn_rate)
    tile_new = jnp.where(in_use, tile_upd[0], tile_master)
    tile_one = jnp.where(in_use, tile_upd[1], tile_first)
    tile_two = jnp.where(in_use, tile_upd[2], tile_second)
    embed_upd = adamw_update(embedding, embed_first, embed_second, embed_grad, learn_rate)
    position_upd = adamw_update(
        position_table, position_first, position_second, position_grad, learn_rate
    )
    norm_upd = adamw_update(norm_params, norm_first, norm_second, norm_grad, small_rate)
    bias_upd = adamw_update(head_bias, bias_first, bias_second, bias_grad, small_rate)
    return (
        loss_value,
        tile_new,
        tile_one,
        tile_two,
        embed_upd[0],
        embed_upd[1],
        embed_upd[2],
        position_upd[0],
        position_upd[1],
        position_upd[2],
        norm_upd[0],
        norm_upd[1],
        norm_upd[2],
        bias_upd[0],
        bias_upd[1],
        bias_upd[2],
    )


def solution(mesh):
    placed = (
        P("fsdp", "ctx"),
        P("fsdp", "ctx"),
        P(),
        P("fsdp", "tp", None),
        P("fsdp", "tp", None),
        P("fsdp", "tp", None),
        P("fsdp", None),
        P("fsdp", None),
        P("fsdp", None),
        P("fsdp", None),
        P("fsdp", None),
        P("fsdp", None),
        P(None, None, "fsdp"),
        P(None, None, "fsdp"),
        P(None, None, "fsdp"),
        P(),
        P(),
        P(),
    )
    return jax.shard_map(
        body,
        mesh=mesh,
        in_specs=placed,
        out_specs=(
            P(),
            P("fsdp", "tp", None),
            P("fsdp", "tp", None),
            P("fsdp", "tp", None),
            P("fsdp", None),
            P("fsdp", None),
            P("fsdp", None),
            P("fsdp", None),
            P("fsdp", None),
            P("fsdp", None),
            P(None, None, "fsdp"),
            P(None, None, "fsdp"),
            P(None, None, "fsdp"),
            P(),
            P(),
            P(),
        ),
        check_vma=False,
    )
```

profile of v0, /device:TPU:0, one launch (start us, length us, event | category | flops | bytes accessed | tf_op | source)
XLA Modules:
  0.0 1730.2 jit_solution(15479206718880842699)
XLA Ops:
  16.5 21.3 %all_gather.36 = bf16[2,7,768]{1,0,2:T(2,128)(2,1)S(1)} all-gather(bf16[2,7,192]{1,0,2:T(2,128)(2,1)S(1)} %copy.119), channel_id=1, replica_groups=mesh['fsdp'=4,'ctx'=2,'tp'=4] {'fsdp'}, dimensions={2}, use_global_device_ids=true | all-gather | bytes 26880 | tf_op jit(solution)/shard_map/all_gather | solution.py:240
  38.8 39.3 %slice_reduce_fusion.1 = (f32[768]{0:T(1024)S(1)}, f32[768]{0:T(1024)S(1)}, f32[768]{0:T(1024)S(1)}, f32[768]{0:T(1024)S(1)}, f32[768]{0:T(1024)S(1)}, /*index=5...) fusion(f32[2,7,768]{1,0,2:T(2,128)S(1)} %convert_element_type.450), kind=kLoop, calls=%fused_computation.279 | loop fusion | bytes 86016 | tf_op jit(solution)/shard_map/slice | solution.py:263
  80.6 39.7 %all-gather.4.cloned.1.call-done = bf16[768,2025]{1,0:T(8,128)(2,1)} async-done(((bf16[192,2025]{1,0:T(8,128)(2,1)}), bf16[768,2025]{1,0:T(8,128)(2,1)}) %all-gather.4.cloned.1.call-update) | async-done | bytes 3110416 | tf_op jit(solution)/shard_map/all_gather | solution.py:238
  130.2 234.9 %all-gather.8.cloned.1.call-done = bf16[48,192,768]{2,1,0:T(8,128)(2,1)} async-done(((bf16[12,192,768]{2,1,0:T(8,128)(2,1)}), bf16[48,192,768]{2,1,0:T(8,128)(2,1)}) %all-gather.8.cloned.1.call-update) | async-done | bytes 14155792 | tf_op jit(solution)/shard_map/all_gather | solution.py:237
  390.3 47.0 %all-reduce.17.cloned.1.call-done = bf16[512,768]{1,0:T(8,128)(2,1)} async-done(((bf16[512,768]{1,0:T(8,128)(2,1)}), bf16[512,768]{1,0:T(8,128)(2,1)}) %all-reduce.17.cloned.1.call-update) | async-done | bytes 786448 | tf_op jit(solution)/shard_map/psum | solution.py:45
  450.1 48.8 %all-reduce.19.cloned.1.call-done = bf16[512,768]{1,0:T(8,128)(2,1)} async-done(((bf16[512,768]{1,0:T(8,128)(2,1)}), bf16[512,768]{1,0:T(8,128)(2,1)}) %all-reduce.19.cloned.1.call-update) | async-done | bytes 786448 | tf_op jit(solution)/shard_map/psum | solution.py:45
  516.6 48.8 %all-reduce.21.cloned.1.call-done = bf16[512,768]{1,0:T(8,128)(2,1)} async-done(((bf16[512,768]{1,0:T(8,128)(2,1)}), bf16[512,768]{1,0:T(8,128)(2,1)}) %all-reduce.21.cloned.1.call-update) | async-done | bytes 786448 | tf_op jit(solution)/shard_map/psum | solution.py:45
  578.7 48.8 %all-reduce.23.cloned.1.call-done = bf16[512,768]{1,0:T(8,128)(2,1)} async-done(((bf16[512,768]{1,0:T(8,128)(2,1)}), bf16[512,768]{1,0:T(8,128)(2,1)}) %all-reduce.23.cloned.1.call-update) | async-done | bytes 786448 | tf_op jit(solution)/shard_map/psum | solution.py:45
  645.0 48.6 %all-reduce.25.cloned.1.call-done = bf16[512,768]{1,0:T(8,128)(2,1)} async-done(((bf16[512,768]{1,0:T(8,128)(2,1)}), bf16[512,768]{1,0:T(8,128)(2,1)}) %all-reduce.25.cloned.1.call-update) | async-done | bytes 786448 | tf_op jit(solution)/shard_map/psum | solution.py:45
  707.8 39.6 %psum.140 = f32[]{:T(128)} all-reduce(f32[]{:T(128)} %fusion.170), channel_id=1, replica_groups=mesh['fsdp'=4,'ctx'=2,'tp'=4] {'fsdp','ctx','tp'}, use_global_device_ids=true, to_apply=%region_32.33 | all-reduce | flops 1 | bytes 8 | tf_op jit(solution)/shard_map/psum | solution.py:275
  784.6 48.6 %all-reduce.29.cloned.1.call-done = bf16[512,768]{1,0:T(8,128)(2,1)} async-done(((bf16[512,768]{1,0:T(8,128)(2,1)}), bf16[512,768]{1,0:T(8,128)(2,1)}) %all-reduce.29.cloned.1.call-update) | async-done | bytes 786448 | tf_op jit(solution)/shard_map/psum | solution.py:49
  872.2 50.6 %all-reduce.31.cloned.1.call-done = bf16[512,768]{1,0:T(8,128)(2,1)} async-done(((bf16[512,768]{1,0:T(8,128)(2,1)}), bf16[512,768]{1,0:T(8,128)(2,1)}) %all-reduce.31.cloned.1.call-update) | async-done | bytes 786448 | tf_op jit(solution)/shard_map/psum | solution.py:49
  934.5 48.4 %all-reduce.33.cloned.1.call-done = bf16[512,768]{1,0:T(8,128)(2,1)} async-done(((bf16[512,768]{1,0:T(8,128)(2,1)}), bf16[512,768]{1,0:T(8,128)(2,1)}) %all-reduce.33.cloned.1.call-update) | async-done | bytes 786448 | tf_op jit(solution)/shard_map/psum | solution.py:49
  1020.0 50.6 %all-reduce.35.cloned.1.call-done = bf16[512,768]{1,0:T(8,128)(2,1)} async-done(((bf16[512,768]{1,0:T(8,128)(2,1)}), bf16[512,768]{1,0:T(8,128)(2,1)}) %all-reduce.35.cloned.1.call-update) | async-done | bytes 786448 | tf_op jit(solution)/shard_map/psum | solution.py:49
  1081.6 48.6 %all-reduce.37.cloned.1.call-done = bf16[512,768]{1,0:T(8,128)(2,1)} async-done(((bf16[512,768]{1,0:T(8,128)(2,1)}), bf16[512,768]{1,0:T(8,128)(2,1)}) %all-reduce.37.cloned.1.call-update) | async-done | bytes 786448 | tf_op jit(solution)/shard_map/psum | solution.py:49
  1171.5 46.5 %all-reduce.41.cloned.1.call-done = bf16[512,768]{1,0:T(8,128)(2,1)} async-done(((bf16[512,768]{1,0:T(8,128)(2,1)}), bf16[512,768]{1,0:T(8,128)(2,1)}) %all-reduce.41.cloned.1.call-update) | async-done | bytes 786448 | tf_op jit(solution)/shard_map/psum | solution.py:49
  1306.2 36.3 %scatter_fusion = f32[48,192,768]{2,1,0:T(8,128)} fusion(f32[48,192,768]{2,1,0:T(8,128)} %broadcast_in_dim.51, s32[36]{0:T(128)S(1)} %copy-done.161, f32[36,192,768]{2,1,0:T(8,128)} %convolution_dynamic-update-slice_fusion), kind=kCustom, calls=%fused_computation.2 | custom fusion | bytes 63701136 | tf_op jit(solution)/shard_map/scatter | solution.py:329
  1342.5 16.1 convert_element_type.548
  1389.3 207.2 %reduce-scatter.29.cloned.1.call-done = bf16[12,192,768]{2,1,0:T(8,128)(2,1)} async-done(((bf16[48,192,768]{2,1,0:T(8,128)(2,1)}), bf16[12,192,768]{2,1,0:T(8,128)(2,1)}) %reduce-scatter.29.cloned.1.call-update) | async-done | bytes 3538960 | tf_op jit(solution)/shard_map/reduce_scatter | solution.py:332
  1597.4 41.5 %all-reduce = (f32[]{:T(128)}, f32[2025]{0:T(1024)S(1)}) all-reduce(f32[]{:T(128)} %get-tuple-element.336, f32[2025]{0:T(1024)S(1)} %copy-done.125), channel_id=1, replica_groups=mesh['fsdp'=4,'ctx'=2,'tp'=4] {'fsdp','ctx','tp'}, use_global_device_ids=true, to_apply=%region_30.31 | all-reduce | flops 2026 | bytes 16208 | tf_op jit(solution)/shard_map/psum | solution.py:275
  1642.2 15.5 psum.150
  1658.5 20.9 %all-reduce.43.cloned.1.call-done = (bf16[192,2025]{1,0:T(8,128)(2,1)}, bf16[192,1024]{1,0:T(8,128)(2,1)}) async-done(((bf16[192,2025]{1,0:T(8,128)(2,1)}, bf16[192,1024]{1,0:T(8,128)(2,1)}), (bf16[192,2025]{1,0:T(8,128)(2,1)}, bf16[192,1024]{1,0:T(8,128)(2,1)})) %all-reduce.43.cloned.1.call-update) | async-done | bytes 1170832 | tf_op jit(solution)/shard_map/psum | solution.py:347
  1686.5 18.0 %all-reduce.39.cloned.1.call-done = bf16[12,192,768]{2,1,0:T(8,128)(2,1)} async-done(((bf16[12,192,768]{2,1,0:T(8,128)(2,1)}), bf16[12,192,768]{2,1,0:T(8,128)(2,1)}) %all-reduce.39.cloned.1.call-update) | async-done | bytes 3538960 | tf_op jit(solution)/shard_map/psum | solution.py:345
  1704.5 17.6 %fusion.2 = (f32[12,192,768]{2,1,0:T(8,128)}, f32[12,192,768]{2,1,0:T(8,128)}, f32[12,192,768]{2,1,0:T(8,128)}) fusion(f32[12,192,768]{2,1,0:T(8,128)} %param.51, bf16[12,192,768]{2,1,0:T(8,128)(2,1)} %all-reduce.39.cloned.1.call-done, pred[12]{0:T(512)(128)(4,1)S(1)} %compare_reduce_fusion, f32[12,192,768]{2,1,0:T(8,128)} %param.49, f32[12,192,768]{2,1,0:T(8,128)} %param.50), kind=kLoop, calls=%fused_computation.25 | loop fusion | flops 33619968 | bytes 46006284 | tf_op jit(solution)/shard_map/jit(_where)/select_n | solution.py:358
  (697 shorter events, 427.1 us)
Async XLA Ops:
  7.2 71.1 %all-gather.6.cloned.1.call-start = ((), (), s32[]{:S(2)}) async-start(), calls=%async_computation.11 | async-start | bytes 1966080 | tf_op jit(solution)/shard_map/all_gather | solution.py:239
  9.3 111.0 %all-gather.4.cloned.1.call-start = ((), (), s32[]{:S(2)}) async-start(), calls=%async_computation.10 | async-start | bytes 3932160 | tf_op jit(solution)/shard_map/all_gather | solution.py:238
  10.4 354.7 %all-gather.8.cloned.1.call-start = ((), (), s32[]{:S(2)}) async-start(), calls=%async_computation.12 | async-start | bytes 17694720 | tf_op jit(solution)/shard_map/all_gather | solution.py:237
  15.7 421.7 %all-reduce.17.cloned.1.call-start = ((), (), s32[]{:S(2)}) async-start(), calls=%async_computation.13 | async-start | bytes 1572864 | tf_op jit(solution)/shard_map/psum | solution.py:45
  390.3 108.6 %all-reduce.19.cloned.1.call-start = ((), (), s32[]{:S(2)}) async-start(), calls=%async_computation.14 | async-start | bytes 1572864 | tf_op jit(solution)/shard_map/psum | solution.py:45
  450.0 115.4 %all-reduce.21.cloned.1.call-start = ((), (), s32[]{:S(2)}) async-start(), calls=%async_computation.15 | async-start | bytes 1572864 | tf_op jit(solution)/shard_map/psum | solution.py:45
  516.6 111.0 %all-reduce.23.cloned.1.call-start = ((), (), s32[]{:S(2)}) async-start(), calls=%async_computation.16 | async-start | bytes 1572864 | tf_op jit(solution)/shard_map/psum | solution.py:45
  578.7 115.0 %all-reduce.25.cloned.1.call-start = ((), (), s32[]{:S(2)}) async-start(), calls=%async_computation.17 | async-start | bytes 1572864 | tf_op jit(solution)/shard_map/psum | solution.py:45
  644.8 111.4 %all-reduce.27.cloned.1.call-start = ((), (), s32[]{:S(2)}) async-start(), calls=%async_computation.18 | async-start | bytes 1572864 | tf_op jit(solution)/shard_map/psum | solution.py:45
  707.1 126.1 %all-reduce.29.cloned.1.call-start = ((), (), s32[]{:S(2)}) async-start(), calls=%async_computation.19 | async-start | bytes 1572864 | tf_op jit(solution)/shard_map/psum | solution.py:49
  784.3 75.3 %reduce-scatter.17.cloned.1.call-start = ((), (), s32[]{:S(2)}) async-start(), calls=%async_computation.20 | async-start | bytes 589824 | tf_op jit(solution)/shard_map/reduce_scatter | solution.py:166
  855.1 67.6 %all-reduce.31.cloned.1.call-start = ((), (), s32[]{:S(2)}) async-start(), calls=%async_computation.22 | async-start | bytes 1572864 | tf_op jit(solution)/shard_map/psum | solution.py:49
  872.1 110.8 %all-reduce.33.cloned.1.call-start = ((), (), s32[]{:S(2)}) async-start(), calls=%async_computation.23 | async-start | bytes 1572864 | tf_op jit(solution)/shard_map/psum | solution.py:49
  934.0 72.8 %reduce-scatter.21.cloned.1.call-start = ((), (), s32[]{:S(2)}) async-start(), calls=%async_computation.24 | async-start | bytes 589824 | tf_op jit(solution)/shard_map/reduce_scatter | solution.py:166
  1003.1 67.4 %all-reduce.35.cloned.1.call-start = ((), (), s32[]{:S(2)}) async-start(), calls=%async_computation.26 | async-start | bytes 1572864 | tf_op jit(solution)/shard_map/psum | solution.py:49
  1020.0 110.3 %all-reduce.37.cloned.1.call-start = ((), (), s32[]{:S(2)}) async-start(), calls=%async_computation.27 | async-start | bytes 1572864 | tf_op jit(solution)/shard_map/psum | solution.py:49
  1081.4 72.7 %reduce-scatter.25.cloned.1.call-start = ((), (), s32[]{:S(2)}) async-start(), calls=%async_computation.28 | async-start | bytes 589824 | tf_op jit(solution)/shard_map/reduce_scatter | solution.py:166
  1150.4 67.6 %all-reduce.41.cloned.1.call-start = ((), (), s32[]{:S(2)}) async-start(), calls=%async_computation.32 | async-start | bytes 1572864 | tf_op jit(solution)/shard_map/psum | solution.py:49
  1167.2 221.5 %reduce-scatter.33.cloned.1.call-start = ((), (), s32[]{:S(2)}) async-start(), calls=%async_computation.34 | async-start | bytes 1966080 | tf_op jit(solution)/shard_map/reduce_scatter | solution.py:338
  1233.3 155.5 %reduce-scatter.31.cloned.1.call-start = ((), (), s32[]{:S(2)}) async-start(), calls=%async_computation.33 | async-start | bytes 3932160 | tf_op jit(solution)/shard_map/reduce_scatter | solution.py:335
  1256.2 340.3 %reduce-scatter.29.cloned.1.call-start = ((), (), s32[]{:S(2)}) async-start(), calls=%async_computation.30 | async-start | bytes 17694720 | tf_op jit(solution)/shard_map/reduce_scatter | solution.py:332
  1358.7 282.2 %reduce-scatter.35.cloned.1.call-start = ((), (), s32[]{:S(2)}) async-start(), calls=%async_computation.35 | async-start | bytes 245760
  1388.7 290.6 %all-reduce.43.cloned.1.call-start = ((), (), s32[]{:S(2)}) async-start(), calls=%async_computation.36 | async-start | bytes 2359296 | tf_op jit(solution)/shard_map/psum | solution.py:347
  1389.3 315.2 %all-reduce.39.cloned.1.call-start = ((), (), s32[]{:S(2)}) async-start(), calls=%async_computation.31 | async-start | bytes 7077888 | tf_op jit(solution)/shard_map/psum | solution.py:345
  (202 other events, 7127.8 us)
Sparse Core Ops, SparseCore 0:
  10.2 45.0 all-gather.5
  57.4 62.8 all-gather.3
  122.5 242.5 all-gather.7
  390.4 46.9 all-reduce.16
  450.2 48.7 all-reduce.18
  516.7 48.7 all-reduce.20
  578.8 48.7 all-reduce.22
  644.9 48.7 all-reduce.24
  707.2 48.8 all-reduce.26
  784.5 48.7 all-reduce.28
  860.0 8.9 reduce-scatter.18
  872.8 49.8 all-reduce.30
  934.1 48.7 all-reduce.32
  1007.9 8.9 reduce-scatter.22
  1020.6 49.8 all-reduce.34
  1081.5 48.7 all-reduce.36
  1155.1 8.9 reduce-scatter.26
  1168.1 49.8 all-reduce.40
  1233.4 35.2 reduce-scatter.32
  1271.6 59.2 reduce-scatter.30
  1358.8 237.6 reduce-scatter.28
  1599.4 20.4 reduce-scatter.34
  1623.3 55.9 all-reduce.42
  1681.5 22.9 all-reduce.38
  (3 shorter events, 23.1 us)
where the time goes:
time: 1740 us; the launch traced here: 1730 us
  waiting for transfers between devices  1090 us (63%)
  matrix products  180 us (10%)
  local copies, waits for them, and re-layouts  150 us (9%)
  other arithmetic  142 us (8%)
  blocking collectives  142 us (8%)
  between operations  19.6 us (1%)
    psum x6, waiting for transfers between devices, tensor_backward(): return lax.psum(partial_grad.astype(jnp.bfloat16), 'tp').astype(jnp.float32)  293 us
    psum x6, waiting for transfers between devices, tensor_forward(): return lax.psum(partial_out.astype(jnp.bfloat16), 'tp').astype(jnp.float32)  250 us
    all_gather x1, waiting for transfers between devices, body(): lax.all_gather(tile_master.astype(jnp.bfloat16), 'fsdp', axis=0, tiled=True)  235 us
    reduce_scatter x1, waiting for transfers between devices, body(): lax.psum_scatter(slot_grads.astype(jnp.bfloat16), 'fsdp', scatter_dimensi...  207 us
    psum x2, blocking collectives, body(): lax.psum((jnp.sum((log_total[:, 0] - picked) * row_weights), jnp.sum(row_...  81.1 us
    all_gather x1, waiting for transfers between devices, body(): lax.all_gather(embedding.astype(jnp.bfloat16), 'fsdp', axis=0, tiled=True)  39.7 us
    slice x1, local copies, waits for them, and re-layouts, body(): gains[0, 2 * LAYERS]  39.3 us
    scatter x1, local copies, waits for them, and re-layouts, body(): jnp.zeros(slot_all.shape, jnp.float32).at[tile_slot]  36.3 us
  transfers between devices with their start and end apart: 27, of which 20 were waited for; matrix products, arithmetic and copies ran while one was open for 15% of the time, Pallas kernels for 0%

commit v1 on v0

v1 whole, which is shorter than its diff:
```python
import functools

import jax
import jax.numpy as jnp
from jax import lax
from jax.experimental import pallas as pl
from jax.experimental.pallas import tpu as pltpu
from jax.sharding import PartitionSpec as P

HEAD_DIM = 48
VOCAB = 2025
LAYERS = 3
STEP = 10
TILES = 36
BLOCK = 256
GROUP = 2
LAG = 2

norm_eps = 1e-05
beta_first = 0.9
beta_second = 0.999
learn_rate = 0.05
small_rate = 0.5
weight_decay = 0.01
adam_eps = 1e-08

bf16 = jnp.bfloat16
f32 = jnp.float32
FLIP_X = [(i, i ^ 1) for i in range(4)]
FLIP_Y = [(i, i ^ 2) for i in range(4)]
FLIP_CORE = [(0, 1), (1, 0)]


def over_x(v):
    return lax.ppermute(v, "tp", FLIP_X)


def over_y(v):
    return lax.ppermute(v, "tp", FLIP_Y)


def over_core(v):
    return lax.ppermute(v, "ctx", FLIP_CORE)


def dot(left, right, dims):
    return lax.dot_general(left, right, (dims, ((), ())), preferred_element_type=f32)


def norm_parts(stream, gain, shift):
    centered = stream - jnp.mean(stream, -1, keepdims=True)
    inverse = lax.rsqrt(jnp.mean(centered * centered, -1, keepdims=True) + norm_eps)
    normal_hat = centered * inverse
    return (normal_hat * gain + shift, normal_hat, inverse)


def norm_back(gradient, normal_hat, inverse, gain):
    scaled = gradient * gain
    return inverse * (
        scaled
        - jnp.mean(scaled, -1, keepdims=True)
        - normal_hat * jnp.mean(scaled * normal_hat, -1, keepdims=True)
    )


def gelu_slope(pre_gelu):
    return (
        0.5 * (1.0 + lax.erf(pre_gelu * 0.7071067811865476))
        + pre_gelu * jnp.exp(-0.5 * pre_gelu * pre_gelu) * 0.3989422804014327
    )


def sum_over_x(partial):
    mine = partial.astype(bf16)
    return mine.astype(f32) + over_x(mine).astype(f32)


def pick(options):
    out = options[-1][1]
    for cond, value in options[-2::-1]:
        out = jnp.where(cond, value, out)
    return out


class Wave:
    def __init__(self, count, n, at):
        self.count, self.n, self.at = count, n, at
        self.right, self.left, self.chunks = [], [], []
        self.steps = count + LAG * max(n - 2, 0) if n > 1 else 0

    def advance(self, chunks):
        n, at = self.n, self.at
        self.chunks = chunks
        while len(self.right) < self.steps:
            s = len(self.right)
            if min(s, self.count - 1) >= len(chunks):
                break
            own_right = [(at == i, chunks[s - LAG * i]) for i in range(n - 1) if 0 <= s - LAG * i < self.count]
            own_left = [(at == n - 1 - i, chunks[s - LAG * i]) for i in range(n - 1) if 0 <= s - LAG * i < self.count]
            go_right, go_left = pick(own_right), pick(own_left)
            if s >= LAG:
                go_right = (go_right.astype(f32) + self.right[s - LAG].astype(f32)).astype(bf16)
                go_left = (go_left.astype(f32) + self.left[s - LAG].astype(f32)).astype(bf16)
            self.right.append(lax.ppermute(go_right, "fsdp", [(i, i + 1) for i in range(n - 1)]))
            self.left.append(lax.ppermute(go_left, "fsdp", [(i + 1, i) for i in range(n - 1)]))

    def total(self, c):
        n, at = self.n, self.at
        own = self.chunks[c].astype(f32)
        if n == 1:
            return own.astype(bf16)
        zero = jnp.zeros((), bf16)
        from_left = pick([(at == j, self.right[c + LAG * (j - 1)]) for j in range(1, n)] + [(None, zero)])
        from_right = pick([(at == j, self.left[c + LAG * (n - 2 - j)]) for j in range(n - 1)] + [(None, zero)])
        return (own + (from_left.astype(f32) + from_right.astype(f32))).astype(bf16)


def spread_kernel(where_ref, mine_ref, core_ref, tile_ref, out_ref):
    t = pl.program_id(0)
    out_ref[...] = jnp.where(mine_ref[t] == 1, tile_ref[...], 0.0).astype(bf16)


def spread_tiles(tile_master, place, mine, core, first, count, half):
    width = tile_master.shape[2]
    return pl.pallas_call(
        spread_kernel,
        grid_spec=pltpu.PrefetchScalarGridSpec(
            num_scalar_prefetch=3,
            grid=(count,),
            in_specs=[pl.BlockSpec((1, half, width), lambda t, w, m, c: (w[t], c[0], 0))],
            out_specs=pl.BlockSpec((1, half, width), lambda t, w, m, c: (t, 0, 0)),
        ),
        out_shape=jax.ShapeDtypeStruct((count, half, width), bf16),
        name="spread_tiles",
    )(place[first:first + count], mine[first:first + count], core, tile_master)


def adamw_update(weight, moment_one, moment_two, gradient, rate):
    moment_one = beta_first * moment_one + (1.0 - beta_first) * gradient
    moment_two = beta_second * moment_two + (1.0 - beta_second) * gradient * gradient
    first_hat = moment_one / (1.0 - beta_first**STEP)
    second_hat = moment_two / (1.0 - beta_second**STEP)
    weight = weight - rate * (first_hat / (jnp.sqrt(second_hat) + adam_eps) + weight_decay * weight)
    return (weight, moment_one, moment_two)


def tile_adamw_kernel(tile_ref, used_ref, core_ref, w_ref, m_ref, v_ref, g_ref, w_out, m_out, v_out):
    slot = pl.program_id(0)

    @pl.when(used_ref[slot] == 1)
    def _():
        new = adamw_update(w_ref[...], m_ref[...], v_ref[...], g_ref[0].astype(f32), learn_rate)
        w_out[...], m_out[...], v_out[...] = new

    @pl.when(used_ref[slot] != 1)
    def _():
        w_out[...], m_out[...], v_out[...] = w_ref[...], m_ref[...], v_ref[...]


def tile_adamw(tile_of, used, core, weight, first, second, grads):
    slots, rows, width = weight.shape
    half = rows // 2
    block = pl.BlockSpec((1, half, width), lambda s, h, t, u, c: (s, h, 0))
    grad_block = pl.BlockSpec((1, 1, half, width), lambda s, h, t, u, c: (h ^ c[0], t[s], 0, 0))
    return pl.pallas_call(
        tile_adamw_kernel,
        grid_spec=pltpu.PrefetchScalarGridSpec(
            num_scalar_prefetch=3,
            grid=(slots, 2),
            in_specs=[block, block, block, grad_block],
            out_specs=[block, block, block],
        ),
        out_shape=[jax.ShapeDtypeStruct(weight.shape, f32)] * 3,
        name="tile_adamw",
    )(tile_of, used, core, weight, first, second, grads)


def line_parts(take, n, at):
    got = []
    for m in range(-(n - 1), n):
        k = -m
        part = take(jnp.clip(at + k, 0, n - 1))
        if m:
            part = lax.ppermute(part, "fsdp", [(i, i + k) for i in range(n) if 0 <= i + k < n])
        got.append(part)
    return lax.dynamic_slice_in_dim(jnp.stack(got), n - 1 - at, n, 0)


def sum_all(v, axes, n):
    for axis in axes:
        if axis == "fsdp":
            bit = 1
            while bit < n:
                v = v + lax.ppermute(v, "fsdp", [(i, i ^ bit) for i in range(n)])
                bit *= 2
        elif axis == "ctx":
            v = v + over_core(v)
        elif axis == "x":
            v = v + over_x(v)
        else:
            v = v + over_y(v)
    return v


def turn(v, bit, axis):
    half = v.shape[axis] // 2
    a = lax.slice_in_dim(v, 0, half, axis=axis)
    b = lax.slice_in_dim(v, half, 2 * half, axis=axis)
    return lax.concatenate([jnp.where(bit == 1, b, a), jnp.where(bit == 1, a, b)], axis)


def by_place(v, index, bits, axis):
    size = v.shape[axis] >> bits
    shape = v.shape[:axis] + (2,) * bits + (size,) + v.shape[axis + 1:]
    v = v.reshape(shape)
    for b in range(bits):
        v = turn(v, (index >> (bits - 1 - b)) & 1, axis + b)
    return v.reshape(v.shape[:axis] + (size << bits,) + v.shape[axis + bits + 1:])


def swap_rows(kv, outer, piece):
    v = kv.reshape(2, 2, 2, piece, kv.shape[-1])
    v = v[:, ::-1] if outer else v[:, :, ::-1]
    return v.reshape(kv.shape)


def body(
    token_ids,
    masked,
    tile_slot,
    tile_master,
    tile_first,
    tile_second,
    embedding,
    embed_first,
    embed_second,
    position_table,
    position_first,
    position_second,
    norm_params,
    norm_first,
    norm_second,
    head_bias,
    bias_first,
    bias_second,
):
    n = lax.axis_size("fsdp")
    z = lax.axis_index("fsdp")
    core = lax.axis_index("ctx")
    tp = lax.axis_index("tp")
    tx, ty = tp % 2, tp // 2
    slots, width, model = tile_master.shape
    half = width // 2
    columns = 2 * width
    heads = columns // HEAD_DIM
    half_len = token_ids.shape[1]
    rows = half_len // 2
    share = rows // 2
    own_dim = embedding.shape[0]
    norms = norm_params.shape[1]
    core_arr = core.reshape(1).astype(jnp.int32)

    ids_half = jnp.where(masked == 1, VOCAB - 1, token_ids)
    ids = lax.dynamic_slice(ids_half, (0, ty * rows), (1, rows))
    count = sum_all(
        jnp.broadcast_to(jnp.sum(masked).astype(f32), (8, 128)), ("fsdp", "ctx"), n
    )[0, 0]

    local = tile_slot - z * slots
    mine = ((local >= 0) & (local < slots)).astype(jnp.int32)
    place = jnp.clip(local, 0, slots - 1)
    own_tiles = spread_tiles(tile_master, place, mine, core_arr, 0, TILES, half)
    chunk_count = TILES // GROUP
    wave = Wave(chunk_count, n, z)
    wave.advance([own_tiles[c * GROUP:(c + 1) * GROUP] for c in range(chunk_count)])

    def full_rows(c):
        own = wave.total(c)
        both = jnp.stack([own, over_y(own)], 1)
        every = jnp.stack([both, over_core(both)], 1)
        return every.reshape(GROUP, columns, model)

    block_at = core * 4 + tp
    vocab_pad = 8 * BLOCK - VOCAB
    embed_pad = jnp.pad(embedding.astype(bf16), ((0, 0), (0, vocab_pad)))
    packed = jnp.concatenate(
        [
            lax.dynamic_slice(embed_pad, (0, block_at * BLOCK), (own_dim, BLOCK)),
            lax.dynamic_slice(
                position_table, (0, core * half_len + ty * rows), (own_dim, rows)
            ).astype(bf16),
            jnp.pad(
                norm_params.astype(bf16).reshape(2 * norms, own_dim).T, ((0, 0), (0, 128 - 2 * norms))
            ),
        ],
        1,
    )
    tables = line_parts(lambda j: packed, n, z).reshape(model, BLOCK + rows + 128)
    embed_own = tables[:, :BLOCK]
    places_own = tables[:, BLOCK:BLOCK + rows].T.astype(f32)
    gains = tables[:, BLOCK + rows:BLOCK + rows + 2 * norms].T.reshape(2, norms, model).astype(f32)
    embed_two = jnp.concatenate([embed_own, over_x(embed_own)], 1)
    embed_four = jnp.concatenate([embed_two, over_y(embed_two)], 1)
    embed_all = jnp.concatenate([embed_four, over_core(embed_four)], 1)

    def own_column(token):
        return (((token // BLOCK) ^ block_at) * BLOCK) + token % BLOCK

    column_at = lax.broadcasted_iota(jnp.int32, (1, 8 * BLOCK), 1)
    real = own_column(column_at) < VOCAB
    pick_ids = (own_column(ids).reshape(rows, 1) == column_at).astype(bf16)
    stream = dot(pick_ids, embed_all, ((1,), (1,))) + places_own

    all_ids = line_parts(lambda j: ids, n, z).reshape(n, 1, rows)
    all_ids = jnp.concatenate([all_ids, over_y(all_ids)], 1)
    all_ids = jnp.concatenate([all_ids, over_core(all_ids)], 1)

    scale = HEAD_DIM ** (-0.5)
    weights, kept_layers = [], []
    for layer in range(LAYERS):
        first = layer * 12 // GROUP
        got = [full_rows(c) for c in range(first, first + 12 // GROUP)]
        tiles = jnp.concatenate(got, 0)
        w_qkv = tiles[0:3].reshape(3 * columns, model)
        w_o = tiles[3]
        w_in = tiles[4:8].reshape(4 * columns, model)
        w_out = tiles[8:12].reshape(4 * columns, model)
        weights.append((w_qkv, w_o, w_in, w_out))
        normed = norm_parts(stream, gains[0, 2 * layer], gains[1, 2 * layer])[0].astype(bf16)
        kv = dot(w_qkv[columns:], normed, ((1,), (1,))).astype(bf16)
        kv_two = jnp.stack([kv, swap_rows(over_y(kv), False, half)])
        kv_other = over_core(kv_two)
        kv_other = jnp.stack([swap_rows(kv_other[0], True, half), swap_rows(kv_other[1], True, half)])
        kv_all = jnp.concatenate([kv_two, kv_other], 0)
        kv_all = kv_all.transpose(1, 0, 2).reshape(2, heads, HEAD_DIM, 4 * rows)
        queries = dot(w_qkv[:columns], normed, ((1,), (1,))).astype(bf16).reshape(heads, HEAD_DIM, rows)
        keys, values = kv_all[0], kv_all[1]
        scores = jnp.einsum("hcq,hck->hqk", queries, keys, preferred_element_type=f32) * scale
        row_top = jnp.max(scores, -1, keepdims=True)
        log_total = row_top + jnp.log(jnp.sum(jnp.exp(scores - row_top), -1, keepdims=True))
        attn = jnp.exp(scores - log_total).astype(bf16)
        mixed = (
            jnp.einsum("hqk,hck->hcq", attn, values, preferred_element_type=f32)
            .astype(bf16)
            .reshape(columns, rows)
        )
        middle = stream + sum_over_x(dot(mixed, w_o, ((0,), (0,))))
        normed_mlp = norm_parts(middle, gains[0, 2 * layer + 1], gains[1, 2 * layer + 1])[0].astype(bf16)
        pre_gelu = dot(normed_mlp, w_in, ((1,), (1,)))
        activation = jax.nn.gelu(pre_gelu, approximate=False).astype(bf16)
        kept_layers.append((stream, middle, queries, keys, values, log_total, mixed, pre_gelu))
        stream = middle + sum_over_x(dot(activation, w_out, ((1,), (0,))))

    final_rows = lax.dynamic_slice_in_dim(stream, tx * share, share, 0)
    final_normed, hat_final, inv_final = norm_parts(final_rows, gains[0, 2 * LAYERS], gains[1, 2 * LAYERS])
    final_normed = final_normed.astype(bf16)
    bias_own = by_place(jnp.pad(head_bias, (0, vocab_pad)).reshape(1, 8 * BLOCK), block_at, 3, 1)
    logits = dot(final_normed, embed_all, ((1,), (0,))) + bias_own
    logits = jnp.where(real, logits, -1e30)
    start = ty * rows + tx * share
    targets = lax.dynamic_slice(token_ids, (0, start), (1, share)).reshape(share, 1)
    row_weights = lax.dynamic_slice(masked, (0, start), (1, share)).reshape(share, 1).astype(f32)
    row_top = jnp.max(logits, -1, keepdims=True)
    log_total = row_top + jnp.log(jnp.sum(jnp.exp(logits - row_top), -1, keepdims=True))
    is_target = own_column(targets) == column_at
    picked = jnp.sum(jnp.where(is_target, logits, 0.0), -1, keepdims=True)
    loss_part = jnp.sum((log_total - picked) * row_weights)
    grad_logits = (
        (jnp.exp(logits - log_total) - is_target.astype(f32)) * (row_weights / count)
    ).astype(bf16)
    bias_part = by_place(jnp.sum(grad_logits.astype(f32), 0, keepdims=True), block_at, 3, 1)
    bias_part = jnp.where(column_at == 8 * BLOCK - 1, loss_part, bias_part)
    bias_sum = sum_all(bias_part, ("x", "y", "ctx", "fsdp"), n)
    bias_grad = bias_sum[0, :VOCAB]
    loss_value = bias_sum[0, 8 * BLOCK - 1] / count
    grad_final = dot(grad_logits, embed_all, ((1,), (1,)))
    part = norm_back(grad_final, hat_final, inv_final, gains[0, 2 * LAYERS]).astype(bf16)
    other = over_x(part)
    gradient = jnp.concatenate(
        [jnp.where(tx == 0, part, other), jnp.where(tx == 0, other, part)], 0
    ).astype(f32)
    final_norm_grad = jnp.stack([jnp.sum(grad_final * hat_final, 0), jnp.sum(grad_final, 0)])
    final_norm_grad = final_norm_grad + over_x(final_norm_grad)

    embed_part = dot(final_normed, grad_logits, ((0,), (0,))).astype(bf16)

    def fold(v, send):
        cut = v.shape[1] // 2
        return (v[:, :cut].astype(f32) + send(v[:, cut:]).astype(f32)).astype(bf16)

    embed_part = fold(fold(fold(embed_part, over_core), over_y), over_x)
    embed_head = line_parts(
        lambda j: lax.dynamic_slice_in_dim(embed_part, j * own_dim, own_dim, 0), n, z
    )
    embed_head = jnp.sum(embed_head.astype(f32), 0).astype(bf16)
    embed_head = jnp.concatenate([embed_head, over_x(embed_head)], 1)
    embed_head = jnp.concatenate([embed_head, over_y(embed_head)], 1)
    embed_head = jnp.concatenate([embed_head, over_core(embed_head)], 1)

    norm_grads = [None] * norms
    norm_grads[2 * LAYERS] = final_norm_grad
    back = Wave(chunk_count, n, z)
    order, chunks = [], []

    def reduce_tiles(grads, first):
        for c in range(grads.shape[0] // GROUP):
            g = grads[c * GROUP:(c + 1) * GROUP].astype(bf16)
            g = fold(g, over_core)
            g = fold(g, over_y)
            order.append(first // GROUP + c)
            chunks.append(g)
        back.advance(chunks)

    for layer in reversed(range(LAYERS)):
        stream, middle, queries, keys, values, log_total, mixed, pre_gelu = kept_layers[layer]
        w_qkv, w_o, w_in, w_out = weights[layer]
        branch = gradient.astype(bf16)
        activation = jax.nn.gelu(pre_gelu, approximate=False).astype(bf16)
        grad_out = dot(activation, branch, ((0,), (0,))).reshape(4, columns, model)
        reduce_tiles(grad_out, 12 * layer + 8)
        grad_act = dot(branch, w_out, ((1,), (1,)))
        grad_pre = (grad_act * gelu_slope(pre_gelu)).astype(bf16)
        normed_mlp, hat_mlp, inv_mlp = norm_parts(middle, gains[0, 2 * layer + 1], gains[1, 2 * layer + 1])
        grad_normed = sum_over_x(dot(grad_pre, w_in, ((1,), (0,))))
        grad_in = dot(grad_pre, normed_mlp.astype(bf16), ((0,), (0,))).reshape(4, columns, model)
        reduce_tiles(grad_in, 12 * layer + 4)
        grad_middle = gradient + norm_back(grad_normed, hat_mlp, inv_mlp, gains[0, 2 * layer + 1])
        norm_grads[2 * layer + 1] = jnp.stack([jnp.sum(grad_normed * hat_mlp, 0), jnp.sum(grad_normed, 0)])
        branch = grad_middle.astype(bf16)
        grad_proj_out = dot(mixed, branch, ((1,), (0,)))
        grad_mixed = dot(w_o, branch, ((1,), (1,))).astype(bf16).reshape(heads, HEAD_DIM, rows)
        soft = jnp.exp(
            jnp.einsum("hcq,hck->hqk", queries, keys, preferred_element_type=f32) * scale - log_total
        )
        grad_soft = jnp.einsum("hcq,hck->hqk", grad_mixed, values, preferred_element_type=f32)
        grad_scores = (soft * (grad_soft - jnp.sum(soft * grad_soft, -1, keepdims=True))).astype(bf16)
        grad_keys = jnp.einsum("hcq,hqk->hck", queries, grad_scores, preferred_element_type=f32) * scale
        grad_values = jnp.einsum("hcq,hqk->hck", grad_mixed, soft.astype(bf16), preferred_element_type=f32)
        grad_queries = jnp.einsum("hck,hqk->hcq", keys, grad_scores, preferred_element_type=f32) * scale
        grad_kv = jnp.stack([grad_keys, grad_values]).astype(bf16).reshape(2 * columns, 4, rows)
        grad_kv = grad_kv.transpose(1, 0, 2)
        from_core = over_core(grad_kv[2:4])
        pair = [
            grad_kv[i].astype(f32) + swap_rows(from_core[i], True, half).astype(f32) for i in range(2)
        ]
        from_y = swap_rows(over_y(pair[1].astype(bf16)), False, half)
        grad_kv = (pair[0] + from_y.astype(f32)).astype(bf16)
        grad_qkv = jnp.concatenate([grad_queries.astype(bf16).reshape(columns, rows), grad_kv], 0)
        normed, hat_attn, inv_attn = norm_parts(stream, gains[0, 2 * layer], gains[1, 2 * layer])
        grad_normed = sum_over_x(dot(grad_qkv, w_qkv, ((0,), (0,))))
        grad_w = dot(grad_qkv, normed.astype(bf16), ((1,), (0,)))
        grad_w = jnp.concatenate([grad_w, grad_proj_out], 0).reshape(4, columns, model)
        reduce_tiles(grad_w, 12 * layer)
        gradient = grad_middle + norm_back(grad_normed, hat_attn, inv_attn, gains[0, 2 * layer])
        norm_grads[2 * layer] = jnp.stack([jnp.sum(grad_normed * hat_attn, 0), jnp.sum(grad_normed, 0)])

    norm_rows = jnp.stack(norm_grads, 1).reshape(2 * norms, model)
    state = jnp.concatenate(
        [gradient.astype(bf16), norm_rows.astype(bf16), jnp.zeros((16 - 2 * norms, model), bf16)], 0
    )
    state = state.reshape(rows + 16, n, own_dim).transpose(1, 0, 2)
    state = line_parts(lambda j: lax.dynamic_index_in_dim(state, j, 0, False), n, z)[:, None]
    state = jnp.concatenate([state, over_y(state)], 1)
    state = jnp.concatenate([state, over_core(state)], 1)
    norm_grad = jnp.sum(state[:, :, rows:rows + 2 * norms].astype(f32), (0, 1)).reshape(2, norms, own_dim)
    token_grads = state[:, :, :rows]
    position_grad = jnp.sum(token_grads.astype(f32), 0).reshape(4 * rows, own_dim)
    position_grad = by_place(position_grad, core * 2 + ty, 2, 0).T
    choose = (all_ids.reshape(n * 4 * rows, 1) == column_at).astype(bf16)
    embed_tail = dot(token_grads.reshape(n * 4 * rows, own_dim), choose, ((0,), (0,)))
    embed_grad = (embed_tail + by_place(embed_head, block_at, 3, 1).astype(f32))[:, :VOCAB]

    halves = [None] * chunk_count
    for i, c in enumerate(order):
        own = back.total(i)
        halves[c] = jnp.stack([own, over_core(own)])
    grads = jnp.concatenate(halves, 1)
    is_slot = (z * slots + jnp.arange(slots, dtype=jnp.int32))[:, None] == tile_slot[None, :]
    used = jnp.any(is_slot, 1).astype(jnp.int32)
    tile_of = jnp.sum(jnp.where(is_slot, jnp.arange(TILES, dtype=jnp.int32)[None, :], 0), 1)
    tile_upd = tile_adamw(tile_of, used, core_arr, tile_master, tile_first, tile_second, grads)
    embed_upd = adamw_update(embedding, embed_first, embed_second, embed_grad, learn_rate)
    position_upd = adamw_update(position_table, position_first, position_second, position_grad, learn_rate)
    norm_upd = adamw_update(norm_params, norm_first, norm_second, norm_grad, small_rate)
    bias_upd = adamw_update(head_bias, bias_first, bias_second, bias_grad, small_rate)
    return (loss_value, *tile_upd, *embed_upd, *position_upd, *norm_upd, *bias_upd)


def solution(mesh):
    halves, tiles, table = P("fsdp", "ctx"), P("fsdp", "tp", None), P("fsdp", None)
    norms, copied = P(None, None, "fsdp"), P()
    three = lambda spec: (spec,) * 3
    return jax.shard_map(
        body,
        mesh=mesh,
        in_specs=(halves, halves, copied, *three(tiles), *three(table), *three(table), *three(norms), *three(copied)),
        out_specs=(copied, *three(tiles), *three(table), *three(table), *three(norms), *three(copied)),
        check_vma=False,
    )
```

time: 1740 us -> 1410 us (0.81)
  waiting for transfers between devices: 1090 us -> 414 us
  starting transfers between devices: 2.08 us -> 404 us
  blocking collectives: 142 us -> 0 us
  other arithmetic: 142 us -> 231 us
  matrix products: 180 us -> 114 us
  Pallas kernels: 0 us -> 42.2 us
  local copies, waits for them, and re-layouts: 150 us -> 176 us
    psum x14 -> x0, waiting for transfers between devices: 583 us -> none  [the longest x6 293 us: tensor_backward(): return lax.psum(partial_grad.astype(jnp.bfloat16), 'tp').astype(jnp.float32)]
    ppermute x0 -> x249, waiting for transfers between devices: none -> 414 us  [the longest x44 111 us: advance(): lax.ppermute(go_left, 'fsdp', [(i + 1, i) for i in range(n - 1)])]
    ppermute x0 -> x249, starting transfers between devices: none -> 404 us  [the longest x44 193 us: advance(): lax.ppermute(go_right, 'fsdp', [(i, i + 1) for i in range(n - 1)])]
    all_gather x3 -> x0, waiting for transfers between devices: 275 us -> none  [the longest x1 235 us: body(): lax.all_gather(tile_master.astype(jnp.bfloat16), 'fsdp', axis=0, tiled=True)]
    reduce_scatter x9 -> x0, waiting for transfers between devices: 237 us -> none  [the longest x1 207 us: body(): lax.psum_scatter(slot_grads.astype(jnp.bfloat16), 'fsdp', scatter_dimensi...]
    psum x3 -> x0, blocking collectives: 96.6 us -> none  [the longest x2 81.1 us: body(): lax.psum((jnp.sum((log_total[:, 0] - picked) * row_weights), jnp.sum(row_...]
    convert_element_type x17 -> x109, other arithmetic: 45.4 us -> 114 us  [the longest x37 45.4 us: advance(): (go_right.astype(f32) + self.right[s - LAG].astype(f32)).astype(bf16)]
    dot_general x57 -> x62, matrix products: 180 us -> 114 us  [the longest x44 68.9 us: dot(): lax.dot_general(left, right, (dims, ((), ())), preferred_element_type=f32)]
  transfers between devices with their start and end apart: 27 -> 249, of which waited for: 20 -> 87; matrix products, arithmetic and copies ran while one was open for 15% -> 32% of each run, Pallas kernels for 0% -> 0%
where the time goes in v1:
time: 1410 us; the launch traced here: 1390 us
  waiting for transfers between devices  414 us (29%)
  starting transfers between devices  404 us (29%)
  other arithmetic  231 us (16%)
  local copies, waits for them, and re-layouts  176 us (12%)
  matrix products  114 us (8%)
  Pallas kernels  42.2 us (3%)
    ppermute x44, starting transfers between devices, advance(): lax.ppermute(go_right, 'fsdp', [(i, i + 1) for i in range(n - 1)])  193 us
    ppermute x44, waiting for transfers between devices, advance(): lax.ppermute(go_left, 'fsdp', [(i + 1, i) for i in range(n - 1)])  111 us
    ppermute x48, waiting for transfers between devices, over_y(): return lax.ppermute(v, 'tp', FLIP_Y)  100 us
    ppermute x44, waiting for transfers between devices, advance(): lax.ppermute(go_right, 'fsdp', [(i, i + 1) for i in range(n - 1)])  79.6 us
    dot_general x44, matrix products, dot(): lax.dot_general(left, right, (dims, ((), ())), preferred_element_type=f32)  68.9 us
    ppermute x24, waiting for transfers between devices, line_parts(): lax.ppermute(part, 'fsdp', [(i, i + k) for i in range(n) if 0 <= i + k < n])  61.4 us
    ppermute x24, starting transfers between devices, line_parts(): lax.ppermute(part, 'fsdp', [(i, i + k) for i in range(n) if 0 <= i + k < n])  60.7 us
    ppermute x44, starting transfers between devices, advance(): lax.ppermute(go_left, 'fsdp', [(i + 1, i) for i in range(n - 1)])  59.2 us
  transfers between devices with their start and end apart: 249, of which 87 were waited for; matrix products, arithmetic and copies ran while one was open for 32% of the time, Pallas kernels for 0%

profile of v1, /device:TPU:0, one launch (start us, length us, event | category | flops | bytes accessed | tf_op | source)
XLA Modules:
  0.0 1393.4 jit_solution(12791659420422360887)
XLA Ops:
  3.0 16.8 %spread_tiles.1 = bf16[36,96,768]{2,1,0:T(8,128)(2,1)} custom-call(s32[36]{0:T(128)} %subtract_clamp_fusion.where_ref, s32[36]{0:T(128)} %and_convert_fusion.mine_ref, s32[1]{0:T(128)} %bitcast.11.core_ref, f32[12,192,768]{2,1,0:T(8,128)} %w_ref.1), custom_call_target="tpu_custom_call" | custom-call | tf_op jit(solution)/shard_map/spread_tiles/pallas_call | solution.py:125
  21.7 8.0 collective-permute-start.9
  120.0 7.0 collective-permute-done.73
  154.3 8.4 collective-permute-start.229
  235.4 12.8 collective-permute-done.21
  267.0 10.3 collective-permute-done.33
  289.4 9.4 collective-permute-done.50
  303.2 8.1 collective-permute-done.61
  352.6 7.9 collective-permute-done.29
  374.3 8.1 collective-permute-done.46
  409.1 7.4 collective-permute-done.74
  563.2 10.6 collective-permute-done.53
  796.0 7.2 collective-permute-done.138
  836.7 6.9 collective-permute-done.113
  923.8 7.8 collective-permute-start.242
  949.7 7.0 collective-permute-done.245
  1036.7 7.8 collective-permute-done.117
  1191.6 8.4 collective-permute-start.223
  1204.0 7.2 collective-permute-done.224
  1212.5 9.5 collective-permute-done.225
  1223.3 7.5 collective-permute-done.226
  1248.2 10.6 collective-permute-done.122
  1304.8 8.8 fusion
  1366.4 25.4 %tile_adamw.1 = (f32[12,192,768]{2,1,0:T(8,128)}, f32[12,192,768]{2,1,0:T(8,128)}, f32[12,192,768]{2,1,0:T(8,128)}) custom-call(s32[12]{0:T(128)} %fusion.142.tile_ref, s32[12]{0:T(128)} %convert_element_type.2256.used_ref, s32[1]{0:T(128)} %bitcast.11.core_ref, f32[12,192,768]{2,1,0:T(8,128)} %w_ref.1, f32[12,192,768]{2,1,0:T(8,128)} %m_ref.1, ...), custom_call_target="tpu_custom_call" | custom-call | tf_op jit(solution)/shard_map/tile_adamw/pallas_call | solution.py:165
  (1966 shorter events, 1152.2 us)
Async XLA Ops:
  151.6 71.0 %collective-permute-start.12 = (bf16[2,96,768]{2,1,0:T(8,128)(2,1)}, bf16[2,96,768]{2,1,0:T(8,128)(2,1)}, u32[]{:S(2)}, u32[]{:S(2)}) collective-permute-start(bf16[2,96,768]{2,1,0:T(8,128)(2,1)} %get-tuple-element.228), channel_id=1, source_target_pairs={{8,0},{16,8},{24,16},{9,1},{17,9},{25,17},{10,2},{18,10},{26,18},{... | collective-permute-start | bytes 884744 | tf_op jit(solution)/shard_map/ppermute | solution.py:105
  152.9 71.0 %collective-permute-start.20 = (bf16[2,96,768]{2,1,0:T(8,128)(2,1)}, bf16[2,96,768]{2,1,0:T(8,128)(2,1)}, u32[]{:S(2)}, u32[]{:S(2)}) collective-permute-start(bf16[2,96,768]{2,1,0:T(8,128)(2,1)} %get-tuple-element.229), channel_id=1, source_target_pairs={{8,0},{16,8},{24,16},{9,1},{17,9},{25,17},{10,2},{18,10},{26,18},{... | collective-permute-start | bytes 884744 | tf_op jit(solution)/shard_map/ppermute | solution.py:105
  154.3 62.6 %collective-permute-start.229 = (s32[1,256]{1,0:T(1,128)S(1)}, s32[1,256]{1,0:T(1,128)S(1)}, u32[]{:S(2)}, u32[]{:S(2)}) collective-permute-start(s32[1,256]{1,0:T(1,128)S(1)} %get-tuple-element.197), channel_id=1, source_target_pairs={{0,24},{1,25},{2,26},{3,27},{4,28},{5,29},{6,30},{7,31}} | collective-permute-start | bytes 3080 | tf_op jit(solution)/shard_map/ppermute | solution.py:184
  162.6 58.6 %collective-permute-start.230 = (s32[1,256]{1,0:T(1,128)S(1)}, s32[1,256]{1,0:T(1,128)S(1)}, u32[]{:S(2)}, u32[]{:S(2)}) collective-permute-start(s32[1,256]{1,0:T(1,128)S(1)} %get-tuple-element.197), channel_id=1, source_target_pairs={{0,16},{8,24},{1,17},{9,25},{2,18},{10,26},{3,19},{11,27},{4,20},{... | collective-permute-start | bytes 3080 | tf_op jit(solution)/shard_map/ppermute | solution.py:184
  386.3 154.7 %collective-permute-start.88 = (bf16[2,96,768]{2,1,0:T(8,128)(2,1)}, bf16[2,96,768]{2,1,0:T(8,128)(2,1)}, u32[]{:S(2)}, u32[]{:S(2)}) collective-permute-start(bf16[2,96,768]{2,1,0:T(8,128)(2,1)} %get-tuple-element.222), channel_id=1, source_target_pairs={{0,8},{8,16},{16,24},{1,9},{9,17},{17,25},{2,10},{10,18},{18,26},{... | collective-permute-start | bytes 884744 | tf_op jit(solution)/shard_map/ppermute | solution.py:104
  480.5 60.9 %collective-permute-start.92 = (bf16[2,96,768]{2,1,0:T(8,128)(2,1)}, bf16[2,96,768]{2,1,0:T(8,128)(2,1)}, u32[]{:S(2)}, u32[]{:S(2)}) collective-permute-start(bf16[2,96,768]{2,1,0:T(8,128)(2,1)} %get-tuple-element.219), channel_id=1, source_target_pairs={{0,8},{8,16},{16,24},{1,9},{9,17},{17,25},{2,10},{10,18},{18,26},{... | collective-permute-start | bytes 884744 | tf_op jit(solution)/shard_map/ppermute | solution.py:104
  487.2 93.9 %collective-permute-start.97 = (bf16[2,96,768]{2,1,0:T(8,128)(2,1)}, bf16[2,96,768]{2,1,0:T(8,128)(2,1)}, u32[]{:S(2)}, u32[]{:S(2)}) collective-permute-start(bf16[2,96,768]{2,1,0:T(8,128)(2,1)} %get-tuple-element.224), channel_id=1, source_target_pairs={{8,0},{16,8},{24,16},{9,1},{17,9},{25,17},{10,2},{18,10},{26,18},{... | collective-permute-start | bytes 884744 | tf_op jit(solution)/shard_map/ppermute | solution.py:105
  490.9 57.3 %collective-permute-start.48 = (bf16[2,2,96,768]{3,2,0,1:T(8,128)(2,1)}, bf16[2,2,96,768]{3,2,0,1:T(8,128)(2,1)}, u32[]{:S(2)}, u32[]{:S(2)}) collective-permute-start(bf16[2,2,96,768]{3,2,0,1:T(8,128)(2,1)} %get-tuple-element.329), channel_id=1, source_target_pairs={{0,4},{4,0},{1,5},{5,1},{2,6},{6,2},{3,7},{7,3},{8,12},{12,8},{9,1... | collective-permute-start | bytes 1769480 | tf_op jit(solution)/shard_map/ppermute | solution.py:43
  734.8 88.5 %collective-permute-start.237 = (bf16[768,1024]{1,0:T(8,128)(2,1)}, bf16[768,1024]{1,0:T(8,128)(2,1)}, u32[]{:S(2)}, u32[]{:S(2)}) collective-permute-start(bf16[768,1024]{1,0:T(8,128)(2,1)} %slice.1094), channel_id=1, source_target_pairs={{0,4},{4,0},{1,5},{5,1},{2,6},{6,2},{3,7},{7,3},{8,12},{12,8},{9,1... | collective-permute-start | bytes 4718600 | tf_op jit(solution)/shard_map/ppermute | solution.py:43
  804.7 82.7 %collective-permute-start.191 = (bf16[2,96,768]{2,1,0:T(8,128)(2,1)S(1)}, bf16[2,96,768]{2,1,0:T(8,128)(2,1)}, u32[]{:S(2)}, u32[]{:S(2)}) collective-permute-start(bf16[2,96,768]{2,1,0:T(8,128)(2,1)S(1)} %add_convert_fusion.62), channel_id=1, source_target_pairs={{8,0},{16,8},{24,16},{9,1},{17,9},{25,17},{10,2},{18,10},{26,18},{... | collective-permute-start | bytes 884744 | tf_op jit(solution)/shard_map/ppermute | solution.py:105
  812.2 86.0 %collective-permute-start.150 = (bf16[2,96,768]{2,1,0:T(8,128)(2,1)}, bf16[2,96,768]{2,1,0:T(8,128)(2,1)}, u32[]{:S(2)}, u32[]{:S(2)}) collective-permute-start(bf16[2,96,768]{2,1,0:T(8,128)(2,1)} %add_convert_fusion.89), channel_id=1, source_target_pairs={{8,0},{16,8},{24,16},{9,1},{17,9},{25,17},{10,2},{18,10},{26,18},{... | collective-permute-start | bytes 884744 | tf_op jit(solution)/shard_map/ppermute | solution.py:105
  898.5 59.6 %collective-permute-start.131 = (bf16[2,192,768]{2,1,0:T(8,128)(2,1)S(1)}, bf16[2,192,768]{2,1,0:T(8,128)(2,1)S(1)}, u32[]{:S(2)}, u32[]{:S(2)}) collective-permute-start(bf16[2,192,768]{2,1,0:T(8,128)(2,1)S(1)} %copy-done.344), channel_id=1, source_target_pairs={{0,4},{4,0},{1,5},{5,1},{2,6},{6,2},{3,7},{7,3},{8,12},{12,8},{9,1... | collective-permute-start | bytes 1769480 | tf_op jit(solution)/shard_map/ppermute | solution.py:43
  901.9 101.8 %collective-permute-start.115 = (bf16[2,768,256]{2,1,0:T(8,128)(2,1)S(1)}, bf16[2,768,256]{2,1,0:T(8,128)(2,1)S(1)}, u32[]{:S(2)}, u32[]{:S(2)}) collective-permute-start(bf16[2,768,256]{2,1,0:T(8,128)(2,1)S(1)} %slice.996), channel_id=1, source_target_pairs={{0,4},{4,0},{1,5},{5,1},{2,6},{6,2},{3,7},{7,3},{8,12},{12,8},{9,1... | collective-permute-start | bytes 2359304 | tf_op jit(solution)/shard_map/ppermute | solution.py:43
  902.2 62.0 %collective-permute-start.182 = (bf16[2,96,768]{2,1,0:T(8,128)(2,1)S(1)}, bf16[2,96,768]{2,1,0:T(8,128)(2,1)S(1)}, u32[]{:S(2)}, u32[]{:S(2)}) collective-permute-start(bf16[2,96,768]{2,1,0:T(8,128)(2,1)S(1)} %get-tuple-element.158), channel_id=1, source_target_pairs={{0,8},{8,16},{16,24},{1,9},{9,17},{17,25},{2,10},{10,18},{18,26},{... | collective-permute-start | bytes 884744 | tf_op jit(solution)/shard_map/ppermute | solution.py:104
  910.1 55.4 %collective-permute-start.192 = (bf16[2,96,768]{2,1,0:T(8,128)(2,1)S(1)}, bf16[2,96,768]{2,1,0:T(8,128)(2,1)S(1)}, u32[]{:S(2)}, u32[]{:S(2)}) collective-permute-start(bf16[2,96,768]{2,1,0:T(8,128)(2,1)S(1)} %get-tuple-element.300), channel_id=1, source_target_pairs={{8,0},{16,8},{24,16},{9,1},{17,9},{25,17},{10,2},{18,10},{26,18},{... | collective-permute-start | bytes 884744 | tf_op jit(solution)/shard_map/ppermute | solution.py:105
  991.4 99.2 %collective-permute-start.184 = (bf16[2,96,768]{2,1,0:T(8,128)(2,1)}, bf16[2,96,768]{2,1,0:T(8,128)(2,1)}, u32[]{:S(2)}, u32[]{:S(2)}) collective-permute-start(bf16[2,96,768]{2,1,0:T(8,128)(2,1)} %get-tuple-element.154), channel_id=1, source_target_pairs={{0,8},{8,16},{16,24},{1,9},{9,17},{17,25},{2,10},{10,18},{18,26},{... | collective-permute-start | bytes 884744 | tf_op jit(solution)/shard_map/ppermute | solution.py:104
  995.8 94.9 %collective-permute-start.194 = (bf16[2,96,768]{2,1,0:T(8,128)(2,1)}, bf16[2,96,768]{2,1,0:T(8,128)(2,1)}, u32[]{:S(2)}, u32[]{:S(2)}) collective-permute-start(bf16[2,96,768]{2,1,0:T(8,128)(2,1)} %get-tuple-element.298), channel_id=1, source_target_pairs={{8,0},{16,8},{24,16},{9,1},{17,9},{25,17},{10,2},{18,10},{26,18},{... | collective-permute-start | bytes 884744 | tf_op jit(solution)/shard_map/ppermute | solution.py:105
  998.5 95.5 %collective-permute-start.143 = (bf16[2,96,768]{2,1,0:T(8,128)(2,1)}, bf16[2,96,768]{2,1,0:T(8,128)(2,1)}, u32[]{:S(2)}, u32[]{:S(2)}) collective-permute-start(bf16[2,96,768]{2,1,0:T(8,128)(2,1)} %get-tuple-element.170), channel_id=1, source_target_pairs={{0,8},{8,16},{16,24},{1,9},{9,17},{17,25},{2,10},{10,18},{18,26},{... | collective-permute-start | bytes 884744 | tf_op jit(solution)/shard_map/ppermute | solution.py:104
  1094.0 84.4 %collective-permute-start.220 = (f32[2,768]{1,0:T(2,128)}, f32[2,768]{1,0:T(2,128)}, u32[]{:S(2)}, u32[]{:S(2)}) collective-permute-start(f32[2,768]{1,0:T(2,128)} %pad_maximum_fusion.80), channel_id=1, source_target_pairs={{0,1},{1,0},{2,3},{3,2},{4,5},{5,4},{6,7},{7,6},{8,9},{9,8},{10,11... | collective-permute-start | bytes 18440 | tf_op jit(solution)/shard_map/ppermute | solution.py:35
  1155.8 78.5 %collective-permute-start.187 = (bf16[2,96,768]{2,1,0:T(8,128)(2,1)}, bf16[2,96,768]{2,1,0:T(8,128)(2,1)}, u32[]{:S(2)}, u32[]{:S(2)}) collective-permute-start(bf16[2,96,768]{2,1,0:T(8,128)(2,1)} %get-tuple-element.148), channel_id=1, source_target_pairs={{0,8},{8,16},{16,24},{1,9},{9,17},{17,25},{2,10},{10,18},{18,26},{... | collective-permute-start | bytes 884744 | tf_op jit(solution)/shard_map/ppermute | solution.py:104
  1165.7 69.4 %collective-permute-start.197 = (bf16[2,96,768]{2,1,0:T(8,128)(2,1)}, bf16[2,96,768]{2,1,0:T(8,128)(2,1)}, u32[]{:S(2)}, u32[]{:S(2)}) collective-permute-start(bf16[2,96,768]{2,1,0:T(8,128)(2,1)} %get-tuple-element.295), channel_id=1, source_target_pairs={{8,0},{16,8},{24,16},{9,1},{17,9},{25,17},{10,2},{18,10},{26,18},{... | collective-permute-start | bytes 884744 | tf_op jit(solution)/shard_map/ppermute | solution.py:105
  1171.3 72.3 %collective-permute-start.146 = (bf16[2,96,768]{2,1,0:T(8,128)(2,1)}, bf16[2,96,768]{2,1,0:T(8,128)(2,1)}, u32[]{:S(2)}, u32[]{:S(2)}) collective-permute-start(bf16[2,96,768]{2,1,0:T(8,128)(2,1)} %get-tuple-element.164), channel_id=1, source_target_pairs={{0,8},{8,16},{16,24},{1,9},{9,17},{17,25},{2,10},{10,18},{18,26},{... | collective-permute-start | bytes 884744 | tf_op jit(solution)/shard_map/ppermute | solution.py:104
  1284.6 76.4 %collective-permute-start.214 = (bf16[2,96,768]{2,1,0:T(8,128)(2,1)}, bf16[2,96,768]{2,1,0:T(8,128)(2,1)}, u32[]{:S(2)}, u32[]{:S(2)}) collective-permute-start(bf16[2,96,768]{2,1,0:T(8,128)(2,1)} %get-tuple-element.256), channel_id=1, source_target_pairs={{0,4},{4,0},{1,5},{5,1},{2,6},{6,2},{3,7},{7,3},{8,12},{12,8},{9,1... | collective-permute-start | bytes 884744 | tf_op jit(solution)/shard_map/ppermute | solution.py:43
  1284.7 74.3 %collective-permute-start.213 = (bf16[2,96,768]{2,1,0:T(8,128)(2,1)}, bf16[2,96,768]{2,1,0:T(8,128)(2,1)}, u32[]{:S(2)}, u32[]{:S(2)}) collective-permute-start(bf16[2,96,768]{2,1,0:T(8,128)(2,1)} %get-tuple-element.259), channel_id=1, source_target_pairs={{0,4},{4,0},{1,5},{5,1},{2,6},{6,2},{3,7},{7,3},{8,12},{12,8},{9,1... | collective-permute-start | bytes 884744 | tf_op jit(solution)/shard_map/ppermute | solution.py:43
  (679 other events, 9305.1 us)

commit v2 on v1

v2 whole, which is shorter than its diff:
```python
import jax
import jax.numpy as jnp
from jax import lax
from jax.experimental import pallas as pl
from jax.experimental.pallas import tpu as pltpu
from jax.sharding import Mesh
from jax.sharding import PartitionSpec as P

HEAD_DIM = 48
VOCAB = 2025
LAYERS = 3
STEP = 10
TILES = 36
BLOCK = 256

norm_eps = 1e-05
beta_first = 0.9
beta_second = 0.999
learn_rate = 0.05
small_rate = 0.5
weight_decay = 0.01
adam_eps = 1e-08

bf16 = jnp.bfloat16
f32 = jnp.float32
FLIP = [(0, 1), (1, 0)]
PLANE = ("ctx", "ty", "tx")
EVERY = ("fsdp", "ctx", "ty", "tx")


def over(axis, v):
    return lax.ppermute(v, axis, FLIP)


def dot(left, right, dims):
    return lax.dot_general(left, right, (dims, ((), ())), preferred_element_type=f32)


def norm_parts(stream, gain, shift):
    centered = stream - jnp.mean(stream, -1, keepdims=True)
    inverse = lax.rsqrt(jnp.mean(centered * centered, -1, keepdims=True) + norm_eps)
    normal_hat = centered * inverse
    return (normal_hat * gain + shift, normal_hat, inverse)


def norm_back(gradient, normal_hat, inverse, gain):
    scaled = gradient * gain
    return inverse * (
        scaled
        - jnp.mean(scaled, -1, keepdims=True)
        - normal_hat * jnp.mean(scaled * normal_hat, -1, keepdims=True)
    )


def gelu_slope(pre_gelu):
    return (
        0.5 * (1.0 + lax.erf(pre_gelu * 0.7071067811865476))
        + pre_gelu * jnp.exp(-0.5 * pre_gelu * pre_gelu) * 0.3989422804014327
    )


def sum_over_x(partial):
    mine = partial.astype(bf16)
    return mine.astype(f32) + over("tx", mine).astype(f32)


def add_halves(keep, come):
    return (keep.astype(f32) + come.astype(f32)).astype(bf16)


def choose(bit, one, zero):
    return jnp.where(bit == 1, one, zero)


def both(axis, v, at, dim):
    other = over(axis, v)
    return lax.concatenate([choose(at, other, v), choose(at, v, other)], dim)


def after(value, event):
    return lax.optimization_barrier((value, event))[0]


def order_kernel(slot_ref, held_ref, out_ref):
    out_ref[0] = held_ref[0, :, 0]


def order_tiles(held, slot, first, count):
    _, pieces, slots, half, model = held.shape
    return pl.pallas_call(
        order_kernel,
        grid_spec=pltpu.PrefetchScalarGridSpec(
            num_scalar_prefetch=1,
            grid=(count,),
            in_specs=[
                pl.BlockSpec((1, pieces, 1, half, model), lambda t, s: (s[t] // slots, 0, s[t] % slots, 0, 0))
            ],
            out_specs=pl.BlockSpec((1, pieces, half, model), lambda t, s: (t, 0, 0, 0)),
        ),
        out_shape=jax.ShapeDtypeStruct((count, pieces, half, model), bf16),
        name="order_tiles",
    )(slot[first:first + count], held)


def adamw_update(weight, moment_one, moment_two, gradient, rate):
    moment_one = beta_first * moment_one + (1.0 - beta_first) * gradient
    moment_two = beta_second * moment_two + (1.0 - beta_second) * gradient * gradient
    first_hat = moment_one / (1.0 - beta_first**STEP)
    second_hat = moment_two / (1.0 - beta_second**STEP)
    weight = weight - rate * (first_hat / (jnp.sqrt(second_hat) + adam_eps) + weight_decay * weight)
    return (weight, moment_one, moment_two)


def tile_adamw_kernel(tile_ref, used_ref, core_ref, w_ref, m_ref, v_ref, low_ref, high_ref, w_out, m_out, v_out):
    slot = pl.program_id(0)
    half = low_ref.shape[2]

    @pl.when(used_ref[slot] == 1)
    def _():
        for h, g_ref in enumerate((low_ref, high_ref)):
            at = pl.ds(h * half, half)
            new = adamw_update(w_ref[0, at], m_ref[0, at], v_ref[0, at], g_ref[0, 0].astype(f32), learn_rate)
            w_out[0, at], m_out[0, at], v_out[0, at] = new

    @pl.when(used_ref[slot] != 1)
    def _():
        w_out[...], m_out[...], v_out[...] = w_ref[...], m_ref[...], v_ref[...]


def tile_adamw(tile_of, used, core, weight, first, second, grads):
    slots, rows, width = weight.shape
    half = rows // 2
    block = pl.BlockSpec((1, rows, width), lambda s, t, u, c: (s, 0, 0))
    low = pl.BlockSpec((1, 1, half, width), lambda s, t, u, c: (c[0], t[s], 0, 0))
    high = pl.BlockSpec((1, 1, half, width), lambda s, t, u, c: (1 - c[0], t[s], 0, 0))
    return pl.pallas_call(
        tile_adamw_kernel,
        grid_spec=pltpu.PrefetchScalarGridSpec(
            num_scalar_prefetch=3,
            grid=(slots,),
            in_specs=[block, block, block, low, high],
            out_specs=[block, block, block],
        ),
        out_shape=[jax.ShapeDtypeStruct(weight.shape, f32)] * 3,
        compiler_params=pltpu.CompilerParams(vmem_limit_bytes=32 * 2**20),
        name="tile_adamw",
    )(tile_of, used, core, weight, first, second, grads, grads)


def body(
    token_ids,
    masked,
    tile_slot,
    tile_master,
    tile_first,
    tile_second,
    embedding,
    embed_first,
    embed_second,
    position_table,
    position_first,
    position_second,
    norm_params,
    norm_first,
    norm_second,
    head_bias,
    bias_first,
    bias_second,
):
    n = lax.axis_size("fsdp")
    z, core, ty, tx = (lax.axis_index(a) for a in EVERY)
    slots, width, model = tile_master.shape
    half = width // 2
    columns = 2 * width
    heads = columns // HEAD_DIM
    half_len = token_ids.shape[1]
    rows = half_len // 2
    share = rows // 2
    own_dim = embedding.shape[0]
    norms = norm_params.shape[1]
    core_arr = core.reshape(1).astype(jnp.int32)
    piece_at = core * 2 + ty

    held = lax.dynamic_slice(tile_master, (0, core * half, 0), (slots, half, model)).astype(bf16)

    held = lax.all_gather(held, ("fsdp", "ctx", "ty"), axis=0, tiled=True).reshape(n, 4, slots, half, model)

    block_at = piece_at * 2 + tx
    vocab_pad = 8 * BLOCK - VOCAB
    wide = BLOCK + rows
    embed_pad = jnp.pad(embedding.astype(bf16), ((0, 0), (0, vocab_pad)))
    ids_half = jnp.where(masked == 1, VOCAB - 1, token_ids)
    ids = lax.dynamic_slice(ids_half, (0, ty * rows), (1, rows))
    coded = lax.dynamic_slice(ids_half * 2 + masked, (0, ty * rows), (1, rows))
    coded = jnp.concatenate([coded // 256, coded % 256], 1).astype(bf16)
    packed = jnp.concatenate(
        [
            lax.dynamic_slice(embed_pad, (0, block_at * BLOCK), (own_dim, BLOCK)),
            lax.dynamic_slice(position_table, (0, piece_at * rows), (own_dim, rows)).astype(bf16),
        ],
        1,
    )
    packed = jnp.concatenate(
        [
            packed,
            jnp.pad(norm_params.astype(bf16).reshape(2 * norms, own_dim), ((0, 0), (0, wide - own_dim))),
            jnp.pad(coded, ((0, 15 - 2 * norms), (0, wide - 2 * rows))),
        ],
        0,
    )
    tables = lax.all_gather(packed, "fsdp", axis=0)
    embed_all = tables[:, :own_dim, :BLOCK].reshape(model, BLOCK)
    for axis, at in (("tx", tx), ("ty", ty), ("ctx", core)):
        embed_all = both(axis, embed_all, at, 1)
    places_own = tables[:, :own_dim, BLOCK:].reshape(model, rows).T.astype(f32)
    gains = tables[:, own_dim:own_dim + 2 * norms, :own_dim].transpose(1, 0, 2)
    gains = gains.reshape(2, norms, model).astype(f32)
    coded = tables[:, own_dim + 2 * norms, :2 * rows].reshape(n, 1, 2, rows)
    for axis, at in (("ty", ty), ("ctx", core)):
        coded = both(axis, coded, at, 1)
    coded = coded.astype(f32).astype(jnp.int32)
    coded = coded[:, :, 0] * 256 + coded[:, :, 1]
    all_ids = coded // 2
    count = jnp.sum(coded % 2).astype(f32)
    column_at = lax.broadcasted_iota(jnp.int32, (1, 8 * BLOCK), 1)
    pick_ids = (ids.reshape(rows, 1) == column_at).astype(bf16)
    stream = dot(pick_ids, embed_all, ((1,), (1,))) + places_own

    scale = HEAD_DIM ** (-0.5)
    weights, kept_layers = [], []
    for layer in range(LAYERS):
        tiles = order_tiles(held, tile_slot, 12 * layer, 12)
        tiles = tiles.reshape(12 * columns, model)
        w_qkv, w_o = tiles[:3 * columns], tiles[3 * columns:4 * columns]
        w_in, w_out = tiles[4 * columns:8 * columns], tiles[8 * columns:]
        weights.append((w_qkv, w_o, w_in, w_out))
        normed = norm_parts(stream, gains[0, 2 * layer], gains[1, 2 * layer])[0].astype(bf16)
        kv = dot(w_qkv[columns:], normed, ((1,), (1,))).astype(bf16)
        kv_two = jnp.concatenate([kv, over("ty", kv)], 1)
        kv_all = jnp.concatenate([kv_two, over("ctx", kv_two)], 1).reshape(2, heads, HEAD_DIM, 4 * rows)
        queries = dot(w_qkv[:columns], normed, ((1,), (1,))).astype(bf16).reshape(heads, HEAD_DIM, rows)
        keys, values = kv_all[0], kv_all[1]
        scores = jnp.einsum("hcq,hck->hqk", queries, keys, preferred_element_type=f32) * scale
        row_top = jnp.max(scores, -1, keepdims=True)
        log_total = row_top + jnp.log(jnp.sum(jnp.exp(scores - row_top), -1, keepdims=True))
        attn = jnp.exp(scores - log_total).astype(bf16)
        mixed = (
            jnp.einsum("hqk,hck->hcq", attn, values, preferred_element_type=f32)
            .astype(bf16)
            .reshape(columns, rows)
        )
        middle = stream + sum_over_x(dot(mixed, w_o, ((0,), (0,))))
        normed_mlp = norm_parts(middle, gains[0, 2 * layer + 1], gains[1, 2 * layer + 1])[0].astype(bf16)
        pre_gelu = dot(normed_mlp, w_in, ((1,), (1,)))
        activation = jax.nn.gelu(pre_gelu, approximate=False).astype(bf16)
        kept_layers.append((stream, middle, queries, keys, values, log_total, mixed, pre_gelu))
        stream = middle + sum_over_x(dot(activation, w_out, ((1,), (0,))))

    final_rows = lax.dynamic_slice_in_dim(stream, tx * share, share, 0)
    final_normed, hat_final, inv_final = norm_parts(final_rows, gains[0, 2 * LAYERS], gains[1, 2 * LAYERS])
    final_normed = final_normed.astype(bf16)
    bias_row = jnp.pad(head_bias, (0, vocab_pad)).reshape(1, 8 * BLOCK)
    logits = dot(final_normed, embed_all, ((1,), (0,))) + bias_row
    logits = jnp.where(column_at < VOCAB, logits, -1e30)
    start = ty * rows + tx * share
    targets = lax.dynamic_slice(token_ids, (0, start), (1, share)).reshape(share, 1)
    row_weights = lax.dynamic_slice(masked, (0, start), (1, share)).reshape(share, 1).astype(f32)
    row_top = jnp.max(logits, -1, keepdims=True)
    log_total = row_top + jnp.log(jnp.sum(jnp.exp(logits - row_top), -1, keepdims=True))
    is_target = targets == column_at
    picked = jnp.sum(jnp.where(is_target, logits, 0.0), -1, keepdims=True)
    loss_part = jnp.sum((log_total - picked) * row_weights)
    grad_logits = (
        (jnp.exp(logits - log_total) - is_target.astype(f32)) * (row_weights / count)
    ).astype(bf16)
    bias_sum = jnp.sum(grad_logits.astype(f32), 0, keepdims=True)
    bias_sum = jnp.where(column_at == 8 * BLOCK - 1, loss_part, bias_sum)
    for axis in PLANE:
        bias_sum = bias_sum + over(axis, bias_sum)
    bit = 1
    while bit < n:
        bias_sum = bias_sum + lax.ppermute(bias_sum, "fsdp", [(i, i ^ bit) for i in range(n)])
        bit *= 2
    bias_grad = bias_sum[0, :VOCAB]
    loss_value = bias_sum[0, 8 * BLOCK - 1] / count
    grad_final = dot(grad_logits, embed_all, ((1,), (1,)))
    part = norm_back(grad_final, hat_final, inv_final, gains[0, 2 * LAYERS]).astype(bf16)
    gradient = both("tx", part, tx, 0).astype(f32)
    final_norm_grad = jnp.stack([jnp.sum(grad_final * hat_final, 0), jnp.sum(grad_final, 0)])
    final_norm_grad = final_norm_grad + over("tx", final_norm_grad)

    embed_part = dot(final_normed, grad_logits, ((0,), (0,))).astype(bf16)
    for axis, at in (("ctx", core), ("ty", ty), ("tx", tx)):
        cut = embed_part.shape[1] // 2
        keep = lax.dynamic_slice_in_dim(embed_part, at * cut, cut, 1)
        send = lax.dynamic_slice_in_dim(embed_part, cut - at * cut, cut, 1)
        embed_part = add_halves(keep, over(axis, send))
    embed_head = lax.all_to_all(embed_part.reshape(n, own_dim, BLOCK), "fsdp", 0, 0)
    embed_head = jnp.sum(embed_head.astype(f32), 0).astype(bf16)
    for axis, at in (("tx", tx), ("ty", ty), ("ctx", core)):
        embed_head = both(axis, embed_head, at, 1)

    norm_grads = [None] * norms
    norm_grads[2 * LAYERS] = final_norm_grad
    crossed = []

    def plane_sum(grads):
        keep = lax.dynamic_slice_in_dim(grads, core * 2, 2, 1).astype(bf16)
        send = lax.dynamic_slice_in_dim(grads, 2 - core * 2, 2, 1).astype(bf16)
        two = add_halves(keep, over("ctx", send))
        keep = lax.dynamic_index_in_dim(two, ty, 1, False)
        send = lax.dynamic_index_in_dim(two, 1 - ty, 1, False)
        return add_halves(keep, over("ty", send))

    def cross(own):
        crossed.append(lax.psum(after(own, crossed[-1]) if crossed else own, "fsdp"))

    attn_own = None
    for layer in reversed(range(LAYERS)):
        stream, middle, queries, keys, values, log_total, mixed, pre_gelu = kept_layers[layer]
        w_qkv, w_o, w_in, w_out = weights[layer]
        branch = gradient.astype(bf16)
        activation = jax.nn.gelu(pre_gelu, approximate=False).astype(bf16)
        grad_act = dot(branch, w_out, ((1,), (1,)))
        grad_pre = (grad_act * gelu_slope(pre_gelu)).astype(bf16)
        normed_mlp, hat_mlp, inv_mlp = norm_parts(middle, gains[0, 2 * layer + 1], gains[1, 2 * layer + 1])
        grad_normed = sum_over_x(dot(grad_pre, w_in, ((1,), (0,))))
        grad_out = dot(activation, branch, ((0,), (0,))).reshape(4, 4, half, model)
        grad_in = dot(grad_pre, normed_mlp.astype(bf16), ((0,), (0,))).reshape(4, 4, half, model)
        mlp_own = plane_sum(jnp.concatenate([grad_in, grad_out], 0))
        cross(mlp_own if attn_own is None else jnp.concatenate([mlp_own, attn_own], 0))
        grad_middle = gradient + norm_back(grad_normed, hat_mlp, inv_mlp, gains[0, 2 * layer + 1])
        norm_grads[2 * layer + 1] = jnp.stack([jnp.sum(grad_normed * hat_mlp, 0), jnp.sum(grad_normed, 0)])
        branch = grad_middle.astype(bf16)
        grad_proj_out = dot(mixed, branch, ((1,), (0,)))
        grad_mixed = dot(w_o, branch, ((1,), (1,))).astype(bf16).reshape(heads, HEAD_DIM, rows)
        soft = jnp.exp(
            jnp.einsum("hcq,hck->hqk", queries, keys, preferred_element_type=f32) * scale - log_total
        )
        grad_soft = jnp.einsum("hcq,hck->hqk", grad_mixed, values, preferred_element_type=f32)
        grad_scores = (soft * (grad_soft - jnp.sum(soft * grad_soft, -1, keepdims=True))).astype(bf16)
        grad_keys = jnp.einsum("hcq,hqk->hck", queries, grad_scores, preferred_element_type=f32) * scale
        grad_values = jnp.einsum("hcq,hqk->hck", grad_mixed, soft.astype(bf16), preferred_element_type=f32)
        grad_queries = jnp.einsum("hck,hqk->hcq", keys, grad_scores, preferred_element_type=f32) * scale
        grad_kv = jnp.stack([grad_keys, grad_values]).astype(bf16).reshape(2 * columns, 4 * rows)
        pair = grad_kv[:, :2 * rows].astype(f32) + over("ctx", grad_kv[:, 2 * rows:]).astype(f32)
        grad_kv = (pair[:, :rows] + over("ty", pair[:, rows:].astype(bf16)).astype(f32)).astype(bf16)
        grad_qkv = jnp.concatenate([grad_queries.astype(bf16).reshape(columns, rows), grad_kv], 0)
        normed, hat_attn, inv_attn = norm_parts(stream, gains[0, 2 * layer], gains[1, 2 * layer])
        grad_normed = sum_over_x(dot(grad_qkv, w_qkv, ((0,), (0,))))
        grad_w = dot(grad_qkv, normed.astype(bf16), ((1,), (0,)))
        grad_w = jnp.concatenate([grad_w, grad_proj_out], 0).reshape(4, 4, half, model)
        attn_own = plane_sum(grad_w)
        if layer == 0:
            cross(attn_own)
        gradient = grad_middle + norm_back(grad_normed, hat_attn, inv_attn, gains[0, 2 * layer])
        norm_grads[2 * layer] = jnp.stack([jnp.sum(grad_normed * hat_attn, 0), jnp.sum(grad_normed, 0)])

    norm_rows = jnp.stack(norm_grads, 1).reshape(2 * norms, model)
    state = jnp.concatenate(
        [gradient.astype(bf16), norm_rows.astype(bf16), jnp.zeros((16 - 2 * norms, model), bf16)], 0
    )
    state = state.reshape(rows + 16, n, own_dim).transpose(1, 0, 2)
    state = lax.all_to_all(state, "fsdp", 0, 0)[:, None]
    state = both("ty", state, ty, 1)
    state = both("ctx", state, core, 1)
    norm_grad = jnp.sum(state[:, :, rows:rows + 2 * norms].astype(f32), (0, 1)).reshape(2, norms, own_dim)
    token_grads = state[:, :, :rows]
    position_grad = jnp.sum(token_grads.astype(f32), 0).reshape(4 * rows, own_dim).T
    picks = (all_ids.reshape(n * 4 * rows, 1) == column_at).astype(bf16)
    embed_tail = dot(token_grads.reshape(n * 4 * rows, own_dim), picks, ((0,), (0,)))
    embed_grad = (embed_tail + embed_head.astype(f32))[:, :VOCAB]

    def to_both_cores(own):
        return jnp.stack([own, over("ctx", own)])

    top, middle, bottom, last = (to_both_cores(own) for own in crossed)
    grads = jnp.concatenate(
        [last, bottom[:, :8], bottom[:, 8:], middle[:, :8], middle[:, 8:], top], 1
    )
    is_slot = (z * slots + jnp.arange(slots, dtype=jnp.int32))[:, None] == tile_slot[None, :]
    used = jnp.any(is_slot, 1).astype(jnp.int32)
    tile_of = jnp.sum(jnp.where(is_slot, jnp.arange(TILES, dtype=jnp.int32)[None, :], 0), 1)
    tile_upd = tile_adamw(tile_of, used, core_arr, tile_master, tile_first, tile_second, grads)
    embed_upd = adamw_update(embedding, embed_first, embed_second, embed_grad, learn_rate)
    position_upd = adamw_update(position_table, position_first, position_second, position_grad, learn_rate)
    norm_upd = adamw_update(norm_params, norm_first, norm_second, norm_grad, small_rate)
    bias_upd = adamw_update(head_bias, bias_first, bias_second, bias_grad, small_rate)
    return (loss_value, *tile_upd, *embed_upd, *position_upd, *norm_upd, *bias_upd)


def solution(mesh):
    grid = Mesh(mesh.devices.reshape(-1, 2, 2, 2), EVERY)
    halves, tiles, table = P("fsdp", "ctx"), P("fsdp", ("ty", "tx"), None), P("fsdp", None)
    norms, copied = P(None, None, "fsdp"), P()

    def three(spec):
        return (spec,) * 3

    return jax.shard_map(
        body,
        mesh=grid,
        in_specs=(halves, halves, copied, *three(tiles), *three(table), *three(table), *three(norms), *three(copied)),
        out_specs=(copied, *three(tiles), *three(table), *three(table), *three(norms), *three(copied)),
        check_vma=False,
    )
```

time: 1410 us -> 841 us (0.60)
  starting transfers between devices: 404 us -> 62.4 us
  other arithmetic: 231 us -> 117 us
  local copies, waits for them, and re-layouts: 176 us -> 97.5 us
  waiting for transfers between devices: 414 us -> 374 us
  blocking collectives: 0 us -> 26.8 us
  matrix products: 114 us -> 90.9 us
    ppermute x249 -> x60, starting transfers between devices: 404 us -> 53.4 us  [the longest x58 50.5 us: over(): return lax.ppermute(v, axis, FLIP)]
    ppermute x249 -> x60, waiting for transfers between devices: 414 us -> 162 us  [the longest x58 162 us: over(): return lax.ppermute(v, axis, FLIP)]
    psum x0 -> x4, waiting for transfers between devices: none -> 95 us  [cross(): lax.psum(after(own, crossed[-1]) if crossed else own, 'fsdp')]
    all_gather x0 -> x1, waiting for transfers between devices: none -> 88.7 us  [body(): lax.all_gather(held, ('fsdp', 'ctx', 'ty'), axis=0, tiled=True)]
    convert_element_type x99 -> x21, other arithmetic: 104 us -> 29.1 us  [the longest x15 25.4 us: add_halves(): return (keep.astype(f32) + come.astype(f32)).astype(bf16)]
    another operation x45 -> x2, other arithmetic: 33.8 us -> 0.03 us  [the longest x42 31.5 us: full_rows(): every = jnp.stack([both, over_core(both)], 1)]
    all_to_all x0 -> x2, waiting for transfers between devices: none -> 27.8 us  [the longest x1 20.4 us: body(): state = lax.all_to_all(state, 'fsdp', 0, 0)[:, None]]
    all_gather x0 -> x1, blocking collectives: none -> 26.8 us  [body(): tables = lax.all_gather(packed, 'fsdp', axis=0)]
  transfers between devices with their start and end apart: 249 -> 67, of which waited for: 87 -> 32; matrix products, arithmetic and copies ran while one was open for 32% -> 24% of each run, Pallas kernels for 0% -> 3%
where the time goes in v2:
time: 841 us; the launch traced here: 834 us
  waiting for transfers between devices  374 us (44%)
  other arithmetic  117 us (14%)
  local copies, waits for them, and re-layouts  97.5 us (12%)
  matrix products  90.9 us (11%)
  starting transfers between devices  62.4 us (7%)
  Pallas kernels  45.2 us (5%)
  blocking collectives  26.8 us (3%)
  between operations  20.3 us (2%)
    ppermute x58, waiting for transfers between devices, over(): return lax.ppermute(v, axis, FLIP)  162 us
    psum x4, waiting for transfers between devices, cross(): lax.psum(after(own, crossed[-1]) if crossed else own, 'fsdp')  95 us
    all_gather x1, waiting for transfers between devices, body(): lax.all_gather(held, ('fsdp', 'ctx', 'ty'), axis=0, tiled=True)  88.7 us
    dot_general x44, matrix products, dot(): lax.dot_general(left, right, (dims, ((), ())), preferred_element_type=f32)  57.1 us
    ppermute x58, starting transfers between devices, over(): return lax.ppermute(v, axis, FLIP)  50.5 us
    unnamed x416, local copies, waits for them, and re-layouts  34.1 us
    pallas_call x3, Pallas kernels, order_tiles(): pl.pallas_call(order_kernel, grid_spec=pltpu.PrefetchScalarGridSpec(num_s...  31.7 us
    all_gather x1, blocking collectives, body(): tables = lax.all_gather(packed, 'fsdp', axis=0)  26.8 us
  transfers between devices with their start and end apart: 67, of which 32 were waited for; matrix products, arithmetic and copies ran while one was open for 24% of the time, Pallas kernels for 3%

profile of v2, /device:TPU:0, one launch (start us, length us, event | category | flops | bytes accessed | tf_op | source)
XLA Modules:
  0.0 833.5 jit_solution(4584527118774381886)
XLA Ops:
  13.3 26.8 %all-gather = bf16[832,512]{1,0:T(8,128)(2,1)S(1)} all-gather(bf16[208,512]{1,0:T(8,128)(2,1)S(1)} %fusion.113), channel_id=2, replica_groups=mesh['fsdp'=4,'ctx'=2,'ty'=2,'tx'=2] {'fsdp'}, dimensions={0}, use_global_device_ids=true | all-gather | bytes 1064960 | tf_op jit(solution)/shard_map/all_gather | solution.py:211
  50.9 25.0 %collective-permute-done.1 = bf16[768,512]{1,0:T(8,128)(2,1)} collective-permute-done((bf16[768,512]{1,0:T(8,128)(2,1)S(1)}, bf16[768,512]{1,0:T(8,128)(2,1)}, u32[]{:S(2)}, u32[]{:S(2)}) %collective-permute-start.1) | collective-permute-done | bytes 786464 | tf_op jit(solution)/shard_map/ppermute | solution.py:32
  86.9 88.7 %all-gather.3.cloned.1.call-done = bf16[192,96,768]{2,1,0:T(8,128)(2,1)} async-done(((bf16[12,96,768]{2,1,0:T(8,128)(2,1)}), bf16[192,96,768]{2,1,0:T(8,128)(2,1)}) %all-gather.3.cloned.1.call-update) | async-done | bytes 28311568 | tf_op jit(solution)/shard_map/all_gather | solution.py:186
  175.7 10.5 %order_tiles.3 = bf16[12,4,96,768]{3,2,1,0:T(8,128)(2,1)} custom-call(s32[12]{0:T(128)} %get-tuple-element.225.slot_ref, bf16[4,4,12,96,768]{4,3,2,1,0:T(8,128)(2,1)} %bitcast.281), custom_call_target="tpu_custom_call" | custom-call | tf_op jit(solution)/shard_map/order_tiles/pallas_call | solution.py:90
  194.6 9.0 %collective-permute-done.3 = bf16[768,256]{0,1:T(8,128)(2,1)S(1)} collective-permute-done((bf16[768,256]{0,1:T(8,128)(2,1)S(1)}, bf16[768,256]{0,1:T(8,128)(2,1)S(1)}, u32[]{:S(2)}, u32[]{:S(2)}) %collective-permute-start.3) | collective-permute-done | bytes 393248 | tf_op jit(solution)/shard_map/ppermute | solution.py:32
  219.9 9.2 %collective-permute-done.5 = bf16[256,768]{1,0:T(8,128)(2,1)S(1)} collective-permute-done((bf16[256,768]{1,0:T(8,128)(2,1)S(1)}, bf16[256,768]{1,0:T(8,128)(2,1)S(1)}, u32[]{:S(2)}, u32[]{:S(2)}) %collective-permute-start.5) | collective-permute-done | bytes 393248 | tf_op jit(solution)/shard_map/ppermute | solution.py:32
  237.7 10.5 %order_tiles.4 = bf16[12,4,96,768]{3,2,1,0:T(8,128)(2,1)} custom-call(s32[12]{0:T(128)} %get-tuple-element.224.slot_ref, bf16[4,4,12,96,768]{4,3,2,1,0:T(8,128)(2,1)} %bitcast.282), custom_call_target="tpu_custom_call" | custom-call | tf_op jit(solution)/shard_map/order_tiles/pallas_call | solution.py:90
  251.7 9.0 %collective-permute-done.7 = bf16[768,256]{0,1:T(8,128)(2,1)S(1)} collective-permute-done((bf16[768,256]{0,1:T(8,128)(2,1)S(1)}, bf16[768,256]{0,1:T(8,128)(2,1)S(1)}, u32[]{:S(2)}, u32[]{:S(2)}) %collective-permute-start.7) | collective-permute-done | bytes 393248 | tf_op jit(solution)/shard_map/ppermute | solution.py:32
  275.0 10.3 %collective-permute-done.9 = bf16[256,768]{1,0:T(8,128)(2,1)S(1)} collective-permute-done((bf16[256,768]{1,0:T(8,128)(2,1)S(1)}, bf16[256,768]{1,0:T(8,128)(2,1)S(1)}, u32[]{:S(2)}, u32[]{:S(2)}) %collective-permute-start.9) | collective-permute-done | bytes 393248 | tf_op jit(solution)/shard_map/ppermute | solution.py:32
  296.0 10.7 %order_tiles.5 = bf16[12,4,96,768]{3,2,1,0:T(8,128)(2,1)} custom-call(s32[12]{0:T(128)} %get-tuple-element.226.slot_ref, bf16[4,4,12,96,768]{4,3,2,1,0:T(8,128)(2,1)} %bitcast.283), custom_call_target="tpu_custom_call" | custom-call | tf_op jit(solution)/shard_map/order_tiles/pallas_call | solution.py:90
  311.7 7.9 collective-permute-done.11
  344.4 9.5 %collective-permute-done.13 = bf16[256,768]{1,0:T(8,128)(2,1)S(1)} collective-permute-done((bf16[256,768]{1,0:T(8,128)(2,1)S(1)}, bf16[256,768]{1,0:T(8,128)(2,1)S(1)}, u32[]{:S(2)}, u32[]{:S(2)}) %collective-permute-start.13) | collective-permute-done | bytes 393248 | tf_op jit(solution)/shard_map/ppermute | solution.py:32
  364.6 8.1 collective-permute-done.14
  425.5 7.7 collective-permute-done.25
  461.2 7.6 collective-permute-done.27
  494.7 7.4 all-to-all-done.1
  526.8 7.6 collective-permute-done.30
  571.2 9.2 %collective-permute-done.41 = bf16[8,96,768]{2,1,0:T(8,128)(2,1)} collective-permute-done((bf16[8,96,768]{2,1,0:T(8,128)(2,1)}, bf16[8,96,768]{2,1,0:T(8,128)(2,1)}, u32[]{:S(2)}, u32[]{:S(2)}) %collective-permute-start.41) | collective-permute-done | bytes 1179680 | tf_op jit(solution)/shard_map/ppermute | solution.py:32
  633.6 20.4 %all-to-all-done = bf16[4,272,192]{2,1,0:T(8,128)(2,1)} async-done(((bf16[4,272,192]{2,1,0:T(8,128)(2,1)}), bf16[4,272,192]{2,1,0:T(8,128)(2,1)}, u32[]{:S(2)}, u32[]{:S(2)}) %all-to-all-start) | async-done | bytes 417824 | tf_op jit(solution)/shard_map/all_to_all | solution.py:364
  689.2 57.2 %all-reduce.13.cloned.1.call-done = bf16[12,96,768]{2,1,0:T(8,128)(2,1)} async-done(((bf16[12,96,768]{2,1,0:T(8,128)(2,1)}), bf16[12,96,768]{2,1,0:T(8,128)(2,1)}) %all-reduce.13.cloned.1.call-update) | async-done | bytes 1769488 | tf_op jit(solution)/shard_map/psum | solution.py:316
  746.4 9.9 %fusion = f32[192,2048]{1,0:T(8,128)} fusion(bf16[4096,192]{0,1:T(8,128)(2,1)} %reshape.516, s32[4096]{0:T(1024)S(1)} %add_select_fusion), kind=kOutput, calls=%fused_computation.1 | convolution fusion | flops 3229614080 | bytes 3162112 | tf_op jit(solution)/shard_map/dot_general | solution.py:36
  763.3 31.5 %all-reduce.15.cloned.1.call-done = bf16[4,96,768]{2,1,0:T(8,128)(2,1)} async-done(((bf16[4,96,768]{2,1,0:T(8,128)(2,1)}), bf16[4,96,768]{2,1,0:T(8,128)(2,1)}) %all-reduce.15.cloned.1.call-update) | async-done | bytes 589840 | tf_op jit(solution)/shard_map/psum | solution.py:316
  800.9 11.0 %maximum_maximum_fusion.low_ref.high_ref = bf16[2,36,96,768]{3,2,1,0:T(8,128)(2,1)} fusion(bf16[1,8,96,768]{3,2,1,0:T(8,128)(2,1)} %bitcast.84, bf16[1,8,96,768]{3,2,1,0:T(8,128)(2,1)} %bitcast.83, bf16[1,12,96,768]{3,2,1,0:T(8,128)(2,1)} %bitcast.82, bf16[1,12,96,768]{3,2,1,0:T(8,128)(2,1)S(1)} %bitcast.373, bf16[1,12,96,768]{3,2,1,0:T(8,128)(2,1)} %bitcast.80, ...), kind=kLoop, calls=%fused_computation.15 | loop fusion | flops 37158912 | bytes 21233664 | tf_op jit(solution)/shard_map/concatenate | solution.py:378
  812.0 13.4 %tile_adamw.1 = (f32[12,192,768]{2,1,0:T(8,128)}, f32[12,192,768]{2,1,0:T(8,128)}, f32[12,192,768]{2,1,0:T(8,128)}) custom-call(s32[12]{0:T(128)S(1)} %fusion.138.tile_ref, s32[12]{0:T(128)S(1)} %convert_element_type.649.used_ref, s32[1]{0:T(128)} %bitcast.38.core_ref, f32[12,192,768]{2,1,0:T(8,128)S(1)} %bitcast.270, f32[12,192,768]{2,1,0:T(8,128)S(1)} %bitcast.272, ...), custom_call_target="tpu_custom_call" | custom-call | tf_op jit(solution)/shard_map/tile_adamw/pallas_call | solution.py:136
  (857 shorter events, 395.0 us)
Async XLA Ops:
  7.2 168.5 %all-gather.3.cloned.1.call-start = ((), (), s32[]{:S(2)}) async-start(), calls=%async_computation.2 | async-start | bytes 30081024 | tf_op jit(solution)/shard_map/all_gather | solution.py:186
  384.2 221.4 %collective-permute-start.51 = (f32[2,768]{1,0:T(2,128)}, f32[2,768]{1,0:T(2,128)}, u32[]{:S(2)}, u32[]{:S(2)}) collective-permute-start(f32[2,768]{1,0:T(2,128)} %pad_maximum_fusion.38), channel_id=1, source_target_pairs={{0,1},{1,0},{2,3},{3,2},{4,5},{5,4},{6,7},{7,6},{8,9},{9,8},{10,11... | collective-permute-start | bytes 18440 | tf_op jit(solution)/shard_map/ppermute | solution.py:32
  388.6 33.6 %collective-permute-start.54 = (bf16[768,1024]{1,0:T(8,128)(2,1)}, bf16[768,1024]{1,0:T(8,128)(2,1)}, u32[]{:S(2)}, u32[]{:S(2)}) collective-permute-start(bf16[768,1024]{1,0:T(8,128)(2,1)} %constant_dynamic-slice_fusion.2), channel_id=1, source_target_pairs={{0,4},{4,0},{1,5},{5,1},{2,6},{6,2},{3,7},{7,3},{8,12},{12,8},{9,1... | collective-permute-start | bytes 4718600 | tf_op jit(solution)/shard_map/ppermute | solution.py:32
  390.7 234.7 %collective-permute-start.20 = (f32[1,2048]{1,0:T(1,128)}, f32[1,2048]{1,0:T(1,128)}, u32[]{:S(2)}, u32[]{:S(2)}) collective-permute-start(f32[1,2048]{1,0:T(1,128)} %add.648), channel_id=1, source_target_pairs={{0,8},{8,0},{16,24},{24,16},{1,9},{9,1},{17,25},{25,17},{2,10},{10... | collective-permute-start | bytes 24584 | tf_op jit(solution)/shard_map/ppermute | solution.py:282
  417.4 40.9 %collective-permute-start.44 = (bf16[8,2,96,768]{3,2,0,1:T(8,128)(2,1)S(1)}, bf16[8,2,96,768]{3,2,0,1:T(8,128)(2,1)S(1)}, u32[]{:S(2)}, u32[]{:S(2)}) collective-permute-start(bf16[8,2,96,768]{3,2,0,1:T(8,128)(2,1)S(1)} %copy.236), channel_id=1, source_target_pairs={{0,4},{4,0},{1,5},{5,1},{2,6},{6,2},{3,7},{7,3},{8,12},{12,8},{9,1... | collective-permute-start | bytes 7077896 | tf_op jit(solution)/shard_map/ppermute | solution.py:32
  424.4 32.5 %collective-permute-start.55 = (bf16[768,512]{1,0:T(8,128)(2,1)S(1)}, bf16[768,512]{1,0:T(8,128)(2,1)S(1)}, u32[]{:S(2)}, u32[]{:S(2)}) collective-permute-start(bf16[768,512]{1,0:T(8,128)(2,1)S(1)} %constant_dynamic-slice_fusion.1), channel_id=1, source_target_pairs={{0,2},{2,0},{1,3},{3,1},{4,6},{6,4},{5,7},{7,5},{8,10},{10,8},{9,1... | collective-permute-start | bytes 2359304 | tf_op jit(solution)/shard_map/ppermute | solution.py:32
  445.1 44.4 %collective-permute-start.42 = (bf16[4,2,96,768]{3,2,0,1:T(8,128)(2,1)}, bf16[4,2,96,768]{3,2,0,1:T(8,128)(2,1)}, u32[]{:S(2)}, u32[]{:S(2)}) collective-permute-start(bf16[4,2,96,768]{3,2,0,1:T(8,128)(2,1)} %copy.239), channel_id=1, source_target_pairs={{0,4},{4,0},{1,5},{5,1},{2,6},{6,2},{3,7},{7,3},{8,12},{12,8},{9,1... | collective-permute-start | bytes 3538952 | tf_op jit(solution)/shard_map/ppermute | solution.py:32
  468.8 43.6 %collective-permute-start.45 = (bf16[8,96,768]{2,1,0:T(8,128)(2,1)}, bf16[8,96,768]{2,1,0:T(8,128)(2,1)}, u32[]{:S(2)}, u32[]{:S(2)}) collective-permute-start(bf16[8,96,768]{2,1,0:T(8,128)(2,1)} %dynamic-slice_bitcast_fusion), channel_id=1, source_target_pairs={{0,2},{2,0},{1,3},{3,1},{4,6},{6,4},{5,7},{7,5},{8,10},{10,8},{9,1... | collective-permute-start | bytes 3538952 | tf_op jit(solution)/shard_map/ppermute | solution.py:32
  489.2 96.2 %all-reduce.9.cloned.1.call-start = ((), (), s32[]{:S(2)}) async-start(), calls=%async_computation.3 | async-start | bytes 2359296 | tf_op jit(solution)/shard_map/psum | solution.py:316
  507.8 38.8 %collective-permute-start.40 = (bf16[8,2,96,768]{3,2,0,1:T(8,128)(2,1)}, bf16[8,2,96,768]{3,2,0,1:T(8,128)(2,1)}, u32[]{:S(2)}, u32[]{:S(2)}) collective-permute-start(bf16[8,2,96,768]{3,2,0,1:T(8,128)(2,1)} %copy.237), channel_id=1, source_target_pairs={{0,4},{4,0},{1,5},{5,1},{2,6},{6,2},{3,7},{7,3},{8,12},{12,8},{9,1... | collective-permute-start | bytes 7077896 | tf_op jit(solution)/shard_map/ppermute | solution.py:32
  515.1 153.6 %all-reduce.11.cloned.1.call-start = ((), (), s32[]{:S(2)}) async-start(), calls=%async_computation.4 | async-start | bytes 3538944 | tf_op jit(solution)/shard_map/psum | solution.py:316
  526.8 41.4 %collective-permute-start.38 = (bf16[4,2,96,768]{3,2,0,1:T(8,128)(2,1)}, bf16[4,2,96,768]{3,2,0,1:T(8,128)(2,1)}, u32[]{:S(2)}, u32[]{:S(2)}) collective-permute-start(bf16[4,2,96,768]{3,2,0,1:T(8,128)(2,1)} %copy.240), channel_id=1, source_target_pairs={{0,4},{4,0},{1,5},{5,1},{2,6},{6,2},{3,7},{7,3},{8,12},{12,8},{9,1... | collective-permute-start | bytes 3538952 | tf_op jit(solution)/shard_map/ppermute | solution.py:32
  568.2 60.8 %collective-permute-start.58 = (bf16[192,512]{1,0:T(8,128)(2,1)}, bf16[192,512]{1,0:T(8,128)(2,1)}, u32[]{:S(2)}, u32[]{:S(2)}) collective-permute-start(bf16[192,512]{1,0:T(8,128)(2,1)} %pad_maximum_fusion.33), channel_id=1, source_target_pairs={{0,2},{2,0},{1,3},{3,1},{4,6},{6,4},{5,7},{7,5},{8,10},{10,8},{9,1... | collective-permute-start | bytes 589832 | tf_op jit(solution)/shard_map/ppermute | solution.py:32
  570.8 39.4 %collective-permute-start.36 = (bf16[8,2,96,768]{3,2,0,1:T(8,128)(2,1)}, bf16[8,2,96,768]{3,2,0,1:T(8,128)(2,1)}, u32[]{:S(2)}, u32[]{:S(2)}) collective-permute-start(bf16[8,2,96,768]{3,2,0,1:T(8,128)(2,1)} %copy.238), channel_id=1, source_target_pairs={{0,4},{4,0},{1,5},{5,1},{2,6},{6,2},{3,7},{7,3},{8,12},{12,8},{9,1... | collective-permute-start | bytes 7077896 | tf_op jit(solution)/shard_map/ppermute | solution.py:32
  605.6 49.9 %collective-permute-start.34 = (bf16[4,2,96,768]{3,2,0,1:T(8,128)(2,1)}, bf16[4,2,96,768]{3,2,0,1:T(8,128)(2,1)}, u32[]{:S(2)}, u32[]{:S(2)}) collective-permute-start(bf16[4,2,96,768]{3,2,0,1:T(8,128)(2,1)} %copy.241), channel_id=1, source_target_pairs={{0,4},{4,0},{1,5},{5,1},{2,6},{6,2},{3,7},{7,3},{8,12},{12,8},{9,1... | collective-permute-start | bytes 3538952 | tf_op jit(solution)/shard_map/ppermute | solution.py:32
  613.7 45.8 %collective-permute-start.37 = (bf16[8,96,768]{2,1,0:T(8,128)(2,1)}, bf16[8,96,768]{2,1,0:T(8,128)(2,1)}, u32[]{:S(2)}, u32[]{:S(2)}) collective-permute-start(bf16[8,96,768]{2,1,0:T(8,128)(2,1)} %dynamic-slice_bitcast_fusion.2), channel_id=1, source_target_pairs={{0,2},{2,0},{1,3},{3,1},{4,6},{6,4},{5,7},{7,5},{8,10},{10,8},{9,1... | collective-permute-start | bytes 3538952 | tf_op jit(solution)/shard_map/ppermute | solution.py:32
  619.5 34.5 %all-to-all-start = ((bf16[4,272,192]{2,1,0:T(8,128)(2,1)}), bf16[4,272,192]{2,1,0:T(8,128)(2,1)}, u32[]{:S(2)}, u32[]{:S(2)}) async-start(bf16[4,272,192]{2,1,0:T(8,128)(2,1)} %bitcast.348), calls=%async_computation | async-start | bytes 1114112 | tf_op jit(solution)/shard_map/all_to_all | solution.py:364
  623.6 122.7 %all-reduce.13.cloned.1.call-start = ((), (), s32[]{:S(2)}) async-start(), calls=%async_computation.5 | async-start | bytes 3538944 | tf_op jit(solution)/shard_map/psum | solution.py:316
  626.1 46.4 %collective-permute-start.21 = (f32[1,2048]{1,0:T(1,128)S(1)}, f32[1,2048]{1,0:T(1,128)}, u32[]{:S(2)}, u32[]{:S(2)}) collective-permute-start(f32[1,2048]{1,0:T(1,128)S(1)} %add.649), channel_id=1, source_target_pairs={{0,16},{8,24},{16,0},{24,8},{1,17},{9,25},{17,1},{25,9},{2,18},{10... | collective-permute-start | bytes 24584 | tf_op jit(solution)/shard_map/ppermute | solution.py:282
  631.6 43.5 %collective-permute-start.59 = (bf16[192,1024]{1,0:T(8,128)(2,1)}, bf16[192,1024]{1,0:T(8,128)(2,1)}, u32[]{:S(2)}, u32[]{:S(2)}) collective-permute-start(bf16[192,1024]{1,0:T(8,128)(2,1)} %pad_maximum_fusion.26), channel_id=1, source_target_pairs={{0,4},{4,0},{1,5},{5,1},{2,6},{6,2},{3,7},{7,3},{8,12},{12,8},{9,1... | collective-permute-start | bytes 1179656 | tf_op jit(solution)/shard_map/ppermute | solution.py:32
  668.7 126.1 %all-reduce.15.cloned.1.call-start = ((), (), s32[]{:S(2)}) async-start(), calls=%async_computation.6 | async-start | bytes 1179648 | tf_op jit(solution)/shard_map/psum | solution.py:316
  677.2 123.6 %collective-permute-start.49 = (bf16[8,96,768]{2,1,0:T(8,128)(2,1)}, bf16[8,96,768]{2,1,0:T(8,128)(2,1)}, u32[]{:S(2)}, u32[]{:S(2)}) collective-permute-start(bf16[8,96,768]{2,1,0:T(8,128)(2,1)} %all-reduce.9.cloned.1.call-done), channel_id=1, source_target_pairs={{0,4},{4,0},{1,5},{5,1},{2,6},{6,2},{3,7},{7,3},{8,12},{12,8},{9,1... | collective-permute-start | bytes 3538952 | tf_op jit(solution)/shard_map/ppermute | solution.py:32
  677.7 123.1 %collective-permute-start.48 = (bf16[12,96,768]{2,1,0:T(8,128)(2,1)}, bf16[12,96,768]{2,1,0:T(8,128)(2,1)}, u32[]{:S(2)}, u32[]{:S(2)}) collective-permute-start(bf16[12,96,768]{2,1,0:T(8,128)(2,1)} %all-reduce.11.cloned.1.call-done), channel_id=1, source_target_pairs={{0,4},{4,0},{1,5},{5,1},{2,6},{6,2},{3,7},{7,3},{8,12},{12,8},{9,1... | collective-permute-start | bytes 5308424 | tf_op jit(solution)/shard_map/ppermute | solution.py:32
  746.4 54.4 %collective-permute-start.47 = (bf16[12,96,768]{2,1,0:T(8,128)(2,1)}, bf16[12,96,768]{2,1,0:T(8,128)(2,1)}, u32[]{:S(2)}, u32[]{:S(2)}) collective-permute-start(bf16[12,96,768]{2,1,0:T(8,128)(2,1)} %all-reduce.13.cloned.1.call-done), channel_id=1, source_target_pairs={{0,4},{4,0},{1,5},{5,1},{2,6},{6,2},{3,7},{7,3},{8,12},{12,8},{9,1... | collective-permute-start | bytes 5308424 | tf_op jit(solution)/shard_map/ppermute | solution.py:32
  (252 other events, 3410.8 us)
Sparse Core Ops, SparseCore 0:
  10.8 164.8 all-gather.2
  515.2 56.1 all-reduce.8
  585.5 83.1 all-reduce.10
  671.7 74.6 all-reduce.12
  756.4 38.4 all-reduce.14

commit v3 on v2

--- a/solution.py
+++ b/solution.py
@@ -1,3 +1,5 @@
+import functools
+
 import jax
 import jax.numpy as jnp
 from jax import lax
@@ -81,25 +83,132 @@
     return lax.optimization_barrier((value, event))[0]
 
 
-def order_kernel(slot_ref, held_ref, out_ref):
-    out_ref[0] = held_ref[0, :, 0]
-
-
-def order_tiles(held, slot, first, count):
-    _, pieces, slots, half, model = held.shape
+def needs(value, event):
+    first = lax.slice(event, (0,) * event.ndim, (1,) * event.ndim).reshape(())
+    return value + jnp.minimum(jnp.abs(first), 0).astype(value.dtype)
+
+
+def order_kernel(owner_ref, slot_ref, held_ref, out_ref, sem):
+    def copy(t):
+        return pltpu.make_async_copy(held_ref.at[owner_ref[t], :, slot_ref[t]], out_ref.at[t], sem.at[t])
+
+    for t in range(out_ref.shape[0]):
+        copy(t).start()
+    for t in range(out_ref.shape[0]):
+        copy(t).wait()
+
+
+def order_tiles(held, owner, slot):
+    count, (_, pieces, _, half, model) = owner.shape[0], held.shape
+    scalar = pl.BlockSpec(memory_space=pltpu.SMEM)
     return pl.pallas_call(
         order_kernel,
-        grid_spec=pltpu.PrefetchScalarGridSpec(
-            num_scalar_prefetch=1,
-            grid=(count,),
-            in_specs=[
-                pl.BlockSpec((1, pieces, 1, half, model), lambda t, s: (s[t] // slots, 0, s[t] % slots, 0, 0))
-            ],
-            out_specs=pl.BlockSpec((1, pieces, half, model), lambda t, s: (t, 0, 0, 0)),
-        ),
+        in_specs=[scalar, scalar, pl.BlockSpec(memory_space=pl.ANY)],
+        out_specs=pl.BlockSpec(memory_space=pltpu.VMEM),
         out_shape=jax.ShapeDtypeStruct((count, pieces, half, model), bf16),
+        scratch_shapes=[pltpu.SemaphoreType.DMA((count,))],
+        compiler_params=pltpu.CompilerParams(vmem_limit_bytes=24 * 2**20),
         name="order_tiles",
-    )(slot[first:first + count], held)
+    )(owner, slot, held)
+
+
+def collect_kernel(count, owner_ref, slot_ref, *refs):
+    sources, out_ref, sem = refs[:count], refs[-2], refs[-1]
+
+    def copies():
+        t = 0
+        for source in sources:
+            for i in range(source.shape[0]):
+                yield pltpu.make_async_copy(source.at[i], out_ref.at[owner_ref[t], slot_ref[t]], sem.at[t])
+                t += 1
+
+    for copy in copies():
+        copy.start()
+    for copy in copies():
+        copy.wait()
+
+
+def collect(sources, owner, slot, n, slots, into=None):
+    total, (half, model) = owner.shape[0], sources[0].shape[1:]
+    scalar, anywhere = pl.BlockSpec(memory_space=pltpu.SMEM), pl.BlockSpec(memory_space=pl.ANY)
+    whole = pl.BlockSpec(memory_space=pltpu.VMEM)
+    held = [] if into is None else [into]
+    return pl.pallas_call(
+        functools.partial(collect_kernel, len(sources)),
+        in_specs=[scalar] * 2 + [whole] * len(sources) + [anywhere] * len(held),
+        out_specs=anywhere,
+        out_shape=jax.ShapeDtypeStruct((n, slots, half, model), bf16),
+        input_output_aliases={2 + len(sources): 0} if held else {},
+        scratch_shapes=[pltpu.SemaphoreType.DMA((total,))],
+        compiler_params=pltpu.CompilerParams(vmem_limit_bytes=24 * 2**20),
+        name="collect",
+    )(owner, slot, *sources, *held)
+
+
+def attend_kernel(q_ref, *refs):
+    kv_refs, (o_ref, total_ref) = refs[:-2], refs[-2:]
+    scale = HEAD_DIM ** (-0.5)
+    for i in range(q_ref.shape[0]):
+        scores = [dot(kv[0, i], q_ref[i], ((0,), (0,))) * scale for kv in kv_refs]
+        top = functools.reduce(jnp.maximum, [jnp.max(s, 0, keepdims=True) for s in scores])
+        raised = [jnp.exp(s - top) for s in scores]
+        total = sum(jnp.sum(e, 0, keepdims=True) for e in raised)
+        share = 1.0 / total
+        o_ref[i] = sum(
+            dot(kv[1, i], (e * share).astype(bf16), ((1,), (0,))) for kv, e in zip(kv_refs, raised)
+        ).astype(bf16)
+        total_ref[i] = top + jnp.log(total)
+
+
+def attend(queries, blocks):
+    heads, size, rows = queries.shape
+    step = 2
+    short = pl.BlockSpec((step, size, rows), lambda h: (h, 0, 0))
+    block = pl.BlockSpec((2, step, size, rows), lambda h: (0, h, 0, 0))
+    return pl.pallas_call(
+        attend_kernel,
+        grid=(heads // step,),
+        in_specs=[short] + [block] * len(blocks),
+        out_specs=[short, pl.BlockSpec((step, 1, rows), lambda h: (h, 0, 0))],
+        out_shape=[
+            jax.ShapeDtypeStruct((heads, size, rows), bf16),
+            jax.ShapeDtypeStruct((heads, 1, rows), f32),
+        ],
+        compiler_params=pltpu.CompilerParams(vmem_limit_bytes=32 * 2**20),
+        name="attend",
+    )(queries, *blocks)
+
+
+def attend_back_kernel(count, q_ref, g_ref, total_ref, *refs):
+    kv_refs, dq_ref, dkv_refs = refs[:count], refs[count], refs[count + 1:]
+    scale = HEAD_DIM ** (-0.5)
+    for i in range(q_ref.shape[0]):
+        soft = [jnp.exp(dot(kv[0, i], q_ref[i], ((0,), (0,))) * scale - total_ref[i]) for kv in kv_refs]
+        grad_soft = [dot(kv[1, i], g_ref[i], ((0,), (0,))) for kv in kv_refs]
+        mean = sum(jnp.sum(p * g, 0, keepdims=True) for p, g in zip(soft, grad_soft))
+        grad_scores = [(p * (g - mean)).astype(bf16) for p, g in zip(soft, grad_soft)]
+        dq = sum(dot(kv[0, i], ds, ((1,), (0,))) for kv, ds in zip(kv_refs, grad_scores))
+        dq_ref[i] = (dq * scale).astype(bf16)
+        for dkv, p, ds in zip(dkv_refs, soft, grad_scores):
+            dkv[0, i] = (dot(q_ref[i], ds, ((1,), (1,))) * scale).astype(bf16)
+            dkv[1, i] = dot(g_ref[i], p.astype(bf16), ((1,), (1,))).astype(bf16)
+
+
+def attend_back(queries, blocks, gradient, total):
+    heads, size, rows = queries.shape
+    step = 2
+    short = pl.BlockSpec((step, size, rows), lambda h: (h, 0, 0))
+    block = pl.BlockSpec((2, step, size, rows), lambda h: (0, h, 0, 0))
+    return pl.pallas_call(
+        functools.partial(attend_back_kernel, len(blocks)),
+        grid=(heads // step,),
+        in_specs=[short, short, pl.BlockSpec((step, 1, rows), lambda h: (h, 0, 0))] + [block] * len(blocks),
+        out_specs=[short] + [block] * len(blocks),
+        out_shape=[jax.ShapeDtypeStruct((heads, size, rows), bf16)]
+        + [jax.ShapeDtypeStruct(kv.shape, bf16) for kv in blocks],
+        compiler_params=pltpu.CompilerParams(vmem_limit_bytes=32 * 2**20),
+        name="attend_back",
+    )(queries, gradient, total, *blocks)
 
 
 def adamw_update(weight, moment_one, moment_two, gradient, rate):
@@ -111,15 +220,16 @@
     return (weight, moment_one, moment_two)
 
 
-def tile_adamw_kernel(tile_ref, used_ref, core_ref, w_ref, m_ref, v_ref, low_ref, high_ref, w_out, m_out, v_out):
+def tile_adamw_kernel(used_ref, core_ref, w_ref, m_ref, v_ref, own_ref, oth_ref, w_out, m_out, v_out):
     slot = pl.program_id(0)
-    half = low_ref.shape[2]
+    half = w_ref.shape[1] // 2
 
     @pl.when(used_ref[slot] == 1)
     def _():
-        for h, g_ref in enumerate((low_ref, high_ref)):
-            at = pl.ds(h * half, half)
-            new = adamw_update(w_ref[0, at], m_ref[0, at], v_ref[0, at], g_ref[0, 0].astype(f32), learn_rate)
+        for h, g_ref in enumerate((own_ref, oth_ref)):
+            side = core_ref[0] if h == 0 else 1 - core_ref[0]
+            at = pl.ds(pl.multiple_of(side * half, half), half)
+            new = adamw_update(w_ref[0, at], m_ref[0, at], v_ref[0, at], g_ref[0].astype(f32), learn_rate)
             w_out[0, at], m_out[0, at], v_out[0, at] = new
 
     @pl.when(used_ref[slot] != 1)
@@ -127,24 +237,22 @@
         w_out[...], m_out[...], v_out[...] = w_ref[...], m_ref[...], v_ref[...]
 
 
-def tile_adamw(tile_of, used, core, weight, first, second, grads):
-    slots, rows, width = weight.shape
-    half = rows // 2
-    block = pl.BlockSpec((1, rows, width), lambda s, t, u, c: (s, 0, 0))
-    low = pl.BlockSpec((1, 1, half, width), lambda s, t, u, c: (c[0], t[s], 0, 0))
-    high = pl.BlockSpec((1, 1, half, width), lambda s, t, u, c: (1 - c[0], t[s], 0, 0))
+def tile_adamw(used, core, state, own, oth):
+    slots, rows, width = state[0].shape
+    block = pl.BlockSpec((1, rows, width), lambda s, u, c: (s, 0, 0))
+    grad_block = pl.BlockSpec((1, rows // 2, width), lambda s, u, c: (s, 0, 0))
     return pl.pallas_call(
         tile_adamw_kernel,
         grid_spec=pltpu.PrefetchScalarGridSpec(
-            num_scalar_prefetch=3,
+            num_scalar_prefetch=2,
             grid=(slots,),
-            in_specs=[block, block, block, low, high],
+            in_specs=[block, block, block, grad_block, grad_block],
             out_specs=[block, block, block],
         ),
-        out_shape=[jax.ShapeDtypeStruct(weight.shape, f32)] * 3,
-        compiler_params=pltpu.CompilerParams(vmem_limit_bytes=32 * 2**20),
+        out_shape=[jax.ShapeDtypeStruct(state[0].shape, f32)] * 3,
+        compiler_params=pltpu.CompilerParams(vmem_limit_bytes=40 * 2**20),
         name="tile_adamw",
-    )(tile_of, used, core, weight, first, second, grads, grads)
+    )(used, core, *state, own, oth)
 
 
 def body(
@@ -181,11 +289,11 @@
     core_arr = core.reshape(1).astype(jnp.int32)
     piece_at = core * 2 + ty
 
+    owner = tile_slot // slots
     held = lax.dynamic_slice(tile_master, (0, core * half, 0), (slots, half, model)).astype(bf16)
-
     held = lax.all_gather(held, ("fsdp", "ctx", "ty"), axis=0, tiled=True).reshape(n, 4, slots, half, model)
 
-    block_at = piece_at * 2 + tx
+    block_at = (core * 2 + tx) * 2 + ty
     vocab_pad = 8 * BLOCK - VOCAB
     wide = BLOCK + rows
     embed_pad = jnp.pad(embedding.astype(bf16), ((0, 0), (0, vocab_pad)))
@@ -210,7 +318,7 @@
     )
     tables = lax.all_gather(packed, "fsdp", axis=0)
     embed_all = tables[:, :own_dim, :BLOCK].reshape(model, BLOCK)
-    for axis, at in (("tx", tx), ("ty", ty), ("ctx", core)):
+    for axis, at in (("ty", ty), ("tx", tx), ("ctx", core)):
         embed_all = both(axis, embed_all, at, 1)
     places_own = tables[:, :own_dim, BLOCK:].reshape(model, rows).T.astype(f32)
     gains = tables[:, own_dim:own_dim + 2 * norms, :own_dim].transpose(1, 0, 2)
@@ -226,34 +334,26 @@
     pick_ids = (ids.reshape(rows, 1) == column_at).astype(bf16)
     stream = dot(pick_ids, embed_all, ((1,), (1,))) + places_own
 
-    scale = HEAD_DIM ** (-0.5)
     weights, kept_layers = [], []
     for layer in range(LAYERS):
-        tiles = order_tiles(held, tile_slot, 12 * layer, 12)
-        tiles = tiles.reshape(12 * columns, model)
+        mine = slice(12 * layer, 12 * layer + 12)
+        tiles = order_tiles(held, owner[mine], tile_slot[mine] % slots).reshape(12 * columns, model)
         w_qkv, w_o = tiles[:3 * columns], tiles[3 * columns:4 * columns]
         w_in, w_out = tiles[4 * columns:8 * columns], tiles[8 * columns:]
         weights.append((w_qkv, w_o, w_in, w_out))
         normed = norm_parts(stream, gains[0, 2 * layer], gains[1, 2 * layer])[0].astype(bf16)
         kv = dot(w_qkv[columns:], normed, ((1,), (1,))).astype(bf16)
-        kv_two = jnp.concatenate([kv, over("ty", kv)], 1)
-        kv_all = jnp.concatenate([kv_two, over("ctx", kv_two)], 1).reshape(2, heads, HEAD_DIM, 4 * rows)
+        kv_y = over("ty", kv)
+        blocks = [kv, kv_y, over("ctx", kv), over("ctx", kv_y)]
+        blocks = [block.reshape(2, heads, HEAD_DIM, rows) for block in blocks]
         queries = dot(w_qkv[:columns], normed, ((1,), (1,))).astype(bf16).reshape(heads, HEAD_DIM, rows)
-        keys, values = kv_all[0], kv_all[1]
-        scores = jnp.einsum("hcq,hck->hqk", queries, keys, preferred_element_type=f32) * scale
-        row_top = jnp.max(scores, -1, keepdims=True)
-        log_total = row_top + jnp.log(jnp.sum(jnp.exp(scores - row_top), -1, keepdims=True))
-        attn = jnp.exp(scores - log_total).astype(bf16)
-        mixed = (
-            jnp.einsum("hqk,hck->hcq", attn, values, preferred_element_type=f32)
-            .astype(bf16)
-            .reshape(columns, rows)
-        )
+        mixed, log_total = attend(queries, blocks)
+        mixed = mixed.reshape(columns, rows)
         middle = stream + sum_over_x(dot(mixed, w_o, ((0,), (0,))))
         normed_mlp = norm_parts(middle, gains[0, 2 * layer + 1], gains[1, 2 * layer + 1])[0].astype(bf16)
         pre_gelu = dot(normed_mlp, w_in, ((1,), (1,)))
         activation = jax.nn.gelu(pre_gelu, approximate=False).astype(bf16)
-        kept_layers.append((stream, middle, queries, keys, values, log_total, mixed, pre_gelu))
+        kept_layers.append((stream, middle, queries, blocks, log_total, mixed, pre_gelu))
         stream = middle + sum_over_x(dot(activation, w_out, ((1,), (0,))))
 
     final_rows = lax.dynamic_slice_in_dim(stream, tx * share, share, 0)
@@ -290,69 +390,71 @@
     final_norm_grad = final_norm_grad + over("tx", final_norm_grad)
 
     embed_part = dot(final_normed, grad_logits, ((0,), (0,))).astype(bf16)
-    for axis, at in (("ctx", core), ("ty", ty), ("tx", tx)):
+    embed_part = lax.psum_scatter(embed_part, "fsdp", scatter_dimension=0, tiled=True)
+    offloaded = [embed_part]
+    for axis, at in (("ctx", core), ("tx", tx), ("ty", ty)):
         cut = embed_part.shape[1] // 2
         keep = lax.dynamic_slice_in_dim(embed_part, at * cut, cut, 1)
         send = lax.dynamic_slice_in_dim(embed_part, cut - at * cut, cut, 1)
         embed_part = add_halves(keep, over(axis, send))
-    embed_head = lax.all_to_all(embed_part.reshape(n, own_dim, BLOCK), "fsdp", 0, 0)
-    embed_head = jnp.sum(embed_head.astype(f32), 0).astype(bf16)
-    for axis, at in (("tx", tx), ("ty", ty), ("ctx", core)):
+    embed_head = embed_part
+    for axis, at in (("ty", ty), ("tx", tx), ("ctx", core)):
         embed_head = both(axis, embed_head, at, 1)
 
     norm_grads = [None] * norms
     norm_grads[2 * LAYERS] = final_norm_grad
-    crossed = []
-
-    def plane_sum(grads):
+    tile_grads, tile_list = [], []
+
+    def core_sum(grads):
         keep = lax.dynamic_slice_in_dim(grads, core * 2, 2, 1).astype(bf16)
         send = lax.dynamic_slice_in_dim(grads, 2 - core * 2, 2, 1).astype(bf16)
-        two = add_halves(keep, over("ctx", send))
-        keep = lax.dynamic_index_in_dim(two, ty, 1, False)
-        send = lax.dynamic_index_in_dim(two, 1 - ty, 1, False)
+        return add_halves(keep, over("ctx", send)).transpose(1, 0, 2, 3)
+
+    def neighbour_sum(two):
+        keep = lax.dynamic_index_in_dim(two, ty, 0, False)
+        send = lax.dynamic_index_in_dim(two, 1 - ty, 0, False)
         return add_halves(keep, over("ty", send))
 
-    def cross(own):
-        crossed.append(lax.psum(after(own, crossed[-1]) if crossed else own, "fsdp"))
-
-    attn_own = None
+    def offloaded_sum(flat, axis):
+        offloaded.append(lax.psum_scatter(after(flat, offloaded[-1]), axis, scatter_dimension=0, tiled=True))
+        return offloaded[-1]
+
+    attn_two = None
     for layer in reversed(range(LAYERS)):
-        stream, middle, queries, keys, values, log_total, mixed, pre_gelu = kept_layers[layer]
+        stream, middle, queries, blocks, log_total, mixed, pre_gelu = kept_layers[layer]
         w_qkv, w_o, w_in, w_out = weights[layer]
         branch = gradient.astype(bf16)
         activation = jax.nn.gelu(pre_gelu, approximate=False).astype(bf16)
         grad_act = dot(branch, w_out, ((1,), (1,)))
         grad_pre = (grad_act * gelu_slope(pre_gelu)).astype(bf16)
         normed_mlp, hat_mlp, inv_mlp = norm_parts(middle, gains[0, 2 * layer + 1], gains[1, 2 * layer + 1])
-        grad_normed = sum_over_x(dot(grad_pre, w_in, ((1,), (0,))))
-        grad_out = dot(activation, branch, ((0,), (0,))).reshape(4, 4, half, model)
-        grad_in = dot(grad_pre, normed_mlp.astype(bf16), ((0,), (0,))).reshape(4, 4, half, model)
-        mlp_own = plane_sum(jnp.concatenate([grad_in, grad_out], 0))
-        cross(mlp_own if attn_own is None else jnp.concatenate([mlp_own, attn_own], 0))
+        partial = dot(grad_pre, w_in, ((1,), (0,))).astype(bf16)
+        grad_normed = sum_over_x(partial)
+        grad_out = dot(needs(activation, partial), branch, ((0,), (0,))).reshape(4, 4, half, model)
+        grad_in = dot(grad_pre, needs(normed_mlp.astype(bf16), partial), ((0,), (0,))).reshape(4, 4, half, model)
+        two = core_sum(jnp.concatenate([grad_in, grad_out], 0))
+        tile_list += range(12 * layer + 4, 12 * layer + 12)
+        if attn_two is not None:
+            two = jnp.concatenate([two, attn_two], 1)
+            tile_list += range(12 * layer + 12, 12 * layer + 16)
         grad_middle = gradient + norm_back(grad_normed, hat_mlp, inv_mlp, gains[0, 2 * layer + 1])
         norm_grads[2 * layer + 1] = jnp.stack([jnp.sum(grad_normed * hat_mlp, 0), jnp.sum(grad_normed, 0)])
         branch = grad_middle.astype(bf16)
         grad_proj_out = dot(mixed, branch, ((1,), (0,)))
         grad_mixed = dot(w_o, branch, ((1,), (1,))).astype(bf16).reshape(heads, HEAD_DIM, rows)
-        soft = jnp.exp(
-            jnp.einsum("hcq,hck->hqk", queries, keys, preferred_element_type=f32) * scale - log_total
-        )
-        grad_soft = jnp.einsum("hcq,hck->hqk", grad_mixed, values, preferred_element_type=f32)
-        grad_scores = (soft * (grad_soft - jnp.sum(soft * grad_soft, -1, keepdims=True))).astype(bf16)
-        grad_keys = jnp.einsum("hcq,hqk->hck", queries, grad_scores, preferred_element_type=f32) * scale
-        grad_values = jnp.einsum("hcq,hqk->hck", grad_mixed, soft.astype(bf16), preferred_element_type=f32)
-        grad_queries = jnp.einsum("hck,hqk->hcq", keys, grad_scores, preferred_element_type=f32) * scale
-        grad_kv = jnp.stack([grad_keys, grad_values]).astype(bf16).reshape(2 * columns, 4 * rows)
-        pair = grad_kv[:, :2 * rows].astype(f32) + over("ctx", grad_kv[:, 2 * rows:]).astype(f32)
-        grad_kv = (pair[:, :rows] + over("ty", pair[:, rows:].astype(bf16)).astype(f32)).astype(bf16)
-        grad_qkv = jnp.concatenate([grad_queries.astype(bf16).reshape(columns, rows), grad_kv], 0)
+        grad_queries, kv_own, kv_y, kv_core, kv_both = attend_back(queries, blocks, grad_mixed, log_total)
+        kv_own = kv_own.astype(f32) + over("ctx", kv_core).astype(f32)
+        from_y = over("ty", add_halves(kv_y, over("ctx", kv_both)))
+        grad_kv = (kv_own + from_y.astype(f32)).astype(bf16).reshape(2 * columns, rows)
+        two = needs(two, from_y) if layer else two
+        tile_grads.append(offloaded_sum(two.reshape(-1, half, model), "ty"))
+        grad_qkv = jnp.concatenate([grad_queries.reshape(columns, rows), grad_kv], 0)
         normed, hat_attn, inv_attn = norm_parts(stream, gains[0, 2 * layer], gains[1, 2 * layer])
-        grad_normed = sum_over_x(dot(grad_qkv, w_qkv, ((0,), (0,))))
-        grad_w = dot(grad_qkv, normed.astype(bf16), ((1,), (0,)))
+        partial = dot(grad_qkv, w_qkv, ((0,), (0,))).astype(bf16)
+        grad_normed = sum_over_x(partial)
+        grad_w = dot(grad_qkv, needs(normed.astype(bf16), partial), ((1,), (0,)))
         grad_w = jnp.concatenate([grad_w, grad_proj_out], 0).reshape(4, 4, half, model)
-        attn_own = plane_sum(grad_w)
-        if layer == 0:
-            cross(attn_own)
+        attn_two = core_sum(grad_w)
         gradient = grad_middle + norm_back(grad_normed, hat_attn, inv_attn, gains[0, 2 * layer])
         norm_grads[2 * layer] = jnp.stack([jnp.sum(grad_normed * hat_attn, 0), jnp.sum(grad_normed, 0)])
 
@@ -362,6 +464,7 @@
     )
     state = state.reshape(rows + 16, n, own_dim).transpose(1, 0, 2)
     state = lax.all_to_all(state, "fsdp", 0, 0)[:, None]
+    last_grads = needs(neighbour_sum(attn_two), state)
     state = both("ty", state, ty, 1)
     state = both("ctx", state, core, 1)
     norm_grad = jnp.sum(state[:, :, rows:rows + 2 * norms].astype(f32), (0, 1)).reshape(2, norms, own_dim)
@@ -371,21 +474,18 @@
     embed_tail = dot(token_grads.reshape(n * 4 * rows, own_dim), picks, ((0,), (0,)))
     embed_grad = (embed_tail + embed_head.astype(f32))[:, :VOCAB]
 
-    def to_both_cores(own):
-        return jnp.stack([own, over("ctx", own)])
-
-    top, middle, bottom, last = (to_both_cores(own) for own in crossed)
-    grads = jnp.concatenate(
-        [last, bottom[:, :8], bottom[:, 8:], middle[:, :8], middle[:, 8:], top], 1
-    )
-    is_slot = (z * slots + jnp.arange(slots, dtype=jnp.int32))[:, None] == tile_slot[None, :]
-    used = jnp.any(is_slot, 1).astype(jnp.int32)
-    tile_of = jnp.sum(jnp.where(is_slot, jnp.arange(TILES, dtype=jnp.int32)[None, :], 0), 1)
-    tile_upd = tile_adamw(tile_of, used, core_arr, tile_master, tile_first, tile_second, grads)
+    at = jnp.array(tile_list, jnp.int32)
+    sent = collect(tile_grads, owner[at], tile_slot[at] % slots, n, slots)
+    sent = collect([last_grads], owner[:4], tile_slot[:4] % slots, n, slots, sent)
+    tile_sum = offloaded_sum(sent.reshape(-1, half, model), "fsdp")
+    used = jnp.any((tile_slot - z * slots)[None, :] == jnp.arange(slots, dtype=jnp.int32)[:, None], 1).astype(jnp.int32)
+    state = (tile_master, tile_first, tile_second)
     embed_upd = adamw_update(embedding, embed_first, embed_second, embed_grad, learn_rate)
     position_upd = adamw_update(position_table, position_first, position_second, position_grad, learn_rate)
     norm_upd = adamw_update(norm_params, norm_first, norm_second, norm_grad, small_rate)
     bias_upd = adamw_update(head_bias, bias_first, bias_second, bias_grad, small_rate)
+    tile_sum = after(tile_sum, (embed_upd, position_upd, norm_upd, bias_upd, loss_value))
+    tile_upd = tile_adamw(used, core_arr, state, tile_sum, over("ctx", tile_sum))
     return (loss_value, *tile_upd, *embed_upd, *position_upd, *norm_upd, *bias_upd)
 
 

time: 841 us -> 754 us (0.90)
  other arithmetic: 117 us -> 62.7 us
  Pallas kernels: 45.2 us -> 81.8 us
  local copies, waits for them, and re-layouts: 97.5 us -> 61.3 us
  matrix products: 90.9 us -> 64.4 us
  starting transfers between devices: 62.4 us -> 45 us
    psum x4 -> x0, waiting for transfers between devices: 95 us -> none  [cross(): lax.psum(after(own, crossed[-1]) if crossed else own, 'fsdp')]
    reduce_scatter x0 -> x5, waiting for transfers between devices: none -> 64.1 us  [the longest x4 64.1 us: offloaded_sum(): lax.psum_scatter(after(flat, offloaded[-1]), axis, scatter_dimension=0, t...]
    ppermute x58 -> x56, waiting for transfers between devices: 162 us -> 204 us  [over(): return lax.ppermute(v, axis, FLIP)]
    dot_general x18 -> x0, matrix products: 33.8 us -> none  [the longest x3 8.51 us: body(): jnp.einsum('hcq,hck->hqk', grad_mixed, values, preferred_element_type=f32)]
    pallas_call x3 -> x11, Pallas kernels: 31.7 us -> 65.1 us  [the longest x3 27 us: attend_back(): pl.pallas_call(functools.partial(attend_back_kernel, len(blocks)), grid=(...]
    convert_element_type x15 -> x7, other arithmetic: 25.4 us -> 2.11 us  [add_halves(): return (keep.astype(f32) + come.astype(f32)).astype(bf16)]
    concatenate x12 -> x4, other arithmetic: 21.5 us -> 3.86 us  [the longest x1 2.1 us: body(): two = jnp.concatenate([two, attn_two], 1)]
    ppermute x58 -> x56, starting transfers between devices: 50.5 us -> 34.5 us  [over(): return lax.ppermute(v, axis, FLIP)]
  transfers between devices with their start and end apart: 67 -> 65, of which waited for: 32 -> 41; matrix products, arithmetic and copies ran while one was open for 24% -> 16% of each run, Pallas kernels for 3% -> 5%
where the time goes in v3:
time: 754 us; the launch traced here: 747 us
  waiting for transfers between devices  379 us (50%)
  Pallas kernels  81.8 us (11%)
  matrix products  64.4 us (9%)
  other arithmetic  62.7 us (8%)
  local copies, waits for them, and re-layouts  61.3 us (8%)
  starting transfers between devices  45 us (6%)
  blocking collectives  26.8 us (4%)
  between operations  26 us (3%)
    ppermute x56, waiting for transfers between devices, over(): return lax.ppermute(v, axis, FLIP)  204 us
    all_gather x1, waiting for transfers between devices, body(): lax.all_gather(held, ('fsdp', 'ctx', 'ty'), axis=0, tiled=True)  93.3 us
    dot_general x44, matrix products, dot(): lax.dot_general(left, right, (dims, ((), ())), preferred_element_type=f32)  64.4 us
    reduce_scatter x4, waiting for transfers between devices, offloaded_sum(): lax.psum_scatter(after(flat, offloaded[-1]), axis, scatter_dimension=0, t...  64.1 us
    ppermute x56, starting transfers between devices, over(): return lax.ppermute(v, axis, FLIP)  34.5 us
    unnamed x372, local copies, waits for them, and re-layouts  32.5 us
    pallas_call x3, Pallas kernels, attend_back(): pl.pallas_call(functools.partial(attend_back_kernel, len(blocks)), grid=(...  27 us
    all_gather x1, blocking collectives, body(): tables = lax.all_gather(packed, 'fsdp', axis=0)  26.8 us
  transfers between devices with their start and end apart: 65, of which 41 were waited for; matrix products, arithmetic and copies ran while one was open for 16% of the time, Pallas kernels for 5%

profile of v3, /device:TPU:0, one launch (start us, length us, event | category | flops | bytes accessed | tf_op | source)
XLA Modules:
  0.0 746.8 jit_solution(3549782937469779929)
XLA Ops:
  13.3 26.8 %all-gather = bf16[832,512]{1,0:T(8,128)(2,1)S(1)} all-gather(bf16[208,512]{1,0:T(8,128)(2,1)S(1)} %fusion.111), channel_id=2, replica_groups=mesh['fsdp'=4,'ctx'=2,'ty'=2,'tx'=2] {'fsdp'}, dimensions={0}, use_global_device_ids=true | all-gather | bytes 1064960 | tf_op jit(solution)/shard_map/all_gather | solution.py:319
  42.5 12.7 %collective-permute-done = bf16[768,256]{1,0:T(8,128)(2,1)S(1)} collective-permute-done((bf16[768,256]{1,0:T(8,128)(2,1)S(1)}, bf16[768,256]{1,0:T(8,128)(2,1)S(1)}, u32[]{:S(2)}, u32[]{:S(2)}) %collective-permute-start) | collective-permute-done | bytes 393248 | tf_op jit(solution)/shard_map/ppermute | solution.py:34
  56.7 14.6 %collective-permute-done.1 = bf16[768,512]{1,0:T(8,128)(2,1)} collective-permute-done((bf16[768,512]{1,0:T(8,128)(2,1)S(1)}, bf16[768,512]{1,0:T(8,128)(2,1)}, u32[]{:S(2)}, u32[]{:S(2)}) %collective-permute-start.1) | collective-permute-done | bytes 786464 | tf_op jit(solution)/shard_map/ppermute | solution.py:34
  82.4 93.3 %all-gather.3.cloned.1.call-done = bf16[192,96,768]{2,1,0:T(8,128)(2,1)} async-done(((bf16[12,96,768]{2,1,0:T(8,128)(2,1)}), bf16[192,96,768]{2,1,0:T(8,128)(2,1)}) %all-gather.3.cloned.1.call-update) | async-done | bytes 28311568 | tf_op jit(solution)/shard_map/all_gather | solution.py:294
  181.2 9.6 %collective-permute-done.3 = bf16[768,256]{1,0:T(8,128)(2,1)S(1)} collective-permute-done((bf16[768,256]{1,0:T(8,128)(2,1)S(1)}, bf16[768,256]{1,0:T(8,128)(2,1)S(1)}, u32[]{:S(2)}, u32[]{:S(2)}) %collective-permute-start.3) | collective-permute-done | bytes 393248 | tf_op jit(solution)/shard_map/ppermute | solution.py:34
  200.9 9.3 %collective-permute-done.6 = bf16[256,768]{1,0:T(8,128)(2,1)S(1)} collective-permute-done((bf16[256,768]{1,0:T(8,128)(2,1)S(1)}, bf16[256,768]{1,0:T(8,128)(2,1)S(1)}, u32[]{:S(2)}, u32[]{:S(2)}) %collective-permute-start.6) | collective-permute-done | bytes 393248 | tf_op jit(solution)/shard_map/ppermute | solution.py:34
  229.8 8.4 %collective-permute-done.8 = bf16[768,256]{1,0:T(8,128)(2,1)S(1)} collective-permute-done((bf16[768,256]{1,0:T(8,128)(2,1)S(1)}, bf16[768,256]{1,0:T(8,128)(2,1)S(1)}, u32[]{:S(2)}, u32[]{:S(2)}) %collective-permute-start.8) | collective-permute-done | bytes 393248 | tf_op jit(solution)/shard_map/ppermute | solution.py:34
  247.9 9.3 %collective-permute-done.11 = bf16[256,768]{1,0:T(8,128)(2,1)S(1)} collective-permute-done((bf16[256,768]{1,0:T(8,128)(2,1)S(1)}, bf16[256,768]{1,0:T(8,128)(2,1)S(1)}, u32[]{:S(2)}, u32[]{:S(2)}) %collective-permute-start.11) | collective-permute-done | bytes 393248 | tf_op jit(solution)/shard_map/ppermute | solution.py:34
  303.7 8.5 %collective-permute-done.16 = bf16[256,768]{1,0:T(8,128)(2,1)S(1)} collective-permute-done((bf16[256,768]{1,0:T(8,128)(2,1)S(1)}, bf16[256,768]{1,0:T(8,128)(2,1)S(1)}, u32[]{:S(2)}, u32[]{:S(2)}) %collective-permute-start.16) | collective-permute-done | bytes 393248 | tf_op jit(solution)/shard_map/ppermute | solution.py:34
  322.2 8.6 %collective-permute-done.17 = bf16[256,768]{1,0:T(8,128)(2,1)} collective-permute-done((bf16[256,768]{1,0:T(8,128)(2,1)}, bf16[256,768]{1,0:T(8,128)(2,1)}, u32[]{:S(2)}, u32[]{:S(2)}) %collective-permute-start.17) | collective-permute-done | bytes 393248 | tf_op jit(solution)/shard_map/ppermute | solution.py:34
  365.3 9.4 %attend_back.3 = (bf16[8,48,256]{2,1,0:T(8,128)(2,1)S(1)}, bf16[2,8,48,256]{3,2,1,0:T(8,128)(2,1)S(1)}, bf16[2,8,48,256]{3,2,1,0:T(8,128)(2,1)S(1)}, bf16[2,8,48...) custom-call(bf16[8,48,256]{2,1,0:T(8,128)(2,1)S(1)} %bitcast.226, bf16[8,48,256]{2,1,0:T(8,128)(2,1)S(1)} %bitcast.259, ...), custom_call_target="tpu_custom_call" | custom-call | tf_op jit(solution)/shard_map/attend_back/pallas_call | solution.py:202
  380.6 8.1 %collective-permute-done.29 = bf16[2,8,48,256]{3,2,1,0:T(8,128)(2,1)S(1)} collective-permute-done((bf16[2,8,48,256]{3,2,1,0:T(8,128)(2,1)S(1)}, bf16[2,8,48,256]{3,2,1,0:T(8,128)(2,1)S(1)}, u32[]{:S(2)}, u32[]{:S(2)}) %collective-permute-start.29) | collective-permute-done | bytes 393248 | tf_op jit(solution)/shard_map/ppermute | solution.py:34
  422.7 9.1 %attend_back.4 = (bf16[8,48,256]{2,1,0:T(8,128)(2,1)S(1)}, bf16[2,8,48,256]{3,2,1,0:T(8,128)(2,1)S(1)}, bf16[2,8,48,256]{3,2,1,0:T(8,128)(2,1)S(1)}, bf16[2,8,48...) custom-call(bf16[8,48,256]{2,1,0:T(8,128)(2,1)S(1)} %bitcast.224, bf16[8,48,256]{2,1,0:T(8,128)(2,1)S(1)} %bitcast.260, ...), custom_call_target="tpu_custom_call" | custom-call | tf_op jit(solution)/shard_map/attend_back/pallas_call | solution.py:202
  435.1 12.1 %collective-permute-done.34 = bf16[2,8,48,256]{3,2,1,0:T(8,128)(2,1)S(1)} collective-permute-done((bf16[2,8,48,256]{3,2,1,0:T(8,128)(2,1)S(1)}, bf16[2,8,48,256]{3,2,1,0:T(8,128)(2,1)S(1)}, u32[]{:S(2)}, u32[]{:S(2)}) %collective-permute-start.34) | collective-permute-done | bytes 393248 | tf_op jit(solution)/shard_map/ppermute | solution.py:34
  455.9 9.4 %collective-permute-done.35 = bf16[256,768]{1,0:T(8,128)(2,1)S(1)} collective-permute-done((bf16[256,768]{1,0:T(8,128)(2,1)S(1)}, bf16[256,768]{1,0:T(8,128)(2,1)S(1)}, u32[]{:S(2)}, u32[]{:S(2)}) %collective-permute-start.35) | collective-permute-done | bytes 393248 | tf_op jit(solution)/shard_map/ppermute | solution.py:34
  486.0 13.1 %reduce-scatter.10.cloned.1.call-done.refs_1_ = bf16[12,96,768]{2,1,0:T(8,128)(2,1)} async-done(((bf16[24,96,768]{2,1,0:T(8,128)(2,1)}), bf16[12,96,768]{2,1,0:T(8,128)(2,1)}) %reduce-scatter.10.cloned.1.call-update) | async-done | bytes 1769488 | tf_op jit(solution)/shard_map/reduce_scatter | solution.py:419
  504.0 8.5 %attend_back.5 = (bf16[8,48,256]{2,1,0:T(8,128)(2,1)S(1)}, bf16[2,8,48,256]{3,2,1,0:T(8,128)(2,1)S(1)}, bf16[2,8,48,256]{3,2,1,0:T(8,128)(2,1)S(1)}, bf16[2,8,48...) custom-call(bf16[8,48,256]{2,1,0:T(8,128)(2,1)S(1)} %bitcast.222, bf16[8,48,256]{2,1,0:T(8,128)(2,1)S(1)} %bitcast.261, ...), custom_call_target="tpu_custom_call" | custom-call | tf_op jit(solution)/shard_map/attend_back/pallas_call | solution.py:202
  518.0 16.6 %collective-permute-done.39 = bf16[2,8,48,256]{3,2,1,0:T(8,128)(2,1)S(1)} collective-permute-done((bf16[2,8,48,256]{3,2,1,0:T(8,128)(2,1)S(1)}, bf16[2,8,48,256]{3,2,1,0:T(8,128)(2,1)S(1)}, u32[]{:S(2)}, u32[]{:S(2)}) %collective-permute-start.39) | collective-permute-done | bytes 393248 | tf_op jit(solution)/shard_map/ppermute | solution.py:34
  562.9 8.5 %all-to-all-done = bf16[4,272,192]{2,1,0:T(8,128)(2,1)} async-done(((bf16[4,272,192]{2,1,0:T(8,128)(2,1)}), bf16[4,272,192]{2,1,0:T(8,128)(2,1)}, u32[]{:S(2)}, u32[]{:S(2)}) %all-to-all-start) | async-done | bytes 417824 | tf_op jit(solution)/shard_map/all_to_all | solution.py:466
  577.7 7.1 collect.2.refs_1_
  593.6 12.6 %collective-permute-done.21 = f32[1,2048]{1,0:T(1,128)S(1)} collective-permute-done((f32[1,2048]{1,0:T(1,128)S(1)}, f32[1,2048]{1,0:T(1,128)S(1)}, u32[]{:S(2)}, u32[]{:S(2)}) %collective-permute-start.21) | collective-permute-done | bytes 8224 | tf_op jit(solution)/shard_map/ppermute | solution.py:34
  645.2 8.2 %fusion = f32[192,2048]{1,0:T(8,128)} fusion(bf16[4096,192]{1,0:T(8,128)(2,1)S(1)} %bitcast.308, s32[4096]{0:T(1024)S(1)} %add_select_fusion), kind=kOutput, calls=%fused_computation.3 | convolution fusion | flops 3229614080 | bytes 3162112 | tf_op jit(solution)/shard_map/dot_general | solution.py:38
  662.6 50.9 %reduce-scatter.14.cloned.1.call-done.own_ref = bf16[12,96,768]{2,1,0:T(8,128)(2,1)} async-done(((bf16[48,96,768]{2,1,0:T(8,128)(2,1)}), bf16[12,96,768]{2,1,0:T(8,128)(2,1)}) %reduce-scatter.14.cloned.1.call-update) | async-done | bytes 1769488 | tf_op jit(solution)/shard_map/reduce_scatter | solution.py:419
  722.0 16.7 %tile_adamw.1 = (f32[12,192,768]{2,1,0:T(8,128)}, f32[12,192,768]{2,1,0:T(8,128)}, f32[12,192,768]{2,1,0:T(8,128)}) custom-call(s32[12]{0:T(128)S(1)} %convert_element_type.551.used_ref, s32[1]{0:T(128)} %bitcast.44.core_ref, f32[12,192,768]{2,1,0:T(8,128)S(1)} %copy-done.6, f32[12,192,768]{2,1,0:T(8,128)} %m_ref.1, f32[12,192,768]{2,1,0:T(8,128)} %v_ref.1, ...), custom_call_target="tpu_custom_call" | custom-call | tf_op jit(solution)/shard_map/tile_adamw/pallas_call | solution.py:244
  (754 shorter events, 329.2 us)
Async XLA Ops:
  7.2 168.5 %all-gather.3.cloned.1.call-start = ((), (), s32[]{:S(2)}) async-start(), calls=%async_computation.6 | async-start | bytes 30081024 | tf_op jit(solution)/shard_map/all_gather | solution.py:294
  10.7 394.1 %reduce-scatter.6.cloned.1.call-start = ((), (), s32[]{:S(2)}) async-start(), calls=%async_computation.7 | async-start | bytes 3932160 | tf_op jit(solution)/shard_map/reduce_scatter | solution.py:393
  40.9 14.3 %collective-permute-start = (bf16[768,256]{1,0:T(8,128)(2,1)S(1)}, bf16[768,256]{1,0:T(8,128)(2,1)S(1)}, u32[]{:S(2)}, u32[]{:S(2)}) collective-permute-start(bf16[768,256]{1,0:T(8,128)(2,1)S(1)} %bitcast.309), channel_id=1, source_target_pairs={{0,2},{2,0},{1,3},{3,1},{4,6},{6,4},{5,7},{7,5},{8,10},{10,8},{9,1... | collective-permute-start | bytes 1179656 | tf_op jit(solution)/shard_map/ppermute | solution.py:34
  55.3 16.0 %collective-permute-start.1 = (bf16[768,512]{1,0:T(8,128)(2,1)S(1)}, bf16[768,512]{1,0:T(8,128)(2,1)}, u32[]{:S(2)}, u32[]{:S(2)}) collective-permute-start(bf16[768,512]{1,0:T(8,128)(2,1)S(1)} %pad_maximum_fusion.11), channel_id=1, source_target_pairs={{0,1},{1,0},{2,3},{3,2},{4,5},{5,4},{6,7},{7,6},{8,9},{9,8},{10,11... | collective-permute-start | bytes 2359304 | tf_op jit(solution)/shard_map/ppermute | solution.py:34
  199.0 11.2 %collective-permute-start.6 = (bf16[256,768]{1,0:T(8,128)(2,1)S(1)}, bf16[256,768]{1,0:T(8,128)(2,1)S(1)}, u32[]{:S(2)}, u32[]{:S(2)}) collective-permute-start(bf16[256,768]{1,0:T(8,128)(2,1)S(1)} %convolution_convert_fusion.15), channel_id=1, source_target_pairs={{0,1},{1,0},{2,3},{3,2},{4,5},{5,4},{6,7},{7,6},{8,9},{9,8},{10,11... | collective-permute-start | bytes 1179656 | tf_op jit(solution)/shard_map/ppermute | solution.py:34
  265.0 12.7 %collective-permute-start.12 = (bf16[256,768]{1,0:T(8,128)(2,1)}, bf16[256,768]{1,0:T(8,128)(2,1)}, u32[]{:S(2)}, u32[]{:S(2)}) collective-permute-start(bf16[256,768]{1,0:T(8,128)(2,1)} %convolution_convert_fusion.9), channel_id=1, source_target_pairs={{0,1},{1,0},{2,3},{3,2},{4,5},{5,4},{6,7},{7,6},{8,9},{9,8},{10,11... | collective-permute-start | bytes 1179656 | tf_op jit(solution)/shard_map/ppermute | solution.py:34
  300.7 11.5 %collective-permute-start.16 = (bf16[256,768]{1,0:T(8,128)(2,1)S(1)}, bf16[256,768]{1,0:T(8,128)(2,1)S(1)}, u32[]{:S(2)}, u32[]{:S(2)}) collective-permute-start(bf16[256,768]{1,0:T(8,128)(2,1)S(1)} %convolution_convert_fusion.13), channel_id=1, source_target_pairs={{0,1},{1,0},{2,3},{3,2},{4,5},{5,4},{6,7},{7,6},{8,9},{9,8},{10,11... | collective-permute-start | bytes 1179656 | tf_op jit(solution)/shard_map/ppermute | solution.py:34
  343.1 108.1 %reduce-scatter.8.cloned.1.call-start = ((), (), s32[]{:S(2)}) async-start(), calls=%async_computation.8 | async-start | bytes 3538944 | tf_op jit(solution)/shard_map/reduce_scatter | solution.py:419
  379.3 23.3 %collective-permute-start.44 = (bf16[8,2,96,768]{3,2,0,1:T(8,128)(2,1)S(1)}, bf16[8,2,96,768]{3,2,0,1:T(8,128)(2,1)S(1)}, u32[]{:S(2)}, u32[]{:S(2)}) collective-permute-start(bf16[8,2,96,768]{3,2,0,1:T(8,128)(2,1)S(1)} %copy.186), channel_id=1, source_target_pairs={{0,4},{4,0},{1,5},{5,1},{2,6},{6,2},{3,7},{7,3},{8,12},{12,8},{9,1... | collective-permute-start | bytes 7077896 | tf_op jit(solution)/shard_map/ppermute | solution.py:34
  404.8 94.3 %reduce-scatter.10.cloned.1.call-start = ((), (), s32[]{:S(2)}) async-start(), calls=%async_computation.9 | async-start | bytes 5308416 | tf_op jit(solution)/shard_map/reduce_scatter | solution.py:419
  414.1 34.3 %collective-permute-start.45 = (bf16[8,2,96,768]{3,2,0,1:T(8,128)(2,1)S(1)}, bf16[8,2,96,768]{3,2,0,1:T(8,128)(2,1)S(1)}, u32[]{:S(2)}, u32[]{:S(2)}) collective-permute-start(bf16[8,2,96,768]{3,2,0,1:T(8,128)(2,1)S(1)} %copy.185), channel_id=1, source_target_pairs={{0,4},{4,0},{1,5},{5,1},{2,6},{6,2},{3,7},{7,3},{8,12},{12,8},{9,1... | collective-permute-start | bytes 7077896 | tf_op jit(solution)/shard_map/ppermute | solution.py:34
  415.9 18.9 %collective-permute-start.46 = (bf16[4,2,96,768]{3,2,0,1:T(8,128)(2,1)S(1)}, bf16[4,2,96,768]{3,2,0,1:T(8,128)(2,1)S(1)}, u32[]{:S(2)}, u32[]{:S(2)}) collective-permute-start(bf16[4,2,96,768]{3,2,0,1:T(8,128)(2,1)S(1)} %copy.188), channel_id=1, source_target_pairs={{0,4},{4,0},{1,5},{5,1},{2,6},{6,2},{3,7},{7,3},{8,12},{12,8},{9,1... | collective-permute-start | bytes 3538952 | tf_op jit(solution)/shard_map/ppermute | solution.py:34
  433.6 13.6 %collective-permute-start.34 = (bf16[2,8,48,256]{3,2,1,0:T(8,128)(2,1)S(1)}, bf16[2,8,48,256]{3,2,1,0:T(8,128)(2,1)S(1)}, u32[]{:S(2)}, u32[]{:S(2)}) collective-permute-start(bf16[2,8,48,256]{3,2,1,0:T(8,128)(2,1)S(1)} %add_convert_fusion.11), channel_id=1, source_target_pairs={{0,2},{2,0},{1,3},{3,1},{4,6},{6,4},{5,7},{7,5},{8,10},{10,8},{9,1... | collective-permute-start | bytes 1179656 | tf_op jit(solution)/shard_map/ppermute | solution.py:34
  434.8 16.6 %collective-permute-start.32 = (bf16[2,8,48,256]{3,2,1,0:T(8,128)(2,1)}, bf16[2,8,48,256]{3,2,1,0:T(8,128)(2,1)}, u32[]{:S(2)}, u32[]{:S(2)}) collective-permute-start(bf16[2,8,48,256]{3,2,1,0:T(8,128)(2,1)} %get-tuple-element.57), channel_id=1, source_target_pairs={{0,4},{4,0},{1,5},{5,1},{2,6},{6,2},{3,7},{7,3},{8,12},{12,8},{9,1... | collective-permute-start | bytes 1179656 | tf_op jit(solution)/shard_map/ppermute | solution.py:34
  451.3 124.9 %reduce-scatter.12.cloned.1.call-start = ((), (), s32[]{:S(2)}) async-start(), calls=%async_computation.10 | async-start | bytes 5308416 | tf_op jit(solution)/shard_map/reduce_scatter | solution.py:419
  479.8 19.4 %collective-permute-start.36 = (bf16[256,768]{1,0:T(8,128)(2,1)}, bf16[256,768]{1,0:T(8,128)(2,1)S(1)}, u32[]{:S(2)}, u32[]{:S(2)}) collective-permute-start(bf16[256,768]{1,0:T(8,128)(2,1)} %convolution_convert_fusion.2), channel_id=1, source_target_pairs={{0,1},{1,0},{2,3},{3,2},{4,5},{5,4},{6,7},{7,6},{8,9},{9,8},{10,11... | collective-permute-start | bytes 1179656 | tf_op jit(solution)/shard_map/ppermute | solution.py:34
  514.4 20.2 %collective-permute-start.39 = (bf16[2,8,48,256]{3,2,1,0:T(8,128)(2,1)S(1)}, bf16[2,8,48,256]{3,2,1,0:T(8,128)(2,1)S(1)}, u32[]{:S(2)}, u32[]{:S(2)}) collective-permute-start(bf16[2,8,48,256]{3,2,1,0:T(8,128)(2,1)S(1)} %add_convert_fusion.9), channel_id=1, source_target_pairs={{0,2},{2,0},{1,3},{3,1},{4,6},{6,4},{5,7},{7,5},{8,10},{10,8},{9,1... | collective-permute-start | bytes 1179656 | tf_op jit(solution)/shard_map/ppermute | solution.py:34
  515.6 32.0 %collective-permute-start.43 = (f32[2,768]{1,0:T(2,128)S(1)}, f32[2,768]{1,0:T(2,128)S(1)}, u32[]{:S(2)}, u32[]{:S(2)}) collective-permute-start(f32[2,768]{1,0:T(2,128)S(1)} %pad_maximum_fusion.28), channel_id=1, source_target_pairs={{0,1},{1,0},{2,3},{3,2},{4,5},{5,4},{6,7},{7,6},{8,9},{9,8},{10,11... | collective-permute-start | bytes 18440 | tf_op jit(solution)/shard_map/ppermute | solution.py:34
  540.2 17.2 %collective-permute-start.40 = (bf16[4,2,96,768]{3,2,0,1:T(8,128)(2,1)}, bf16[4,2,96,768]{3,2,0,1:T(8,128)(2,1)}, u32[]{:S(2)}, u32[]{:S(2)}) collective-permute-start(bf16[4,2,96,768]{3,2,0,1:T(8,128)(2,1)} %copy.189), channel_id=1, source_target_pairs={{0,4},{4,0},{1,5},{5,1},{2,6},{6,2},{3,7},{7,3},{8,12},{12,8},{9,1... | collective-permute-start | bytes 3538952 | tf_op jit(solution)/shard_map/ppermute | solution.py:34
  552.8 18.6 %all-to-all-start = ((bf16[4,272,192]{2,1,0:T(8,128)(2,1)}), bf16[4,272,192]{2,1,0:T(8,128)(2,1)}, u32[]{:S(2)}, u32[]{:S(2)}) async-start(bf16[4,272,192]{2,1,0:T(8,128)(2,1)} %bitcast.208), calls=%async_computation | async-start | bytes 1114112 | tf_op jit(solution)/shard_map/all_to_all | solution.py:466
  557.4 156.1 %reduce-scatter.14.cloned.1.call-start = ((), (), s32[]{:S(2)}) async-start(), calls=%async_computation.11 | async-start | bytes 8847360 | tf_op jit(solution)/shard_map/reduce_scatter | solution.py:419
  560.9 13.8 %collective-permute-start.41 = (bf16[4,96,768]{2,1,0:T(8,128)(2,1)}, bf16[4,96,768]{2,1,0:T(8,128)(2,1)}, u32[]{:S(2)}, u32[]{:S(2)}) collective-permute-start(bf16[4,96,768]{2,1,0:T(8,128)(2,1)} %dynamic-slice_bitcast_fusion), channel_id=1, source_target_pairs={{0,2},{2,0},{1,3},{3,1},{4,6},{6,4},{5,7},{7,5},{8,10},{10,8},{9,1... | collective-permute-start | bytes 1769480 | tf_op jit(solution)/shard_map/ppermute | solution.py:34
  590.8 34.6 %collective-permute-start.49 = (bf16[4,1,272,192]{3,2,1,0:T(8,128)(2,1)}, bf16[4,1,272,192]{3,2,1,0:T(8,128)(2,1)S(1)}, u32[]{:S(2)}, u32[]{:S(2)}) collective-permute-start(bf16[4,1,272,192]{3,2,1,0:T(8,128)(2,1)} %bitcast.69), channel_id=1, source_target_pairs={{0,2},{2,0},{1,3},{3,1},{4,6},{6,4},{5,7},{7,5},{8,10},{10,8},{9,1... | collective-permute-start | bytes 1253384 | tf_op jit(solution)/shard_map/ppermute | solution.py:34
  592.6 13.6 %collective-permute-start.21 = (f32[1,2048]{1,0:T(1,128)S(1)}, f32[1,2048]{1,0:T(1,128)S(1)}, u32[]{:S(2)}, u32[]{:S(2)}) collective-permute-start(f32[1,2048]{1,0:T(1,128)S(1)} %fusion.239), channel_id=1, source_target_pairs={{0,2},{2,0},{1,3},{3,1},{4,6},{6,4},{5,7},{7,5},{8,10},{10,8},{9,1... | collective-permute-start | bytes 24584 | tf_op jit(solution)/shard_map/ppermute | solution.py:34
  (225 other events, 1995.1 us)
Sparse Core Ops, SparseCore 0:
  10.8 164.8 all-gather.2
  343.3 59.9 reduce-scatter.5
  405.5 37.0 reduce-scatter.7
  451.4 47.6 reduce-scatter.9
  501.8 56.0 reduce-scatter.11
  589.5 124.0 reduce-scatter.13

commit v4 on v3

--- a/solution.py
+++ b/solution.py
@@ -130,17 +130,17 @@
 
 def collect(sources, owner, slot, n, slots, into=None):
     total, (half, model) = owner.shape[0], sources[0].shape[1:]
-    scalar, anywhere = pl.BlockSpec(memory_space=pltpu.SMEM), pl.BlockSpec(memory_space=pl.ANY)
+    scalar = pl.BlockSpec(memory_space=pltpu.SMEM)
     whole = pl.BlockSpec(memory_space=pltpu.VMEM)
     held = [] if into is None else [into]
     return pl.pallas_call(
         functools.partial(collect_kernel, len(sources)),
-        in_specs=[scalar] * 2 + [whole] * len(sources) + [anywhere] * len(held),
-        out_specs=anywhere,
+        in_specs=[scalar] * 2 + [whole] * len(sources) + [pl.BlockSpec(memory_space=pltpu.MemorySpace.HBM)] * len(held),
+        out_specs=pl.BlockSpec(memory_space=pltpu.MemorySpace.HBM),
         out_shape=jax.ShapeDtypeStruct((n, slots, half, model), bf16),
         input_output_aliases={2 + len(sources): 0} if held else {},
         scratch_shapes=[pltpu.SemaphoreType.DMA((total,))],
-        compiler_params=pltpu.CompilerParams(vmem_limit_bytes=24 * 2**20),
+        compiler_params=pltpu.CompilerParams(vmem_limit_bytes=58 * 2**20),
         name="collect",
     )(owner, slot, *sources, *held)
 
@@ -250,7 +250,7 @@
             out_specs=[block, block, block],
         ),
         out_shape=[jax.ShapeDtypeStruct(state[0].shape, f32)] * 3,
-        compiler_params=pltpu.CompilerParams(vmem_limit_bytes=40 * 2**20),
+        compiler_params=pltpu.CompilerParams(vmem_limit_bytes=58 * 2**20),
         name="tile_adamw",
     )(used, core, *state, own, oth)
 
@@ -416,7 +416,8 @@
         return add_halves(keep, over("ty", send))
 
     def offloaded_sum(flat, axis):
-        offloaded.append(lax.psum_scatter(after(flat, offloaded[-1]), axis, scatter_dimension=0, tiled=True))
+        flat = after(flat, offloaded[0]) if len(offloaded) == 1 else flat
+        offloaded.append(lax.psum_scatter(flat, axis, scatter_dimension=0, tiled=True))
         return offloaded[-1]
 
     attn_two = None

time: 754 us -> 740 us (0.981)
  local copies, waits for them, and re-layouts: 61.3 us -> 50.7 us
    reduce_scatter x4, waiting for transfers between devices: 64.1 us -> 51.1 us  [offloaded_sum(): lax.psum_scatter(flat, axis, scatter_dimension=0, tiled=True)]
    unnamed x372 -> x360, local copies, waits for them, and re-layouts: 32.5 us -> 22.7 us
    ppermute x56, waiting for transfers between devices: 204 us -> 212 us  [over(): return lax.ppermute(v, axis, FLIP)]
  transfers between devices with their start and end apart: 65 -> 65, of which waited for: 41 -> 42; matrix products, arithmetic and copies ran while one was open for 16% -> 16% of each run, Pallas kernels for 5% -> 5%
where the time goes in v4:
time: 740 us; the launch traced here: 734 us
  waiting for transfers between devices  372 us (50%)
  Pallas kernels  84.7 us (11%)
  matrix products  64.4 us (9%)
  other arithmetic  62.7 us (8%)
  local copies, waits for them, and re-layouts  50.7 us (7%)
  starting transfers between devices  46.4 us (6%)
  blocking collectives  26.8 us (4%)
  between operations  26 us (4%)
    ppermute x56, waiting for transfers between devices, over(): return lax.ppermute(v, axis, FLIP)  212 us
    all_gather x1, waiting for transfers between devices, body(): lax.all_gather(held, ('fsdp', 'ctx', 'ty'), axis=0, tiled=True)  93.3 us
    dot_general x44, matrix products, dot(): lax.dot_general(left, right, (dims, ((), ())), preferred_element_type=f32)  64.4 us
    reduce_scatter x4, waiting for transfers between devices, offloaded_sum(): lax.psum_scatter(flat, axis, scatter_dimension=0, tiled=True)  51.1 us
    ppermute x56, starting transfers between devices, over(): return lax.ppermute(v, axis, FLIP)  36.1 us
    pallas_call x3, Pallas kernels, attend_back(): pl.pallas_call(functools.partial(attend_back_kernel, len(blocks)), grid=(...  27 us
    all_gather x1, blocking collectives, body(): tables = lax.all_gather(packed, 'fsdp', axis=0)  26.8 us
    unnamed x360, local copies, waits for them, and re-layouts  22.7 us
  transfers between devices with their start and end apart: 65, of which 42 were waited for; matrix products, arithmetic and copies ran while one was open for 16% of the time, Pallas kernels for 5%

profile of v4, /device:TPU:0, one launch (start us, length us, event | category | flops | bytes accessed | tf_op | source)
XLA Modules:
  0.0 734.2 jit_solution(12904849093915314262)
XLA Ops:
  13.3 26.8 %all-gather = bf16[832,512]{1,0:T(8,128)(2,1)S(1)} all-gather(bf16[208,512]{1,0:T(8,128)(2,1)S(1)} %fusion.111), channel_id=2, replica_groups=mesh['fsdp'=4,'ctx'=2,'ty'=2,'tx'=2] {'fsdp'}, dimensions={0}, use_global_device_ids=true | all-gather | bytes 1064960 | tf_op jit(solution)/shard_map/all_gather | solution.py:319
  42.5 12.7 %collective-permute-done = bf16[768,256]{1,0:T(8,128)(2,1)S(1)} collective-permute-done((bf16[768,256]{1,0:T(8,128)(2,1)S(1)}, bf16[768,256]{1,0:T(8,128)(2,1)S(1)}, u32[]{:S(2)}, u32[]{:S(2)}) %collective-permute-start) | collective-permute-done | bytes 393248 | tf_op jit(solution)/shard_map/ppermute | solution.py:34
  56.7 14.6 %collective-permute-done.1 = bf16[768,512]{1,0:T(8,128)(2,1)} collective-permute-done((bf16[768,512]{1,0:T(8,128)(2,1)S(1)}, bf16[768,512]{1,0:T(8,128)(2,1)}, u32[]{:S(2)}, u32[]{:S(2)}) %collective-permute-start.1) | collective-permute-done | bytes 786464 | tf_op jit(solution)/shard_map/ppermute | solution.py:34
  82.4 93.3 %all-gather.3.cloned.1.call-done = bf16[192,96,768]{2,1,0:T(8,128)(2,1)} async-done(((bf16[12,96,768]{2,1,0:T(8,128)(2,1)}), bf16[192,96,768]{2,1,0:T(8,128)(2,1)}) %all-gather.3.cloned.1.call-update) | async-done | bytes 28311568 | tf_op jit(solution)/shard_map/all_gather | solution.py:294
  181.2 9.6 %collective-permute-done.3 = bf16[768,256]{1,0:T(8,128)(2,1)S(1)} collective-permute-done((bf16[768,256]{1,0:T(8,128)(2,1)S(1)}, bf16[768,256]{1,0:T(8,128)(2,1)S(1)}, u32[]{:S(2)}, u32[]{:S(2)}) %collective-permute-start.3) | collective-permute-done | bytes 393248 | tf_op jit(solution)/shard_map/ppermute | solution.py:34
  200.9 9.3 %collective-permute-done.6 = bf16[256,768]{1,0:T(8,128)(2,1)S(1)} collective-permute-done((bf16[256,768]{1,0:T(8,128)(2,1)S(1)}, bf16[256,768]{1,0:T(8,128)(2,1)S(1)}, u32[]{:S(2)}, u32[]{:S(2)}) %collective-permute-start.6) | collective-permute-done | bytes 393248 | tf_op jit(solution)/shard_map/ppermute | solution.py:34
  229.9 8.4 %collective-permute-done.8 = bf16[768,256]{1,0:T(8,128)(2,1)S(1)} collective-permute-done((bf16[768,256]{1,0:T(8,128)(2,1)S(1)}, bf16[768,256]{1,0:T(8,128)(2,1)S(1)}, u32[]{:S(2)}, u32[]{:S(2)}) %collective-permute-start.8) | collective-permute-done | bytes 393248 | tf_op jit(solution)/shard_map/ppermute | solution.py:34
  248.0 9.3 %collective-permute-done.11 = bf16[256,768]{1,0:T(8,128)(2,1)S(1)} collective-permute-done((bf16[256,768]{1,0:T(8,128)(2,1)S(1)}, bf16[256,768]{1,0:T(8,128)(2,1)S(1)}, u32[]{:S(2)}, u32[]{:S(2)}) %collective-permute-start.11) | collective-permute-done | bytes 393248 | tf_op jit(solution)/shard_map/ppermute | solution.py:34
  293.5 6.7 attend.5
  303.7 8.5 %collective-permute-done.16 = bf16[256,768]{1,0:T(8,128)(2,1)S(1)} collective-permute-done((bf16[256,768]{1,0:T(8,128)(2,1)S(1)}, bf16[256,768]{1,0:T(8,128)(2,1)S(1)}, u32[]{:S(2)}, u32[]{:S(2)}) %collective-permute-start.16) | collective-permute-done | bytes 393248 | tf_op jit(solution)/shard_map/ppermute | solution.py:34
  322.0 8.8 %collective-permute-done.17 = bf16[256,768]{1,0:T(8,128)(2,1)} collective-permute-done((bf16[256,768]{1,0:T(8,128)(2,1)}, bf16[256,768]{1,0:T(8,128)(2,1)}, u32[]{:S(2)}, u32[]{:S(2)}) %collective-permute-start.17) | collective-permute-done | bytes 393248 | tf_op jit(solution)/shard_map/ppermute | solution.py:34
  365.3 9.4 %attend_back.3 = (bf16[8,48,256]{2,1,0:T(8,128)(2,1)S(1)}, bf16[2,8,48,256]{3,2,1,0:T(8,128)(2,1)S(1)}, bf16[2,8,48,256]{3,2,1,0:T(8,128)(2,1)S(1)}, bf16[2,8,48...) custom-call(bf16[8,48,256]{2,1,0:T(8,128)(2,1)S(1)} %bitcast.224, bf16[8,48,256]{2,1,0:T(8,128)(2,1)S(1)} %bitcast.257, ...), custom_call_target="tpu_custom_call" | custom-call | tf_op jit(solution)/shard_map/attend_back/pallas_call | solution.py:202
  380.6 8.1 %collective-permute-done.29 = bf16[2,8,48,256]{3,2,1,0:T(8,128)(2,1)S(1)} collective-permute-done((bf16[2,8,48,256]{3,2,1,0:T(8,128)(2,1)S(1)}, bf16[2,8,48,256]{3,2,1,0:T(8,128)(2,1)S(1)}, u32[]{:S(2)}, u32[]{:S(2)}) %collective-permute-start.29) | collective-permute-done | bytes 393248 | tf_op jit(solution)/shard_map/ppermute | solution.py:34
  422.7 9.1 %attend_back.4 = (bf16[8,48,256]{2,1,0:T(8,128)(2,1)S(1)}, bf16[2,8,48,256]{3,2,1,0:T(8,128)(2,1)S(1)}, bf16[2,8,48,256]{3,2,1,0:T(8,128)(2,1)S(1)}, bf16[2,8,48...) custom-call(bf16[8,48,256]{2,1,0:T(8,128)(2,1)S(1)} %bitcast.222, bf16[8,48,256]{2,1,0:T(8,128)(2,1)S(1)} %bitcast.258, ...), custom_call_target="tpu_custom_call" | custom-call | tf_op jit(solution)/shard_map/attend_back/pallas_call | solution.py:202
  435.1 12.2 %collective-permute-done.34 = bf16[2,8,48,256]{3,2,1,0:T(8,128)(2,1)S(1)} collective-permute-done((bf16[2,8,48,256]{3,2,1,0:T(8,128)(2,1)S(1)}, bf16[2,8,48,256]{3,2,1,0:T(8,128)(2,1)S(1)}, u32[]{:S(2)}, u32[]{:S(2)}) %collective-permute-start.34) | collective-permute-done | bytes 393248 | tf_op jit(solution)/shard_map/ppermute | solution.py:34
  455.9 9.4 %collective-permute-done.35 = bf16[256,768]{1,0:T(8,128)(2,1)S(1)} collective-permute-done((bf16[256,768]{1,0:T(8,128)(2,1)S(1)}, bf16[256,768]{1,0:T(8,128)(2,1)S(1)}, u32[]{:S(2)}, u32[]{:S(2)}) %collective-permute-start.35) | collective-permute-done | bytes 393248 | tf_op jit(solution)/shard_map/ppermute | solution.py:34
  495.4 8.5 %attend_back.5 = (bf16[8,48,256]{2,1,0:T(8,128)(2,1)S(1)}, bf16[2,8,48,256]{3,2,1,0:T(8,128)(2,1)S(1)}, bf16[2,8,48,256]{3,2,1,0:T(8,128)(2,1)S(1)}, bf16[2,8,48...) custom-call(bf16[8,48,256]{2,1,0:T(8,128)(2,1)S(1)} %bitcast.220, bf16[8,48,256]{2,1,0:T(8,128)(2,1)S(1)} %bitcast.259, ...), custom_call_target="tpu_custom_call" | custom-call | tf_op jit(solution)/shard_map/attend_back/pallas_call | solution.py:202
  509.3 15.8 %collective-permute-done.39 = bf16[2,8,48,256]{3,2,1,0:T(8,128)(2,1)S(1)} collective-permute-done((bf16[2,8,48,256]{3,2,1,0:T(8,128)(2,1)S(1)}, bf16[2,8,48,256]{3,2,1,0:T(8,128)(2,1)S(1)}, u32[]{:S(2)}, u32[]{:S(2)}) %collective-permute-start.39) | collective-permute-done | bytes 393248 | tf_op jit(solution)/shard_map/ppermute | solution.py:34
  551.8 6.9 all-to-all-done
  559.9 7.7 %collective-permute-done.41 = bf16[4,96,768]{2,1,0:T(8,128)(2,1)S(1)} collective-permute-done((bf16[4,96,768]{2,1,0:T(8,128)(2,1)S(1)}, bf16[4,96,768]{2,1,0:T(8,128)(2,1)S(1)}, u32[]{:S(2)}, u32[]{:S(2)}) %collective-permute-start.41) | collective-permute-done | bytes 589856 | tf_op jit(solution)/shard_map/ppermute | solution.py:34
  579.6 12.4 %collective-permute-done.21 = f32[1,2048]{1,0:T(1,128)S(1)} collective-permute-done((f32[1,2048]{1,0:T(1,128)S(1)}, f32[1,2048]{1,0:T(1,128)S(1)}, u32[]{:S(2)}, u32[]{:S(2)}) %collective-permute-start.21) | collective-permute-done | bytes 8224 | tf_op jit(solution)/shard_map/ppermute | solution.py:34
  630.9 8.2 %fusion = f32[192,2048]{1,0:T(8,128)} fusion(bf16[4096,192]{1,0:T(8,128)(2,1)S(1)} %bitcast.310, s32[4096]{0:T(1024)S(1)} %add_select_fusion), kind=kOutput, calls=%fused_computation.3 | convolution fusion | flops 3229614080 | bytes 3162112 | tf_op jit(solution)/shard_map/dot_general | solution.py:38
  648.3 51.1 %reduce-scatter.14.cloned.1.call-done.own_ref = bf16[12,96,768]{2,1,0:T(8,128)(2,1)} async-done(((bf16[48,96,768]{2,1,0:T(8,128)(2,1)}), bf16[12,96,768]{2,1,0:T(8,128)(2,1)}) %reduce-scatter.14.cloned.1.call-update) | async-done | bytes 1769488 | tf_op jit(solution)/shard_map/reduce_scatter | solution.py:420
  704.5 21.5 %tile_adamw.1 = (f32[12,192,768]{2,1,0:T(8,128)}, f32[12,192,768]{2,1,0:T(8,128)}, f32[12,192,768]{2,1,0:T(8,128)}) custom-call(s32[12]{0:T(128)} %convert_element_type.551.used_ref, s32[1]{0:T(128)} %bitcast.44.core_ref, f32[12,192,768]{2,1,0:T(8,128)} %w_ref.1, f32[12,192,768]{2,1,0:T(8,128)} %m_ref.1, f32[12,192,768]{2,1,0:T(8,128)} %v_ref.1, ...), custom_call_target="tpu_custom_call" | custom-call | tf_op jit(solution)/shard_map/tile_adamw/pallas_call | solution.py:244
  (742 shorter events, 320.2 us)
Async XLA Ops:
  7.2 168.5 %all-gather.3.cloned.1.call-start = ((), (), s32[]{:S(2)}) async-start(), calls=%async_computation.6 | async-start | bytes 30081024 | tf_op jit(solution)/shard_map/all_gather | solution.py:294
  10.7 394.1 %reduce-scatter.6.cloned.1.call-start = ((), (), s32[]{:S(2)}) async-start(), calls=%async_computation.7 | async-start | bytes 3932160 | tf_op jit(solution)/shard_map/reduce_scatter | solution.py:393
  40.9 14.3 %collective-permute-start = (bf16[768,256]{1,0:T(8,128)(2,1)S(1)}, bf16[768,256]{1,0:T(8,128)(2,1)S(1)}, u32[]{:S(2)}, u32[]{:S(2)}) collective-permute-start(bf16[768,256]{1,0:T(8,128)(2,1)S(1)} %bitcast.311), channel_id=1, source_target_pairs={{0,2},{2,0},{1,3},{3,1},{4,6},{6,4},{5,7},{7,5},{8,10},{10,8},{9,1... | collective-permute-start | bytes 1179656 | tf_op jit(solution)/shard_map/ppermute | solution.py:34
  55.4 16.0 %collective-permute-start.1 = (bf16[768,512]{1,0:T(8,128)(2,1)S(1)}, bf16[768,512]{1,0:T(8,128)(2,1)}, u32[]{:S(2)}, u32[]{:S(2)}) collective-permute-start(bf16[768,512]{1,0:T(8,128)(2,1)S(1)} %pad_maximum_fusion.11), channel_id=1, source_target_pairs={{0,1},{1,0},{2,3},{3,2},{4,5},{5,4},{6,7},{7,6},{8,9},{9,8},{10,11... | collective-permute-start | bytes 2359304 | tf_op jit(solution)/shard_map/ppermute | solution.py:34
  199.0 11.2 %collective-permute-start.6 = (bf16[256,768]{1,0:T(8,128)(2,1)S(1)}, bf16[256,768]{1,0:T(8,128)(2,1)S(1)}, u32[]{:S(2)}, u32[]{:S(2)}) collective-permute-start(bf16[256,768]{1,0:T(8,128)(2,1)S(1)} %convolution_convert_fusion.15), channel_id=1, source_target_pairs={{0,1},{1,0},{2,3},{3,2},{4,5},{5,4},{6,7},{7,6},{8,9},{9,8},{10,11... | collective-permute-start | bytes 1179656 | tf_op jit(solution)/shard_map/ppermute | solution.py:34
  265.0 12.7 %collective-permute-start.12 = (bf16[256,768]{1,0:T(8,128)(2,1)}, bf16[256,768]{1,0:T(8,128)(2,1)}, u32[]{:S(2)}, u32[]{:S(2)}) collective-permute-start(bf16[256,768]{1,0:T(8,128)(2,1)} %convolution_convert_fusion.9), channel_id=1, source_target_pairs={{0,1},{1,0},{2,3},{3,2},{4,5},{5,4},{6,7},{7,6},{8,9},{9,8},{10,11... | collective-permute-start | bytes 1179656 | tf_op jit(solution)/shard_map/ppermute | solution.py:34
  300.7 11.5 %collective-permute-start.16 = (bf16[256,768]{1,0:T(8,128)(2,1)S(1)}, bf16[256,768]{1,0:T(8,128)(2,1)S(1)}, u32[]{:S(2)}, u32[]{:S(2)}) collective-permute-start(bf16[256,768]{1,0:T(8,128)(2,1)S(1)} %convolution_convert_fusion.13), channel_id=1, source_target_pairs={{0,1},{1,0},{2,3},{3,2},{4,5},{5,4},{6,7},{7,6},{8,9},{9,8},{10,11... | collective-permute-start | bytes 1179656 | tf_op jit(solution)/shard_map/ppermute | solution.py:34
  343.2 225.4 %reduce-scatter.8.cloned.1.call-start = ((), (), s32[]{:S(2)}) async-start(), calls=%async_computation.8 | async-start | bytes 3538944 | tf_op jit(solution)/shard_map/reduce_scatter | solution.py:420
  379.3 23.3 %collective-permute-start.44 = (bf16[8,2,96,768]{3,2,0,1:T(8,128)(2,1)S(1)}, bf16[8,2,96,768]{3,2,0,1:T(8,128)(2,1)S(1)}, u32[]{:S(2)}, u32[]{:S(2)}) collective-permute-start(bf16[8,2,96,768]{3,2,0,1:T(8,128)(2,1)S(1)} %copy.186), channel_id=1, source_target_pairs={{0,4},{4,0},{1,5},{5,1},{2,6},{6,2},{3,7},{7,3},{8,12},{12,8},{9,1... | collective-permute-start | bytes 7077896 | tf_op jit(solution)/shard_map/ppermute | solution.py:34
  404.8 163.7 %reduce-scatter.10.cloned.1.call-start = ((), (), s32[]{:S(2)}) async-start(), calls=%async_computation.9 | async-start | bytes 5308416 | tf_op jit(solution)/shard_map/reduce_scatter | solution.py:420
  414.1 34.3 %collective-permute-start.45 = (bf16[8,2,96,768]{3,2,0,1:T(8,128)(2,1)S(1)}, bf16[8,2,96,768]{3,2,0,1:T(8,128)(2,1)S(1)}, u32[]{:S(2)}, u32[]{:S(2)}) collective-permute-start(bf16[8,2,96,768]{3,2,0,1:T(8,128)(2,1)S(1)} %copy.185), channel_id=1, source_target_pairs={{0,4},{4,0},{1,5},{5,1},{2,6},{6,2},{3,7},{7,3},{8,12},{12,8},{9,1... | collective-permute-start | bytes 7077896 | tf_op jit(solution)/shard_map/ppermute | solution.py:34
  415.9 18.9 %collective-permute-start.46 = (bf16[4,2,96,768]{3,2,0,1:T(8,128)(2,1)S(1)}, bf16[4,2,96,768]{3,2,0,1:T(8,128)(2,1)S(1)}, u32[]{:S(2)}, u32[]{:S(2)}) collective-permute-start(bf16[4,2,96,768]{3,2,0,1:T(8,128)(2,1)S(1)} %copy.188), channel_id=1, source_target_pairs={{0,4},{4,0},{1,5},{5,1},{2,6},{6,2},{3,7},{7,3},{8,12},{12,8},{9,1... | collective-permute-start | bytes 3538952 | tf_op jit(solution)/shard_map/ppermute | solution.py:34
  433.6 13.6 %collective-permute-start.34 = (bf16[2,8,48,256]{3,2,1,0:T(8,128)(2,1)S(1)}, bf16[2,8,48,256]{3,2,1,0:T(8,128)(2,1)S(1)}, u32[]{:S(2)}, u32[]{:S(2)}) collective-permute-start(bf16[2,8,48,256]{3,2,1,0:T(8,128)(2,1)S(1)} %add_convert_fusion.11), channel_id=1, source_target_pairs={{0,2},{2,0},{1,3},{3,1},{4,6},{6,4},{5,7},{7,5},{8,10},{10,8},{9,1... | collective-permute-start | bytes 1179656 | tf_op jit(solution)/shard_map/ppermute | solution.py:34
  434.8 16.6 %collective-permute-start.32 = (bf16[2,8,48,256]{3,2,1,0:T(8,128)(2,1)}, bf16[2,8,48,256]{3,2,1,0:T(8,128)(2,1)}, u32[]{:S(2)}, u32[]{:S(2)}) collective-permute-start(bf16[2,8,48,256]{3,2,1,0:T(8,128)(2,1)} %get-tuple-element.54), channel_id=1, source_target_pairs={{0,4},{4,0},{1,5},{5,1},{2,6},{6,2},{3,7},{7,3},{8,12},{12,8},{9,1... | collective-permute-start | bytes 1179656 | tf_op jit(solution)/shard_map/ppermute | solution.py:34
  451.3 117.3 %reduce-scatter.12.cloned.1.call-start = ((), (), s32[]{:S(2)}) async-start(), calls=%async_computation.10 | async-start | bytes 5308416 | tf_op jit(solution)/shard_map/reduce_scatter | solution.py:420
  479.8 11.3 %collective-permute-start.36 = (bf16[256,768]{1,0:T(8,128)(2,1)}, bf16[256,768]{1,0:T(8,128)(2,1)S(1)}, u32[]{:S(2)}, u32[]{:S(2)}) collective-permute-start(bf16[256,768]{1,0:T(8,128)(2,1)} %convolution_convert_fusion.2), channel_id=1, source_target_pairs={{0,1},{1,0},{2,3},{3,2},{4,5},{5,4},{6,7},{7,6},{8,9},{9,8},{10,11... | collective-permute-start | bytes 1179656 | tf_op jit(solution)/shard_map/ppermute | solution.py:34
  505.8 19.3 %collective-permute-start.39 = (bf16[2,8,48,256]{3,2,1,0:T(8,128)(2,1)S(1)}, bf16[2,8,48,256]{3,2,1,0:T(8,128)(2,1)S(1)}, u32[]{:S(2)}, u32[]{:S(2)}) collective-permute-start(bf16[2,8,48,256]{3,2,1,0:T(8,128)(2,1)S(1)} %add_convert_fusion.9), channel_id=1, source_target_pairs={{0,2},{2,0},{1,3},{3,1},{4,6},{6,4},{5,7},{7,5},{8,10},{10,8},{9,1... | collective-permute-start | bytes 1179656 | tf_op jit(solution)/shard_map/ppermute | solution.py:34
  507.0 29.5 %collective-permute-start.43 = (f32[2,768]{1,0:T(2,128)S(1)}, f32[2,768]{1,0:T(2,128)S(1)}, u32[]{:S(2)}, u32[]{:S(2)}) collective-permute-start(f32[2,768]{1,0:T(2,128)S(1)} %pad_maximum_fusion.28), channel_id=1, source_target_pairs={{0,1},{1,0},{2,3},{3,2},{4,5},{5,4},{6,7},{7,6},{8,9},{9,8},{10,11... | collective-permute-start | bytes 18440 | tf_op jit(solution)/shard_map/ppermute | solution.py:34
  530.7 15.8 %collective-permute-start.40 = (bf16[4,2,96,768]{3,2,0,1:T(8,128)(2,1)}, bf16[4,2,96,768]{3,2,0,1:T(8,128)(2,1)}, u32[]{:S(2)}, u32[]{:S(2)}) collective-permute-start(bf16[4,2,96,768]{3,2,0,1:T(8,128)(2,1)} %copy.189), channel_id=1, source_target_pairs={{0,4},{4,0},{1,5},{5,1},{2,6},{6,2},{3,7},{7,3},{8,12},{12,8},{9,1... | collective-permute-start | bytes 3538952 | tf_op jit(solution)/shard_map/ppermute | solution.py:34
  541.8 16.9 %all-to-all-start = ((bf16[4,272,192]{2,1,0:T(8,128)(2,1)}), bf16[4,272,192]{2,1,0:T(8,128)(2,1)S(1)}, u32[]{:S(2)}, u32[]{:S(2)}) async-start(bf16[4,272,192]{2,1,0:T(8,128)(2,1)} %bitcast.208), calls=%async_computation | async-start | bytes 1114112 | tf_op jit(solution)/shard_map/all_to_all | solution.py:467
  546.4 153.1 %reduce-scatter.14.cloned.1.call-start = ((), (), s32[]{:S(2)}) async-start(), calls=%async_computation.11 | async-start | bytes 8847360 | tf_op jit(solution)/shard_map/reduce_scatter | solution.py:420
  548.3 19.3 %collective-permute-start.41 = (bf16[4,96,768]{2,1,0:T(8,128)(2,1)S(1)}, bf16[4,96,768]{2,1,0:T(8,128)(2,1)S(1)}, u32[]{:S(2)}, u32[]{:S(2)}) collective-permute-start(bf16[4,96,768]{2,1,0:T(8,128)(2,1)S(1)} %dynamic-slice_bitcast_fusion), channel_id=1, source_target_pairs={{0,2},{2,0},{1,3},{3,1},{4,6},{6,4},{5,7},{7,5},{8,10},{10,8},{9,1... | collective-permute-start | bytes 1769480 | tf_op jit(solution)/shard_map/ppermute | solution.py:34
  576.8 34.4 %collective-permute-start.49 = (bf16[4,1,272,192]{3,2,1,0:T(8,128)(2,1)S(1)}, bf16[4,1,272,192]{3,2,1,0:T(8,128)(2,1)S(1)}, u32[]{:S(2)}, u32[]{:S(2)}) collective-permute-start(bf16[4,1,272,192]{3,2,1,0:T(8,128)(2,1)S(1)} %bitcast.309), channel_id=1, source_target_pairs={{0,2},{2,0},{1,3},{3,1},{4,6},{6,4},{5,7},{7,5},{8,10},{10,8},{9,1... | collective-permute-start | bytes 1253384 | tf_op jit(solution)/shard_map/ppermute | solution.py:34
  578.6 13.4 %collective-permute-start.21 = (f32[1,2048]{1,0:T(1,128)S(1)}, f32[1,2048]{1,0:T(1,128)S(1)}, u32[]{:S(2)}, u32[]{:S(2)}) collective-permute-start(f32[1,2048]{1,0:T(1,128)S(1)} %fusion.239), channel_id=1, source_target_pairs={{0,2},{2,0},{1,3},{3,1},{4,6},{6,4},{5,7},{7,5},{8,10},{10,8},{9,1... | collective-permute-start | bytes 24584 | tf_op jit(solution)/shard_map/ppermute | solution.py:34
  (219 other events, 1963.3 us)
Sparse Core Ops, SparseCore 0:
  10.8 164.8 all-gather.2
  343.3 59.9 reduce-scatter.5
  405.5 37.0 reduce-scatter.7
  451.4 47.6 reduce-scatter.9
  501.8 60.8 reduce-scatter.11
  575.5 123.8 reduce-scatter.13

commit v5 on v4

--- a/solution.py
+++ b/solution.py
@@ -214,8 +214,8 @@
 def adamw_update(weight, moment_one, moment_two, gradient, rate):
     moment_one = beta_first * moment_one + (1.0 - beta_first) * gradient
     moment_two = beta_second * moment_two + (1.0 - beta_second) * gradient * gradient
-    first_hat = moment_one / (1.0 - beta_first**STEP)
-    second_hat = moment_two / (1.0 - beta_second**STEP)
+    first_hat = moment_one * (1.0 / (1.0 - beta_first**STEP))
+    second_hat = moment_two * (1.0 / (1.0 - beta_second**STEP))
     weight = weight - rate * (first_hat / (jnp.sqrt(second_hat) + adam_eps) + weight_decay * weight)
     return (weight, moment_one, moment_two)
 

time: 740 us -> 740 us (level)
  no operation moved by 1% of the time
where the time goes in v5:
time: 740 us; the launch traced here: 734 us
  waiting for transfers between devices  372 us (50%)
  Pallas kernels  84.1 us (11%)
  matrix products  64.4 us (9%)
  other arithmetic  62.7 us (8%)
  local copies, waits for them, and re-layouts  50.7 us (7%)
  starting transfers between devices  46.4 us (6%)
  blocking collectives  26.8 us (4%)
  between operations  26 us (4%)
    ppermute x56, waiting for transfers between devices, over(): return lax.ppermute(v, axis, FLIP)  212 us
    all_gather x1, waiting for transfers between devices, body(): lax.all_gather(held, ('fsdp', 'ctx', 'ty'), axis=0, tiled=True)  93.3 us
    dot_general x44, matrix products, dot(): lax.dot_general(left, right, (dims, ((), ())), preferred_element_type=f32)  64.4 us
    reduce_scatter x4, waiting for transfers between devices, offloaded_sum(): lax.psum_scatter(flat, axis, scatter_dimension=0, tiled=True)  51.1 us
    ppermute x56, starting transfers between devices, over(): return lax.ppermute(v, axis, FLIP)  36.1 us
    pallas_call x3, Pallas kernels, attend_back(): pl.pallas_call(functools.partial(attend_back_kernel, len(blocks)), grid=(...  27 us
    all_gather x1, blocking collectives, body(): tables = lax.all_gather(packed, 'fsdp', axis=0)  26.8 us
    unnamed x360, local copies, waits for them, and re-layouts  22.7 us
  transfers between devices with their start and end apart: 65, of which 42 were waited for; matrix products, arithmetic and copies ran while one was open for 16% of the time, Pallas kernels for 5%

profile of v5, /device:TPU:0, one launch (start us, length us, event | category | flops | bytes accessed | tf_op | source)
XLA Modules:
  0.0 733.6 jit_solution(12904849093915314262)
XLA Ops:
  13.3 26.8 %all-gather = bf16[832,512]{1,0:T(8,128)(2,1)S(1)} all-gather(bf16[208,512]{1,0:T(8,128)(2,1)S(1)} %fusion.111), channel_id=2, replica_groups=mesh['fsdp'=4,'ctx'=2,'ty'=2,'tx'=2] {'fsdp'}, dimensions={0}, use_global_device_ids=true | all-gather | bytes 1064960 | tf_op jit(solution)/shard_map/all_gather | solution.py:319
  42.5 12.7 %collective-permute-done = bf16[768,256]{1,0:T(8,128)(2,1)S(1)} collective-permute-done((bf16[768,256]{1,0:T(8,128)(2,1)S(1)}, bf16[768,256]{1,0:T(8,128)(2,1)S(1)}, u32[]{:S(2)}, u32[]{:S(2)}) %collective-permute-start) | collective-permute-done | bytes 393248 | tf_op jit(solution)/shard_map/ppermute | solution.py:34
  56.7 14.6 %collective-permute-done.1 = bf16[768,512]{1,0:T(8,128)(2,1)} collective-permute-done((bf16[768,512]{1,0:T(8,128)(2,1)S(1)}, bf16[768,512]{1,0:T(8,128)(2,1)}, u32[]{:S(2)}, u32[]{:S(2)}) %collective-permute-start.1) | collective-permute-done | bytes 786464 | tf_op jit(solution)/shard_map/ppermute | solution.py:34
  82.4 93.3 %all-gather.3.cloned.1.call-done = bf16[192,96,768]{2,1,0:T(8,128)(2,1)} async-done(((bf16[12,96,768]{2,1,0:T(8,128)(2,1)}), bf16[192,96,768]{2,1,0:T(8,128)(2,1)}) %all-gather.3.cloned.1.call-update) | async-done | bytes 28311568 | tf_op jit(solution)/shard_map/all_gather | solution.py:294
  181.2 9.6 %collective-permute-done.3 = bf16[768,256]{1,0:T(8,128)(2,1)S(1)} collective-permute-done((bf16[768,256]{1,0:T(8,128)(2,1)S(1)}, bf16[768,256]{1,0:T(8,128)(2,1)S(1)}, u32[]{:S(2)}, u32[]{:S(2)}) %collective-permute-start.3) | collective-permute-done | bytes 393248 | tf_op jit(solution)/shard_map/ppermute | solution.py:34
  200.9 9.3 %collective-permute-done.6 = bf16[256,768]{1,0:T(8,128)(2,1)S(1)} collective-permute-done((bf16[256,768]{1,0:T(8,128)(2,1)S(1)}, bf16[256,768]{1,0:T(8,128)(2,1)S(1)}, u32[]{:S(2)}, u32[]{:S(2)}) %collective-permute-start.6) | collective-permute-done | bytes 393248 | tf_op jit(solution)/shard_map/ppermute | solution.py:34
  229.9 8.4 %collective-permute-done.8 = bf16[768,256]{1,0:T(8,128)(2,1)S(1)} collective-permute-done((bf16[768,256]{1,0:T(8,128)(2,1)S(1)}, bf16[768,256]{1,0:T(8,128)(2,1)S(1)}, u32[]{:S(2)}, u32[]{:S(2)}) %collective-permute-start.8) | collective-permute-done | bytes 393248 | tf_op jit(solution)/shard_map/ppermute | solution.py:34
  248.0 9.3 %collective-permute-done.11 = bf16[256,768]{1,0:T(8,128)(2,1)S(1)} collective-permute-done((bf16[256,768]{1,0:T(8,128)(2,1)S(1)}, bf16[256,768]{1,0:T(8,128)(2,1)S(1)}, u32[]{:S(2)}, u32[]{:S(2)}) %collective-permute-start.11) | collective-permute-done | bytes 393248 | tf_op jit(solution)/shard_map/ppermute | solution.py:34
  293.5 6.7 attend.5
  303.7 8.5 %collective-permute-done.16 = bf16[256,768]{1,0:T(8,128)(2,1)S(1)} collective-permute-done((bf16[256,768]{1,0:T(8,128)(2,1)S(1)}, bf16[256,768]{1,0:T(8,128)(2,1)S(1)}, u32[]{:S(2)}, u32[]{:S(2)}) %collective-permute-start.16) | collective-permute-done | bytes 393248 | tf_op jit(solution)/shard_map/ppermute | solution.py:34
  322.0 8.8 %collective-permute-done.17 = bf16[256,768]{1,0:T(8,128)(2,1)} collective-permute-done((bf16[256,768]{1,0:T(8,128)(2,1)}, bf16[256,768]{1,0:T(8,128)(2,1)}, u32[]{:S(2)}, u32[]{:S(2)}) %collective-permute-start.17) | collective-permute-done | bytes 393248 | tf_op jit(solution)/shard_map/ppermute | solution.py:34
  365.3 9.4 %attend_back.3 = (bf16[8,48,256]{2,1,0:T(8,128)(2,1)S(1)}, bf16[2,8,48,256]{3,2,1,0:T(8,128)(2,1)S(1)}, bf16[2,8,48,256]{3,2,1,0:T(8,128)(2,1)S(1)}, bf16[2,8,48...) custom-call(bf16[8,48,256]{2,1,0:T(8,128)(2,1)S(1)} %bitcast.224, bf16[8,48,256]{2,1,0:T(8,128)(2,1)S(1)} %bitcast.257, ...), custom_call_target="tpu_custom_call" | custom-call | tf_op jit(solution)/shard_map/attend_back/pallas_call | solution.py:202
  380.6 8.1 %collective-permute-done.29 = bf16[2,8,48,256]{3,2,1,0:T(8,128)(2,1)S(1)} collective-permute-done((bf16[2,8,48,256]{3,2,1,0:T(8,128)(2,1)S(1)}, bf16[2,8,48,256]{3,2,1,0:T(8,128)(2,1)S(1)}, u32[]{:S(2)}, u32[]{:S(2)}) %collective-permute-start.29) | collective-permute-done | bytes 393248 | tf_op jit(solution)/shard_map/ppermute | solution.py:34
  422.7 9.1 %attend_back.4 = (bf16[8,48,256]{2,1,0:T(8,128)(2,1)S(1)}, bf16[2,8,48,256]{3,2,1,0:T(8,128)(2,1)S(1)}, bf16[2,8,48,256]{3,2,1,0:T(8,128)(2,1)S(1)}, bf16[2,8,48...) custom-call(bf16[8,48,256]{2,1,0:T(8,128)(2,1)S(1)} %bitcast.222, bf16[8,48,256]{2,1,0:T(8,128)(2,1)S(1)} %bitcast.258, ...), custom_call_target="tpu_custom_call" | custom-call | tf_op jit(solution)/shard_map/attend_back/pallas_call | solution.py:202
  435.1 12.2 %collective-permute-done.34 = bf16[2,8,48,256]{3,2,1,0:T(8,128)(2,1)S(1)} collective-permute-done((bf16[2,8,48,256]{3,2,1,0:T(8,128)(2,1)S(1)}, bf16[2,8,48,256]{3,2,1,0:T(8,128)(2,1)S(1)}, u32[]{:S(2)}, u32[]{:S(2)}) %collective-permute-start.34) | collective-permute-done | bytes 393248 | tf_op jit(solution)/shard_map/ppermute | solution.py:34
  455.9 9.4 %collective-permute-done.35 = bf16[256,768]{1,0:T(8,128)(2,1)S(1)} collective-permute-done((bf16[256,768]{1,0:T(8,128)(2,1)S(1)}, bf16[256,768]{1,0:T(8,128)(2,1)S(1)}, u32[]{:S(2)}, u32[]{:S(2)}) %collective-permute-start.35) | collective-permute-done | bytes 393248 | tf_op jit(solution)/shard_map/ppermute | solution.py:34
  495.4 8.5 %attend_back.5 = (bf16[8,48,256]{2,1,0:T(8,128)(2,1)S(1)}, bf16[2,8,48,256]{3,2,1,0:T(8,128)(2,1)S(1)}, bf16[2,8,48,256]{3,2,1,0:T(8,128)(2,1)S(1)}, bf16[2,8,48...) custom-call(bf16[8,48,256]{2,1,0:T(8,128)(2,1)S(1)} %bitcast.220, bf16[8,48,256]{2,1,0:T(8,128)(2,1)S(1)} %bitcast.259, ...), custom_call_target="tpu_custom_call" | custom-call | tf_op jit(solution)/shard_map/attend_back/pallas_call | solution.py:202
  509.3 15.8 %collective-permute-done.39 = bf16[2,8,48,256]{3,2,1,0:T(8,128)(2,1)S(1)} collective-permute-done((bf16[2,8,48,256]{3,2,1,0:T(8,128)(2,1)S(1)}, bf16[2,8,48,256]{3,2,1,0:T(8,128)(2,1)S(1)}, u32[]{:S(2)}, u32[]{:S(2)}) %collective-permute-start.39) | collective-permute-done | bytes 393248 | tf_op jit(solution)/shard_map/ppermute | solution.py:34
  551.8 6.9 all-to-all-done
  559.9 7.7 %collective-permute-done.41 = bf16[4,96,768]{2,1,0:T(8,128)(2,1)S(1)} collective-permute-done((bf16[4,96,768]{2,1,0:T(8,128)(2,1)S(1)}, bf16[4,96,768]{2,1,0:T(8,128)(2,1)S(1)}, u32[]{:S(2)}, u32[]{:S(2)}) %collective-permute-start.41) | collective-permute-done | bytes 589856 | tf_op jit(solution)/shard_map/ppermute | solution.py:34
  579.6 12.4 %collective-permute-done.21 = f32[1,2048]{1,0:T(1,128)S(1)} collective-permute-done((f32[1,2048]{1,0:T(1,128)S(1)}, f32[1,2048]{1,0:T(1,128)S(1)}, u32[]{:S(2)}, u32[]{:S(2)}) %collective-permute-start.21) | collective-permute-done | bytes 8224 | tf_op jit(solution)/shard_map/ppermute | solution.py:34
  630.9 8.2 %fusion = f32[192,2048]{1,0:T(8,128)} fusion(bf16[4096,192]{1,0:T(8,128)(2,1)S(1)} %bitcast.310, s32[4096]{0:T(1024)S(1)} %add_select_fusion), kind=kOutput, calls=%fused_computation.3 | convolution fusion | flops 3229614080 | bytes 3162112 | tf_op jit(solution)/shard_map/dot_general | solution.py:38
  648.3 51.1 %reduce-scatter.14.cloned.1.call-done.own_ref = bf16[12,96,768]{2,1,0:T(8,128)(2,1)} async-done(((bf16[48,96,768]{2,1,0:T(8,128)(2,1)}), bf16[12,96,768]{2,1,0:T(8,128)(2,1)}) %reduce-scatter.14.cloned.1.call-update) | async-done | bytes 1769488 | tf_op jit(solution)/shard_map/reduce_scatter | solution.py:420
  704.5 20.9 %tile_adamw.1 = (f32[12,192,768]{2,1,0:T(8,128)}, f32[12,192,768]{2,1,0:T(8,128)}, f32[12,192,768]{2,1,0:T(8,128)}) custom-call(s32[12]{0:T(128)} %convert_element_type.551.used_ref, s32[1]{0:T(128)} %bitcast.44.core_ref, f32[12,192,768]{2,1,0:T(8,128)} %w_ref.1, f32[12,192,768]{2,1,0:T(8,128)} %m_ref.1, f32[12,192,768]{2,1,0:T(8,128)} %v_ref.1, ...), custom_call_target="tpu_custom_call" | custom-call | tf_op jit(solution)/shard_map/tile_adamw/pallas_call | solution.py:244
  (742 shorter events, 320.2 us)
Async XLA Ops:
  7.2 168.5 %all-gather.3.cloned.1.call-start = ((), (), s32[]{:S(2)}) async-start(), calls=%async_computation.6 | async-start | bytes 30081024 | tf_op jit(solution)/shard_map/all_gather | solution.py:294
  10.7 394.1 %reduce-scatter.6.cloned.1.call-start = ((), (), s32[]{:S(2)}) async-start(), calls=%async_computation.7 | async-start | bytes 3932160 | tf_op jit(solution)/shard_map/reduce_scatter | solution.py:393
  40.9 14.3 %collective-permute-start = (bf16[768,256]{1,0:T(8,128)(2,1)S(1)}, bf16[768,256]{1,0:T(8,128)(2,1)S(1)}, u32[]{:S(2)}, u32[]{:S(2)}) collective-permute-start(bf16[768,256]{1,0:T(8,128)(2,1)S(1)} %bitcast.311), channel_id=1, source_target_pairs={{0,2},{2,0},{1,3},{3,1},{4,6},{6,4},{5,7},{7,5},{8,10},{10,8},{9,1... | collective-permute-start | bytes 1179656 | tf_op jit(solution)/shard_map/ppermute | solution.py:34
  55.4 16.0 %collective-permute-start.1 = (bf16[768,512]{1,0:T(8,128)(2,1)S(1)}, bf16[768,512]{1,0:T(8,128)(2,1)}, u32[]{:S(2)}, u32[]{:S(2)}) collective-permute-start(bf16[768,512]{1,0:T(8,128)(2,1)S(1)} %pad_maximum_fusion.11), channel_id=1, source_target_pairs={{0,1},{1,0},{2,3},{3,2},{4,5},{5,4},{6,7},{7,6},{8,9},{9,8},{10,11... | collective-permute-start | bytes 2359304 | tf_op jit(solution)/shard_map/ppermute | solution.py:34
  199.0 11.2 %collective-permute-start.6 = (bf16[256,768]{1,0:T(8,128)(2,1)S(1)}, bf16[256,768]{1,0:T(8,128)(2,1)S(1)}, u32[]{:S(2)}, u32[]{:S(2)}) collective-permute-start(bf16[256,768]{1,0:T(8,128)(2,1)S(1)} %convolution_convert_fusion.15), channel_id=1, source_target_pairs={{0,1},{1,0},{2,3},{3,2},{4,5},{5,4},{6,7},{7,6},{8,9},{9,8},{10,11... | collective-permute-start | bytes 1179656 | tf_op jit(solution)/shard_map/ppermute | solution.py:34
  265.0 12.7 %collective-permute-start.12 = (bf16[256,768]{1,0:T(8,128)(2,1)}, bf16[256,768]{1,0:T(8,128)(2,1)}, u32[]{:S(2)}, u32[]{:S(2)}) collective-permute-start(bf16[256,768]{1,0:T(8,128)(2,1)} %convolution_convert_fusion.9), channel_id=1, source_target_pairs={{0,1},{1,0},{2,3},{3,2},{4,5},{5,4},{6,7},{7,6},{8,9},{9,8},{10,11... | collective-permute-start | bytes 1179656 | tf_op jit(solution)/shard_map/ppermute | solution.py:34
  300.7 11.5 %collective-permute-start.16 = (bf16[256,768]{1,0:T(8,128)(2,1)S(1)}, bf16[256,768]{1,0:T(8,128)(2,1)S(1)}, u32[]{:S(2)}, u32[]{:S(2)}) collective-permute-start(bf16[256,768]{1,0:T(8,128)(2,1)S(1)} %convolution_convert_fusion.13), channel_id=1, source_target_pairs={{0,1},{1,0},{2,3},{3,2},{4,5},{5,4},{6,7},{7,6},{8,9},{9,8},{10,11... | collective-permute-start | bytes 1179656 | tf_op jit(solution)/shard_map/ppermute | solution.py:34
  343.2 225.4 %reduce-scatter.8.cloned.1.call-start = ((), (), s32[]{:S(2)}) async-start(), calls=%async_computation.8 | async-start | bytes 3538944 | tf_op jit(solution)/shard_map/reduce_scatter | solution.py:420
  379.3 23.3 %collective-permute-start.44 = (bf16[8,2,96,768]{3,2,0,1:T(8,128)(2,1)S(1)}, bf16[8,2,96,768]{3,2,0,1:T(8,128)(2,1)S(1)}, u32[]{:S(2)}, u32[]{:S(2)}) collective-permute-start(bf16[8,2,96,768]{3,2,0,1:T(8,128)(2,1)S(1)} %copy.186), channel_id=1, source_target_pairs={{0,4},{4,0},{1,5},{5,1},{2,6},{6,2},{3,7},{7,3},{8,12},{12,8},{9,1... | collective-permute-start | bytes 7077896 | tf_op jit(solution)/shard_map/ppermute | solution.py:34
  404.8 163.7 %reduce-scatter.10.cloned.1.call-start = ((), (), s32[]{:S(2)}) async-start(), calls=%async_computation.9 | async-start | bytes 5308416 | tf_op jit(solution)/shard_map/reduce_scatter | solution.py:420
  414.1 34.3 %collective-permute-start.45 = (bf16[8,2,96,768]{3,2,0,1:T(8,128)(2,1)S(1)}, bf16[8,2,96,768]{3,2,0,1:T(8,128)(2,1)S(1)}, u32[]{:S(2)}, u32[]{:S(2)}) collective-permute-start(bf16[8,2,96,768]{3,2,0,1:T(8,128)(2,1)S(1)} %copy.185), channel_id=1, source_target_pairs={{0,4},{4,0},{1,5},{5,1},{2,6},{6,2},{3,7},{7,3},{8,12},{12,8},{9,1... | collective-permute-start | bytes 7077896 | tf_op jit(solution)/shard_map/ppermute | solution.py:34
  415.9 18.9 %collective-permute-start.46 = (bf16[4,2,96,768]{3,2,0,1:T(8,128)(2,1)S(1)}, bf16[4,2,96,768]{3,2,0,1:T(8,128)(2,1)S(1)}, u32[]{:S(2)}, u32[]{:S(2)}) collective-permute-start(bf16[4,2,96,768]{3,2,0,1:T(8,128)(2,1)S(1)} %copy.188), channel_id=1, source_target_pairs={{0,4},{4,0},{1,5},{5,1},{2,6},{6,2},{3,7},{7,3},{8,12},{12,8},{9,1... | collective-permute-start | bytes 3538952 | tf_op jit(solution)/shard_map/ppermute | solution.py:34
  433.6 13.6 %collective-permute-start.34 = (bf16[2,8,48,256]{3,2,1,0:T(8,128)(2,1)S(1)}, bf16[2,8,48,256]{3,2,1,0:T(8,128)(2,1)S(1)}, u32[]{:S(2)}, u32[]{:S(2)}) collective-permute-start(bf16[2,8,48,256]{3,2,1,0:T(8,128)(2,1)S(1)} %add_convert_fusion.11), channel_id=1, source_target_pairs={{0,2},{2,0},{1,3},{3,1},{4,6},{6,4},{5,7},{7,5},{8,10},{10,8},{9,1... | collective-permute-start | bytes 1179656 | tf_op jit(solution)/shard_map/ppermute | solution.py:34
  434.8 16.6 %collective-permute-start.32 = (bf16[2,8,48,256]{3,2,1,0:T(8,128)(2,1)}, bf16[2,8,48,256]{3,2,1,0:T(8,128)(2,1)}, u32[]{:S(2)}, u32[]{:S(2)}) collective-permute-start(bf16[2,8,48,256]{3,2,1,0:T(8,128)(2,1)} %get-tuple-element.54), channel_id=1, source_target_pairs={{0,4},{4,0},{1,5},{5,1},{2,6},{6,2},{3,7},{7,3},{8,12},{12,8},{9,1... | collective-permute-start | bytes 1179656 | tf_op jit(solution)/shard_map/ppermute | solution.py:34
  451.3 117.3 %reduce-scatter.12.cloned.1.call-start = ((), (), s32[]{:S(2)}) async-start(), calls=%async_computation.10 | async-start | bytes 5308416 | tf_op jit(solution)/shard_map/reduce_scatter | solution.py:420
  479.8 11.3 %collective-permute-start.36 = (bf16[256,768]{1,0:T(8,128)(2,1)}, bf16[256,768]{1,0:T(8,128)(2,1)S(1)}, u32[]{:S(2)}, u32[]{:S(2)}) collective-permute-start(bf16[256,768]{1,0:T(8,128)(2,1)} %convolution_convert_fusion.2), channel_id=1, source_target_pairs={{0,1},{1,0},{2,3},{3,2},{4,5},{5,4},{6,7},{7,6},{8,9},{9,8},{10,11... | collective-permute-start | bytes 1179656 | tf_op jit(solution)/shard_map/ppermute | solution.py:34
  505.8 19.3 %collective-permute-start.39 = (bf16[2,8,48,256]{3,2,1,0:T(8,128)(2,1)S(1)}, bf16[2,8,48,256]{3,2,1,0:T(8,128)(2,1)S(1)}, u32[]{:S(2)}, u32[]{:S(2)}) collective-permute-start(bf16[2,8,48,256]{3,2,1,0:T(8,128)(2,1)S(1)} %add_convert_fusion.9), channel_id=1, source_target_pairs={{0,2},{2,0},{1,3},{3,1},{4,6},{6,4},{5,7},{7,5},{8,10},{10,8},{9,1... | collective-permute-start | bytes 1179656 | tf_op jit(solution)/shard_map/ppermute | solution.py:34
  507.0 29.5 %collective-permute-start.43 = (f32[2,768]{1,0:T(2,128)S(1)}, f32[2,768]{1,0:T(2,128)S(1)}, u32[]{:S(2)}, u32[]{:S(2)}) collective-permute-start(f32[2,768]{1,0:T(2,128)S(1)} %pad_maximum_fusion.28), channel_id=1, source_target_pairs={{0,1},{1,0},{2,3},{3,2},{4,5},{5,4},{6,7},{7,6},{8,9},{9,8},{10,11... | collective-permute-start | bytes 18440 | tf_op jit(solution)/shard_map/ppermute | solution.py:34
  530.7 15.8 %collective-permute-start.40 = (bf16[4,2,96,768]{3,2,0,1:T(8,128)(2,1)}, bf16[4,2,96,768]{3,2,0,1:T(8,128)(2,1)}, u32[]{:S(2)}, u32[]{:S(2)}) collective-permute-start(bf16[4,2,96,768]{3,2,0,1:T(8,128)(2,1)} %copy.189), channel_id=1, source_target_pairs={{0,4},{4,0},{1,5},{5,1},{2,6},{6,2},{3,7},{7,3},{8,12},{12,8},{9,1... | collective-permute-start | bytes 3538952 | tf_op jit(solution)/shard_map/ppermute | solution.py:34
  541.8 16.9 %all-to-all-start = ((bf16[4,272,192]{2,1,0:T(8,128)(2,1)}), bf16[4,272,192]{2,1,0:T(8,128)(2,1)S(1)}, u32[]{:S(2)}, u32[]{:S(2)}) async-start(bf16[4,272,192]{2,1,0:T(8,128)(2,1)} %bitcast.208), calls=%async_computation | async-start | bytes 1114112 | tf_op jit(solution)/shard_map/all_to_all | solution.py:467
  546.4 153.1 %reduce-scatter.14.cloned.1.call-start = ((), (), s32[]{:S(2)}) async-start(), calls=%async_computation.11 | async-start | bytes 8847360 | tf_op jit(solution)/shard_map/reduce_scatter | solution.py:420
  548.3 19.3 %collective-permute-start.41 = (bf16[4,96,768]{2,1,0:T(8,128)(2,1)S(1)}, bf16[4,96,768]{2,1,0:T(8,128)(2,1)S(1)}, u32[]{:S(2)}, u32[]{:S(2)}) collective-permute-start(bf16[4,96,768]{2,1,0:T(8,128)(2,1)S(1)} %dynamic-slice_bitcast_fusion), channel_id=1, source_target_pairs={{0,2},{2,0},{1,3},{3,1},{4,6},{6,4},{5,7},{7,5},{8,10},{10,8},{9,1... | collective-permute-start | bytes 1769480 | tf_op jit(solution)/shard_map/ppermute | solution.py:34
  576.8 34.4 %collective-permute-start.49 = (bf16[4,1,272,192]{3,2,1,0:T(8,128)(2,1)S(1)}, bf16[4,1,272,192]{3,2,1,0:T(8,128)(2,1)S(1)}, u32[]{:S(2)}, u32[]{:S(2)}) collective-permute-start(bf16[4,1,272,192]{3,2,1,0:T(8,128)(2,1)S(1)} %bitcast.309), channel_id=1, source_target_pairs={{0,2},{2,0},{1,3},{3,1},{4,6},{6,4},{5,7},{7,5},{8,10},{10,8},{9,1... | collective-permute-start | bytes 1253384 | tf_op jit(solution)/shard_map/ppermute | solution.py:34
  578.6 13.4 %collective-permute-start.21 = (f32[1,2048]{1,0:T(1,128)S(1)}, f32[1,2048]{1,0:T(1,128)S(1)}, u32[]{:S(2)}, u32[]{:S(2)}) collective-permute-start(f32[1,2048]{1,0:T(1,128)S(1)} %fusion.239), channel_id=1, source_target_pairs={{0,2},{2,0},{1,3},{3,1},{4,6},{6,4},{5,7},{7,5},{8,10},{10,8},{9,1... | collective-permute-start | bytes 24584 | tf_op jit(solution)/shard_map/ppermute | solution.py:34
  (219 other events, 1963.3 us)
Sparse Core Ops, SparseCore 0:
  10.8 164.8 all-gather.2
  343.3 59.9 reduce-scatter.5
  405.5 37.0 reduce-scatter.7
  451.4 47.6 reduce-scatter.9
  501.8 60.8 reduce-scatter.11
  575.5 123.8 reduce-scatter.13

commit v6 on v5

--- a/solution.py
+++ b/solution.py
@@ -293,9 +293,9 @@
     held = lax.dynamic_slice(tile_master, (0, core * half, 0), (slots, half, model)).astype(bf16)
     held = lax.all_gather(held, ("fsdp", "ctx", "ty"), axis=0, tiled=True).reshape(n, 4, slots, half, model)
 
-    block_at = (core * 2 + tx) * 2 + ty
+    block_at, block = core * 2 + tx, 2 * BLOCK
     vocab_pad = 8 * BLOCK - VOCAB
-    wide = BLOCK + rows
+    wide = block + rows
     embed_pad = jnp.pad(embedding.astype(bf16), ((0, 0), (0, vocab_pad)))
     ids_half = jnp.where(masked == 1, VOCAB - 1, token_ids)
     ids = lax.dynamic_slice(ids_half, (0, ty * rows), (1, rows))
@@ -303,7 +303,7 @@
     coded = jnp.concatenate([coded // 256, coded % 256], 1).astype(bf16)
     packed = jnp.concatenate(
         [
-            lax.dynamic_slice(embed_pad, (0, block_at * BLOCK), (own_dim, BLOCK)),
+            lax.dynamic_slice(embed_pad, (0, block_at * block), (own_dim, block)),
             lax.dynamic_slice(position_table, (0, piece_at * rows), (own_dim, rows)).astype(bf16),
         ],
         1,
@@ -317,10 +317,10 @@
         0,
     )
     tables = lax.all_gather(packed, "fsdp", axis=0)
-    embed_all = tables[:, :own_dim, :BLOCK].reshape(model, BLOCK)
-    for axis, at in (("ty", ty), ("tx", tx), ("ctx", core)):
+    embed_all = tables[:, :own_dim, :block].reshape(model, block)
+    for axis, at in (("tx", tx), ("ctx", core)):
         embed_all = both(axis, embed_all, at, 1)
-    places_own = tables[:, :own_dim, BLOCK:].reshape(model, rows).T.astype(f32)
+    places_own = tables[:, :own_dim, block:].reshape(model, rows).T.astype(f32)
     gains = tables[:, own_dim:own_dim + 2 * norms, :own_dim].transpose(1, 0, 2)
     gains = gains.reshape(2, norms, model).astype(f32)
     coded = tables[:, own_dim + 2 * norms, :2 * rows].reshape(n, 1, 2, rows)

time: 740 us -> 766 us (1.035)
  waiting for transfers between devices: 372 us -> 423 us
  blocking collectives: 26.8 us -> 0 us
    all_gather x0 -> x1, waiting for transfers between devices: none -> 31.4 us  [body(): tables = lax.all_gather(packed, 'fsdp', axis=0)]
    all_gather x1, waiting for transfers between devices: 93.3 us -> 122 us  [body(): lax.all_gather(held, ('fsdp', 'ctx', 'ty'), axis=0, tiled=True)]
    all_gather x1 -> x0, blocking collectives: 26.8 us -> none  [body(): tables = lax.all_gather(packed, 'fsdp', axis=0)]
    ppermute x56 -> x55, waiting for transfers between devices: 212 us -> 202 us  [over(): return lax.ppermute(v, axis, FLIP)]
    ppermute x56 -> x55, starting transfers between devices: 36.1 us -> 35 us  [over(): return lax.ppermute(v, axis, FLIP)]
    unnamed x360 -> x350, local copies, waits for them, and re-layouts: 22.7 us -> 21.6 us
  transfers between devices with their start and end apart: 65 -> 65, of which waited for: 42 -> 41; matrix products, arithmetic and copies ran while one was open for 16% -> 16% of each run, Pallas kernels for 5% -> 5%
where the time goes in v6:
time: 766 us; the launch traced here: 759 us
  waiting for transfers between devices  423 us (55%)
  Pallas kernels  83.6 us (11%)
  other arithmetic  66.9 us (9%)
  matrix products  64.1 us (8%)
  local copies, waits for them, and re-layouts  50.9 us (7%)
  starting transfers between devices  45.4 us (6%)
  between operations  25.9 us (3%)
    ppermute x55, waiting for transfers between devices, over(): return lax.ppermute(v, axis, FLIP)  202 us
    all_gather x1, waiting for transfers between devices, body(): lax.all_gather(held, ('fsdp', 'ctx', 'ty'), axis=0, tiled=True)  122 us
    dot_general x44, matrix products, dot(): lax.dot_general(left, right, (dims, ((), ())), preferred_element_type=f32)  64.1 us
    reduce_scatter x4, waiting for transfers between devices, offloaded_sum(): lax.psum_scatter(flat, axis, scatter_dimension=0, tiled=True)  51.1 us
    ppermute x55, starting transfers between devices, over(): return lax.ppermute(v, axis, FLIP)  35 us
    all_gather x1, waiting for transfers between devices, body(): tables = lax.all_gather(packed, 'fsdp', axis=0)  31.4 us
    pallas_call x3, Pallas kernels, attend_back(): pl.pallas_call(functools.partial(attend_back_kernel, len(blocks)), grid=(...  27 us
    unnamed x350, local copies, waits for them, and re-layouts  21.6 us
  transfers between devices with their start and end apart: 65, of which 41 were waited for; matrix products, arithmetic and copies ran while one was open for 16% of the time, Pallas kernels for 5%

profile of v6, /device:TPU:0, one launch (start us, length us, event | category | flops | bytes accessed | tf_op | source)
XLA Modules:
  0.0 759.3 jit_solution(17625978216221440008)
XLA Ops:
  16.8 31.4 %all-gather.6.cloned.1.call-done = bf16[832,768]{1,0:T(8,128)(2,1)} async-done(((bf16[208,768]{1,0:T(8,128)(2,1)}), bf16[832,768]{1,0:T(8,128)(2,1)}) %all-gather.6.cloned.1.call-update) | async-done | bytes 1277968 | tf_op jit(solution)/shard_map/all_gather | solution.py:319
  51.0 17.2 %collective-permute-done = bf16[768,512]{1,0:T(8,128)(2,1)S(1)} collective-permute-done((bf16[768,512]{1,0:T(8,128)(2,1)S(1)}, bf16[768,512]{1,0:T(8,128)(2,1)S(1)}, u32[]{:S(2)}, u32[]{:S(2)}) %collective-permute-start) | collective-permute-done | bytes 786464 | tf_op jit(solution)/shard_map/ppermute | solution.py:34
  78.8 122.3 %all-gather.4.cloned.1.call-done = bf16[192,96,768]{2,1,0:T(8,128)(2,1)} async-done(((bf16[12,96,768]{2,1,0:T(8,128)(2,1)}), bf16[192,96,768]{2,1,0:T(8,128)(2,1)}) %all-gather.4.cloned.1.call-update) | async-done | bytes 28311568 | tf_op jit(solution)/shard_map/all_gather | solution.py:294
  206.8 9.8 %collective-permute-done.2 = bf16[768,256]{1,0:T(8,128)(2,1)S(1)} collective-permute-done((bf16[768,256]{1,0:T(8,128)(2,1)S(1)}, bf16[768,256]{1,0:T(8,128)(2,1)S(1)}, u32[]{:S(2)}, u32[]{:S(2)}) %collective-permute-start.2) | collective-permute-done | bytes 393248 | tf_op jit(solution)/shard_map/ppermute | solution.py:34
  226.8 9.3 %collective-permute-done.5 = bf16[256,768]{1,0:T(8,128)(2,1)S(1)} collective-permute-done((bf16[256,768]{1,0:T(8,128)(2,1)S(1)}, bf16[256,768]{1,0:T(8,128)(2,1)S(1)}, u32[]{:S(2)}, u32[]{:S(2)}) %collective-permute-start.5) | collective-permute-done | bytes 393248 | tf_op jit(solution)/shard_map/ppermute | solution.py:34
  255.6 8.5 %collective-permute-done.7 = bf16[768,256]{1,0:T(8,128)(2,1)S(1)} collective-permute-done((bf16[768,256]{1,0:T(8,128)(2,1)S(1)}, bf16[768,256]{1,0:T(8,128)(2,1)S(1)}, u32[]{:S(2)}, u32[]{:S(2)}) %collective-permute-start.7) | collective-permute-done | bytes 393248 | tf_op jit(solution)/shard_map/ppermute | solution.py:34
  273.8 9.3 %collective-permute-done.10 = bf16[256,768]{1,0:T(8,128)(2,1)S(1)} collective-permute-done((bf16[256,768]{1,0:T(8,128)(2,1)S(1)}, bf16[256,768]{1,0:T(8,128)(2,1)S(1)}, u32[]{:S(2)}, u32[]{:S(2)}) %collective-permute-start.10) | collective-permute-done | bytes 393248 | tf_op jit(solution)/shard_map/ppermute | solution.py:34
  319.4 6.7 attend.5
  329.5 8.5 %collective-permute-done.15 = bf16[256,768]{1,0:T(8,128)(2,1)S(1)} collective-permute-done((bf16[256,768]{1,0:T(8,128)(2,1)S(1)}, bf16[256,768]{1,0:T(8,128)(2,1)S(1)}, u32[]{:S(2)}, u32[]{:S(2)}) %collective-permute-start.15) | collective-permute-done | bytes 393248 | tf_op jit(solution)/shard_map/ppermute | solution.py:34
  348.0 8.7 %collective-permute-done.16 = bf16[256,768]{1,0:T(8,128)(2,1)} collective-permute-done((bf16[256,768]{1,0:T(8,128)(2,1)}, bf16[256,768]{1,0:T(8,128)(2,1)}, u32[]{:S(2)}, u32[]{:S(2)}) %collective-permute-start.16) | collective-permute-done | bytes 393248 | tf_op jit(solution)/shard_map/ppermute | solution.py:34
  380.2 6.5 collective-permute-done.25
  391.2 9.4 %attend_back.3 = (bf16[8,48,256]{2,1,0:T(8,128)(2,1)S(1)}, bf16[2,8,48,256]{3,2,1,0:T(8,128)(2,1)S(1)}, bf16[2,8,48,256]{3,2,1,0:T(8,128)(2,1)S(1)}, bf16[2,8,48...) custom-call(bf16[8,48,256]{2,1,0:T(8,128)(2,1)S(1)} %bitcast.224, bf16[8,48,256]{2,1,0:T(8,128)(2,1)S(1)} %bitcast.257, ...), custom_call_target="tpu_custom_call" | custom-call | tf_op jit(solution)/shard_map/attend_back/pallas_call | solution.py:202
  406.4 8.2 %collective-permute-done.28 = bf16[2,8,48,256]{3,2,1,0:T(8,128)(2,1)S(1)} collective-permute-done((bf16[2,8,48,256]{3,2,1,0:T(8,128)(2,1)S(1)}, bf16[2,8,48,256]{3,2,1,0:T(8,128)(2,1)S(1)}, u32[]{:S(2)}, u32[]{:S(2)}) %collective-permute-start.28) | collective-permute-done | bytes 393248 | tf_op jit(solution)/shard_map/ppermute | solution.py:34
  448.6 9.1 %attend_back.4 = (bf16[8,48,256]{2,1,0:T(8,128)(2,1)S(1)}, bf16[2,8,48,256]{3,2,1,0:T(8,128)(2,1)S(1)}, bf16[2,8,48,256]{3,2,1,0:T(8,128)(2,1)S(1)}, bf16[2,8,48...) custom-call(bf16[8,48,256]{2,1,0:T(8,128)(2,1)S(1)} %bitcast.222, bf16[8,48,256]{2,1,0:T(8,128)(2,1)S(1)} %bitcast.258, ...), custom_call_target="tpu_custom_call" | custom-call | tf_op jit(solution)/shard_map/attend_back/pallas_call | solution.py:202
  461.4 12.0 %collective-permute-done.33 = bf16[2,8,48,256]{3,2,1,0:T(8,128)(2,1)S(1)} collective-permute-done((bf16[2,8,48,256]{3,2,1,0:T(8,128)(2,1)S(1)}, bf16[2,8,48,256]{3,2,1,0:T(8,128)(2,1)S(1)}, u32[]{:S(2)}, u32[]{:S(2)}) %collective-permute-start.33) | collective-permute-done | bytes 393248 | tf_op jit(solution)/shard_map/ppermute | solution.py:34
  482.0 9.4 %collective-permute-done.34 = bf16[256,768]{1,0:T(8,128)(2,1)S(1)} collective-permute-done((bf16[256,768]{1,0:T(8,128)(2,1)S(1)}, bf16[256,768]{1,0:T(8,128)(2,1)S(1)}, u32[]{:S(2)}, u32[]{:S(2)}) %collective-permute-start.34) | collective-permute-done | bytes 393248 | tf_op jit(solution)/shard_map/ppermute | solution.py:34
  521.6 8.5 %attend_back.5 = (bf16[8,48,256]{2,1,0:T(8,128)(2,1)S(1)}, bf16[2,8,48,256]{3,2,1,0:T(8,128)(2,1)S(1)}, bf16[2,8,48,256]{3,2,1,0:T(8,128)(2,1)S(1)}, bf16[2,8,48...) custom-call(bf16[8,48,256]{2,1,0:T(8,128)(2,1)S(1)} %bitcast.220, bf16[8,48,256]{2,1,0:T(8,128)(2,1)S(1)} %bitcast.259, ...), custom_call_target="tpu_custom_call" | custom-call | tf_op jit(solution)/shard_map/attend_back/pallas_call | solution.py:202
  535.5 15.7 %collective-permute-done.38 = bf16[2,8,48,256]{3,2,1,0:T(8,128)(2,1)S(1)} collective-permute-done((bf16[2,8,48,256]{3,2,1,0:T(8,128)(2,1)S(1)}, bf16[2,8,48,256]{3,2,1,0:T(8,128)(2,1)S(1)}, u32[]{:S(2)}, u32[]{:S(2)}) %collective-permute-start.38) | collective-permute-done | bytes 393248 | tf_op jit(solution)/shard_map/ppermute | solution.py:34
  578.0 6.9 all-to-all-done
  586.0 7.8 %collective-permute-done.40 = bf16[4,96,768]{2,1,0:T(8,128)(2,1)S(1)} collective-permute-done((bf16[4,96,768]{2,1,0:T(8,128)(2,1)S(1)}, bf16[4,96,768]{2,1,0:T(8,128)(2,1)S(1)}, u32[]{:S(2)}, u32[]{:S(2)}) %collective-permute-start.40) | collective-permute-done | bytes 589856 | tf_op jit(solution)/shard_map/ppermute | solution.py:34
  605.8 12.4 %collective-permute-done.20 = f32[1,2048]{1,0:T(1,128)S(1)} collective-permute-done((f32[1,2048]{1,0:T(1,128)S(1)}, f32[1,2048]{1,0:T(1,128)S(1)}, u32[]{:S(2)}, u32[]{:S(2)}) %collective-permute-start.20) | collective-permute-done | bytes 8224 | tf_op jit(solution)/shard_map/ppermute | solution.py:34
  657.1 8.2 %fusion = f32[192,2048]{1,0:T(8,128)} fusion(bf16[4096,192]{1,0:T(8,128)(2,1)S(1)} %bitcast.308, s32[4096]{0:T(1024)S(1)} %add_select_fusion), kind=kOutput, calls=%fused_computation.3 | convolution fusion | flops 3229614080 | bytes 3162112 | tf_op jit(solution)/shard_map/dot_general | solution.py:38
  674.5 51.1 %reduce-scatter.14.cloned.1.call-done.own_ref = bf16[12,96,768]{2,1,0:T(8,128)(2,1)} async-done(((bf16[48,96,768]{2,1,0:T(8,128)(2,1)}), bf16[12,96,768]{2,1,0:T(8,128)(2,1)}) %reduce-scatter.14.cloned.1.call-update) | async-done | bytes 1769488 | tf_op jit(solution)/shard_map/reduce_scatter | solution.py:420
  730.7 20.4 %tile_adamw.1 = (f32[12,192,768]{2,1,0:T(8,128)}, f32[12,192,768]{2,1,0:T(8,128)}, f32[12,192,768]{2,1,0:T(8,128)}) custom-call(s32[12]{0:T(128)} %convert_element_type.551.used_ref, s32[1]{0:T(128)} %bitcast.44.core_ref, f32[12,192,768]{2,1,0:T(8,128)} %w_ref.1, f32[12,192,768]{2,1,0:T(8,128)} %m_ref.1, f32[12,192,768]{2,1,0:T(8,128)} %v_ref.1, ...), custom_call_target="tpu_custom_call" | custom-call | tf_op jit(solution)/shard_map/tile_adamw/pallas_call | solution.py:244
  (732 shorter events, 316.3 us)
Async XLA Ops:
  7.2 41.1 %all-gather.6.cloned.1.call-start = ((), (), s32[]{:S(2)}) async-start(), calls=%async_computation.12 | async-start | bytes 1597440 | tf_op jit(solution)/shard_map/all_gather | solution.py:319
  13.3 187.8 %all-gather.4.cloned.1.call-start = ((), (), s32[]{:S(2)}) async-start(), calls=%async_computation.6 | async-start | bytes 30081024 | tf_op jit(solution)/shard_map/all_gather | solution.py:294
  16.7 413.9 %reduce-scatter.6.cloned.1.call-start = ((), (), s32[]{:S(2)}) async-start(), calls=%async_computation.7 | async-start | bytes 3932160 | tf_op jit(solution)/shard_map/reduce_scatter | solution.py:393
  49.4 18.7 %collective-permute-start = (bf16[768,512]{1,0:T(8,128)(2,1)S(1)}, bf16[768,512]{1,0:T(8,128)(2,1)S(1)}, u32[]{:S(2)}, u32[]{:S(2)}) collective-permute-start(bf16[768,512]{1,0:T(8,128)(2,1)S(1)} %bitcast.290), channel_id=1, source_target_pairs={{0,1},{1,0},{2,3},{3,2},{4,5},{5,4},{6,7},{7,6},{8,9},{9,8},{10,11... | collective-permute-start | bytes 2359304 | tf_op jit(solution)/shard_map/ppermute | solution.py:34
  205.3 11.3 %collective-permute-start.2 = (bf16[768,256]{1,0:T(8,128)(2,1)S(1)}, bf16[768,256]{1,0:T(8,128)(2,1)S(1)}, u32[]{:S(2)}, u32[]{:S(2)}) collective-permute-start(bf16[768,256]{1,0:T(8,128)(2,1)S(1)} %convolution_convert_fusion.12), channel_id=1, source_target_pairs={{0,2},{2,0},{1,3},{3,1},{4,6},{6,4},{5,7},{7,5},{8,10},{10,8},{9,1... | collective-permute-start | bytes 1179656 | tf_op jit(solution)/shard_map/ppermute | solution.py:34
  205.7 11.4 %collective-permute-start.3 = (bf16[768,256]{1,0:T(8,128)(2,1)S(1)}, bf16[768,256]{1,0:T(8,128)(2,1)S(1)}, u32[]{:S(2)}, u32[]{:S(2)}) collective-permute-start(bf16[768,256]{1,0:T(8,128)(2,1)S(1)} %convolution_convert_fusion.12), channel_id=1, source_target_pairs={{0,4},{4,0},{1,5},{5,1},{2,6},{6,2},{3,7},{7,3},{8,12},{12,8},{9,1... | collective-permute-start | bytes 1179656 | tf_op jit(solution)/shard_map/ppermute | solution.py:34
  290.9 12.7 %collective-permute-start.11 = (bf16[256,768]{1,0:T(8,128)(2,1)}, bf16[256,768]{1,0:T(8,128)(2,1)}, u32[]{:S(2)}, u32[]{:S(2)}) collective-permute-start(bf16[256,768]{1,0:T(8,128)(2,1)} %convolution_convert_fusion.9), channel_id=1, source_target_pairs={{0,1},{1,0},{2,3},{3,2},{4,5},{5,4},{6,7},{7,6},{8,9},{9,8},{10,11... | collective-permute-start | bytes 1179656 | tf_op jit(solution)/shard_map/ppermute | solution.py:34
  326.5 11.5 %collective-permute-start.15 = (bf16[256,768]{1,0:T(8,128)(2,1)S(1)}, bf16[256,768]{1,0:T(8,128)(2,1)S(1)}, u32[]{:S(2)}, u32[]{:S(2)}) collective-permute-start(bf16[256,768]{1,0:T(8,128)(2,1)S(1)} %convolution_convert_fusion.13), channel_id=1, source_target_pairs={{0,1},{1,0},{2,3},{3,2},{4,5},{5,4},{6,7},{7,6},{8,9},{9,8},{10,11... | collective-permute-start | bytes 1179656 | tf_op jit(solution)/shard_map/ppermute | solution.py:34
  369.0 225.7 %reduce-scatter.8.cloned.1.call-start = ((), (), s32[]{:S(2)}) async-start(), calls=%async_computation.8 | async-start | bytes 3538944 | tf_op jit(solution)/shard_map/reduce_scatter | solution.py:420
  405.2 23.3 %collective-permute-start.43 = (bf16[8,2,96,768]{3,2,0,1:T(8,128)(2,1)S(1)}, bf16[8,2,96,768]{3,2,0,1:T(8,128)(2,1)S(1)}, u32[]{:S(2)}, u32[]{:S(2)}) collective-permute-start(bf16[8,2,96,768]{3,2,0,1:T(8,128)(2,1)S(1)} %copy.186), channel_id=1, source_target_pairs={{0,4},{4,0},{1,5},{5,1},{2,6},{6,2},{3,7},{7,3},{8,12},{12,8},{9,1... | collective-permute-start | bytes 7077896 | tf_op jit(solution)/shard_map/ppermute | solution.py:34
  430.7 164.0 %reduce-scatter.10.cloned.1.call-start = ((), (), s32[]{:S(2)}) async-start(), calls=%async_computation.9 | async-start | bytes 5308416 | tf_op jit(solution)/shard_map/reduce_scatter | solution.py:420
  439.9 34.7 %collective-permute-start.44 = (bf16[8,2,96,768]{3,2,0,1:T(8,128)(2,1)S(1)}, bf16[8,2,96,768]{3,2,0,1:T(8,128)(2,1)S(1)}, u32[]{:S(2)}, u32[]{:S(2)}) collective-permute-start(bf16[8,2,96,768]{3,2,0,1:T(8,128)(2,1)S(1)} %copy.185), channel_id=1, source_target_pairs={{0,4},{4,0},{1,5},{5,1},{2,6},{6,2},{3,7},{7,3},{8,12},{12,8},{9,1... | collective-permute-start | bytes 7077896 | tf_op jit(solution)/shard_map/ppermute | solution.py:34
  441.6 19.5 %collective-permute-start.45 = (bf16[4,2,96,768]{3,2,0,1:T(8,128)(2,1)S(1)}, bf16[4,2,96,768]{3,2,0,1:T(8,128)(2,1)S(1)}, u32[]{:S(2)}, u32[]{:S(2)}) collective-permute-start(bf16[4,2,96,768]{3,2,0,1:T(8,128)(2,1)S(1)} %copy.188), channel_id=1, source_target_pairs={{0,4},{4,0},{1,5},{5,1},{2,6},{6,2},{3,7},{7,3},{8,12},{12,8},{9,1... | collective-permute-start | bytes 3538952 | tf_op jit(solution)/shard_map/ppermute | solution.py:34
  459.5 13.8 %collective-permute-start.33 = (bf16[2,8,48,256]{3,2,1,0:T(8,128)(2,1)S(1)}, bf16[2,8,48,256]{3,2,1,0:T(8,128)(2,1)S(1)}, u32[]{:S(2)}, u32[]{:S(2)}) collective-permute-start(bf16[2,8,48,256]{3,2,1,0:T(8,128)(2,1)S(1)} %add_convert_fusion.11), channel_id=1, source_target_pairs={{0,2},{2,0},{1,3},{3,1},{4,6},{6,4},{5,7},{7,5},{8,10},{10,8},{9,1... | collective-permute-start | bytes 1179656 | tf_op jit(solution)/shard_map/ppermute | solution.py:34
  461.1 16.5 %collective-permute-start.31 = (bf16[2,8,48,256]{3,2,1,0:T(8,128)(2,1)}, bf16[2,8,48,256]{3,2,1,0:T(8,128)(2,1)}, u32[]{:S(2)}, u32[]{:S(2)}) collective-permute-start(bf16[2,8,48,256]{3,2,1,0:T(8,128)(2,1)} %get-tuple-element.54), channel_id=1, source_target_pairs={{0,4},{4,0},{1,5},{5,1},{2,6},{6,2},{3,7},{7,3},{8,12},{12,8},{9,1... | collective-permute-start | bytes 1179656 | tf_op jit(solution)/shard_map/ppermute | solution.py:34
  477.5 117.3 %reduce-scatter.12.cloned.1.call-start = ((), (), s32[]{:S(2)}) async-start(), calls=%async_computation.10 | async-start | bytes 5308416 | tf_op jit(solution)/shard_map/reduce_scatter | solution.py:420
  532.0 19.2 %collective-permute-start.38 = (bf16[2,8,48,256]{3,2,1,0:T(8,128)(2,1)S(1)}, bf16[2,8,48,256]{3,2,1,0:T(8,128)(2,1)S(1)}, u32[]{:S(2)}, u32[]{:S(2)}) collective-permute-start(bf16[2,8,48,256]{3,2,1,0:T(8,128)(2,1)S(1)} %add_convert_fusion.9), channel_id=1, source_target_pairs={{0,2},{2,0},{1,3},{3,1},{4,6},{6,4},{5,7},{7,5},{8,10},{10,8},{9,1... | collective-permute-start | bytes 1179656 | tf_op jit(solution)/shard_map/ppermute | solution.py:34
  533.1 29.5 %collective-permute-start.42 = (f32[2,768]{1,0:T(2,128)S(1)}, f32[2,768]{1,0:T(2,128)S(1)}, u32[]{:S(2)}, u32[]{:S(2)}) collective-permute-start(f32[2,768]{1,0:T(2,128)S(1)} %pad_maximum_fusion.27), channel_id=1, source_target_pairs={{0,1},{1,0},{2,3},{3,2},{4,5},{5,4},{6,7},{7,6},{8,9},{9,8},{10,11... | collective-permute-start | bytes 18440 | tf_op jit(solution)/shard_map/ppermute | solution.py:34
  556.9 15.8 %collective-permute-start.39 = (bf16[4,2,96,768]{3,2,0,1:T(8,128)(2,1)}, bf16[4,2,96,768]{3,2,0,1:T(8,128)(2,1)}, u32[]{:S(2)}, u32[]{:S(2)}) collective-permute-start(bf16[4,2,96,768]{3,2,0,1:T(8,128)(2,1)} %copy.189), channel_id=1, source_target_pairs={{0,4},{4,0},{1,5},{5,1},{2,6},{6,2},{3,7},{7,3},{8,12},{12,8},{9,1... | collective-permute-start | bytes 3538952 | tf_op jit(solution)/shard_map/ppermute | solution.py:34
  567.9 16.9 %all-to-all-start = ((bf16[4,272,192]{2,1,0:T(8,128)(2,1)}), bf16[4,272,192]{2,1,0:T(8,128)(2,1)S(1)}, u32[]{:S(2)}, u32[]{:S(2)}) async-start(bf16[4,272,192]{2,1,0:T(8,128)(2,1)} %bitcast.208), calls=%async_computation | async-start | bytes 1114112 | tf_op jit(solution)/shard_map/all_to_all | solution.py:467
  572.5 153.1 %reduce-scatter.14.cloned.1.call-start = ((), (), s32[]{:S(2)}) async-start(), calls=%async_computation.11 | async-start | bytes 8847360 | tf_op jit(solution)/shard_map/reduce_scatter | solution.py:420
  574.4 19.4 %collective-permute-start.40 = (bf16[4,96,768]{2,1,0:T(8,128)(2,1)S(1)}, bf16[4,96,768]{2,1,0:T(8,128)(2,1)S(1)}, u32[]{:S(2)}, u32[]{:S(2)}) collective-permute-start(bf16[4,96,768]{2,1,0:T(8,128)(2,1)S(1)} %dynamic-slice_bitcast_fusion), channel_id=1, source_target_pairs={{0,2},{2,0},{1,3},{3,1},{4,6},{6,4},{5,7},{7,5},{8,10},{10,8},{9,1... | collective-permute-start | bytes 1769480 | tf_op jit(solution)/shard_map/ppermute | solution.py:34
  602.9 34.4 %collective-permute-start.48 = (bf16[4,1,272,192]{3,2,1,0:T(8,128)(2,1)S(1)}, bf16[4,1,272,192]{3,2,1,0:T(8,128)(2,1)S(1)}, u32[]{:S(2)}, u32[]{:S(2)}) collective-permute-start(bf16[4,1,272,192]{3,2,1,0:T(8,128)(2,1)S(1)} %bitcast.307), channel_id=1, source_target_pairs={{0,2},{2,0},{1,3},{3,1},{4,6},{6,4},{5,7},{7,5},{8,10},{10,8},{9,1... | collective-permute-start | bytes 1253384 | tf_op jit(solution)/shard_map/ppermute | solution.py:34
  604.8 13.4 %collective-permute-start.20 = (f32[1,2048]{1,0:T(1,128)S(1)}, f32[1,2048]{1,0:T(1,128)S(1)}, u32[]{:S(2)}, u32[]{:S(2)}) collective-permute-start(f32[1,2048]{1,0:T(1,128)S(1)} %fusion.240), channel_id=1, source_target_pairs={{0,2},{2,0},{1,3},{3,1},{4,6},{6,4},{5,7},{7,5},{8,10},{10,8},{9,1... | collective-permute-start | bytes 24584 | tf_op jit(solution)/shard_map/ppermute | solution.py:34
  (214 other events, 2096.7 us)
Sparse Core Ops, SparseCore 0:
  13.4 34.8 all-gather.5
  50.4 150.6 all-gather.3
  369.1 60.3 reduce-scatter.5
  431.6 37.3 reduce-scatter.7
  477.6 47.6 reduce-scatter.9
  528.0 60.9 reduce-scatter.11
  601.7 123.8 reduce-scatter.13
